TPU v7x, 128 devices: a whole 4x4x4 slice. The times are simulated.
128 devices in a mesh: pipe: 4 (over z_hi, core), expert: 32 (over x, z_lo, y).
Axes of the slice: x: 4, y: 4, z: 4 (z_hi: 2, z_lo: 2; z = z_hi * 2 + z_lo), core: 2. Of those that a mesh axis runs over, the one named last changes fastest.
Arguments:
- activations: bfloat16 [4, 2, 2048, 7168], P('pipe', None, 'expert'), may hold values from -6 to 6
- expert_ids: int32 [4, 2, 2048, 2], P('pipe', None, 'expert'), may hold values from 0 to 7, all different within a row; in each aligned block of 64 rows (0 to 63, 64 to 127, ..., all dimensions but the last counted through in order) at most 20 rows name the same one
- gate_values: float32 [4, 2, 2048, 2], P('pipe', None, 'expert'), may hold values from 0.25 to 1
- gate_weight: bfloat16 [4, 2, 7168, 8192], P('pipe', None, None, 'expert'), may hold values from -0.0625 to 0.0625
- up_weight: bfloat16 [4, 2, 7168, 8192], P('pipe', None, None, 'expert'), may hold values from -0.0625 to 0.0625
- down_weight: bfloat16 [4, 2, 8192, 7168], P('pipe', None, 'expert'), may hold values from -0.1875 to 0.1875
Outputs:
- moved: bfloat16 [4, 2, 2048, 7168], P('pipe', None, 'expert')
Inputs may be any that keep to these rules, and one draw needn't show every extreme that they name: `expert_ids`: each row names 2 different experts; among the 64 rows of one index of expert for one rank and section, no expert is named by more than 20 rows, and in some such blocks one expert is named by exactly 20.
All inputs are finite; a program needn't handle non-finite values.
Results may differ from a plain program's by a relative error of at most 0.0041.
Values may be sent and summed in bfloat16 or wider, within the bound.
No kernel may reach another device: no remote copies, remote signals or barrier semaphores. Data moves between devices by JAX's collectives and lax.ppermute only.
A program may use at most 192 MiB of HBM per device.

v0:
```python
import jax
import jax.numpy as jnp
from jax import lax
from jax.sharding import PartitionSpec as P

EXPERTS = 8


def from_behind(value, axis, steps):
    count = lax.axis_size(axis)
    first, last = (max(0, -steps), min(count, count - steps))
    return lax.ppermute(value, axis, [(source, source + steps) for source in range(first, last)])


def assign_slots(token_rows, chosen_ids, capacity):
    model_width = token_rows.shape[1]
    top_count = chosen_ids.shape[1]
    picks_total = chosen_ids.shape[0] * top_count
    chosen = chosen_ids.reshape(picks_total)
    onehot = (chosen[:, None] == jnp.arange(EXPERTS, dtype=jnp.int32)[None, :]).astype(jnp.int32)
    rank_within = jnp.sum((jnp.cumsum(onehot, axis=0) - 1) * onehot, axis=1)
    slot_index = chosen * capacity + rank_within
    source = (
        jnp.full((EXPERTS * capacity,), picks_total, jnp.int32)
        .at[slot_index]
        .set(jnp.arange(picks_total, dtype=jnp.int32))
    )
    padded = jnp.concatenate([token_rows, jnp.zeros((1, model_width), token_rows.dtype)], axis=0)
    return (padded[source // top_count], slot_index)


def expert_hidden(token_rows, gate_matrix, up_matrix, down_matrix):
    gate_out = jnp.dot(token_rows, gate_matrix, preferred_element_type=jnp.float32)
    up_out = jnp.dot(token_rows, up_matrix, preferred_element_type=jnp.float32)
    hidden = (jax.nn.silu(gate_out) * up_out).astype(jnp.bfloat16)
    return jnp.dot(hidden, down_matrix, preferred_element_type=jnp.float32)


def spread_all(outgoing, gate_matrix, up_matrix, down_matrix, group_size):
    model_width = outgoing.shape[1]
    capacity = outgoing.shape[0] // EXPERTS
    sectioned = jnp.broadcast_to(
        outgoing.reshape(EXPERTS, 1, capacity, model_width),
        (EXPERTS, group_size, capacity, model_width),
    ).reshape(EXPERTS * group_size, capacity, model_width)
    received = lax.all_to_all(sectioned, "expert", split_axis=0, concat_axis=0, tiled=True)
    source_count = received.shape[0]
    slot_count = received.shape[1]
    partial_value = expert_hidden(
        received.reshape(source_count * slot_count, model_width),
        gate_matrix,
        up_matrix,
        down_matrix,
    )
    partial_value = partial_value.astype(jnp.bfloat16).reshape(
        source_count, slot_count, model_width
    )
    returned = lax.all_to_all(partial_value, "expert", split_axis=0, concat_axis=0, tiled=True)
    summed = jnp.sum(
        returned.reshape(EXPERTS, group_size, capacity, model_width).astype(jnp.float32), axis=1
    )
    return summed.reshape(EXPERTS * capacity, model_width)


def send_result(result_rows, slot_number):
    if slot_number == 0:
        return from_behind(result_rows, "pipe", 1)
    return from_behind(result_rows, "pipe", -1)


def local(activations, expert_ids, gate_values, gate_weight, up_weight, down_weight):
    group_size = lax.axis_size("expert") // EXPERTS
    tokens_dev = activations.shape[2]
    model_width = activations.shape[3]
    top_count = expert_ids.shape[3]
    capacity = group_size * (
        (tokens_dev * top_count * 5 // 4 + EXPERTS * group_size - 1) // (EXPERTS * group_size)
    )
    results = []
    shifted = []
    for slot_number in range(2):
        token_rows = activations[0, slot_number]
        outgoing, slot_index = assign_slots(token_rows, expert_ids[0, slot_number], capacity)
        summed = spread_all(
            outgoing,
            gate_weight[0, slot_number],
            up_weight[0, slot_number],
            down_weight[0, slot_number],
            group_size,
        )
        picked = (
            summed[slot_index]
            * gate_values[0, slot_number].reshape(tokens_dev * top_count)[:, None]
        )
        combined = jnp.sum(
            picked.reshape(tokens_dev, top_count, model_width), axis=1
        ) + token_rows.astype(jnp.float32)
        result_rows = combined.astype(jnp.bfloat16)
        results.append(result_rows)
    shifted = [send_result(results[0], 0), send_result(results[1], 1)]
    pipe_index = lax.axis_index("pipe")
    last_index = lax.axis_size("pipe") - 1
    first_slot = jnp.where(pipe_index == 0, results[1], shifted[0])
    second_slot = jnp.where(pipe_index == last_index, results[0], shifted[1])
    return jnp.stack([first_slot, second_slot])[None]


def solution(mesh):
    return jax.shard_map(
        local,
        mesh=mesh,
        in_specs=(
            P("pipe", None, "expert", None),
            P("pipe", None, "expert", None),
            P("pipe", None, "expert", None),
            P("pipe", None, None, "expert"),
            P("pipe", None, None, "expert"),
            P("pipe", None, "expert", None),
        ),
        out_specs=P("pipe", None, "expert", None),
        check_vma=False,
    )
```

profile of v0, /device:TPU:1, one launch (start us, length us, event | category | flops | bytes accessed | tf_op | source)
XLA Modules:
  0.0 907.9 jit_solution(3959211533244084773)
XLA Ops:
  16.8 9.5 %all-to-all-start.2 = ((bf16[32,20,7168]{2,1,0:T(8,128)(2,1)}), bf16[32,20,7168]{2,1,0:T(8,128)(2,1)}, u32[]{:S(2)}, u32[]{:S(2)}) async-start(bf16[32,20,7168]{2,1,0:T(8,128)(2,1)} %bitcast.81), calls=%async_computation.2 | async-start | bytes 22020096 | tf_op jit(solution)/shard_map/all_to_all | solution.py:46
  34.3 183.7 %all-to-all-done.2 = bf16[32,20,7168]{2,1,0:T(8,128)(2,1)} async-done(((bf16[32,20,7168]{2,1,0:T(8,128)(2,1)}), bf16[32,20,7168]{2,1,0:T(8,128)(2,1)}, u32[]{:S(2)}, u32[]{:S(2)}) %all-to-all-start.2) | async-done | bytes 9175072 | tf_op jit(solution)/shard_map/all_to_all | solution.py:46
  223.5 17.3 %all-to-all-start = ((bf16[32,20,7168]{2,1,0:T(8,128)(2,1)}), bf16[32,20,7168]{2,1,0:T(8,128)(2,1)}, u32[]{:S(2)}, u32[]{:S(2)}) async-start(bf16[32,20,7168]{2,1,0:T(8,128)(2,1)} %bitcast.82), calls=%async_computation | async-start | bytes 22020096 | tf_op jit(solution)/shard_map/all_to_all | solution.py:46
  240.8 13.4 %reshape.113 = bf16[640,7168]{1,0:T(8,128)(2,1)} reshape(bf16[32,20,7168]{2,1,0:T(8,128)(2,1)} %all-to-all-done.2) | data formatting | bytes 18350080 | tf_op jit(solution)/shard_map/reshape | solution.py:50
  254.2 7.2 fusion.3
  261.4 18.9 %convolution_convert_fusion = bf16[640,7168]{1,0:T(8,128)(2,1)} fusion(bf16[1,2,256,7168]{3,2,1,0:T(8,128)(2,1)} %param.11, bf16[640,7168]{1,0:T(8,128)(2,1)} %reshape.113, bf16[1,2,7168,256]{3,2,1,0:T(8,128)(2,1)} %param.10, f32[640,256]{1,0:T(8,128)S(1)} %fusion.3), kind=kOutput, calls=%fused_computation.8 | convolution fusion | flops 4703191040 | bytes 26345472 | tf_op jit(solution)/shard_map/dot_general | solution.py:36
  280.3 13.2 %reshape.114 = bf16[32,20,7168]{2,1,0:T(8,128)(2,1)} reshape(bf16[640,7168]{1,0:T(8,128)(2,1)} %convolution_convert_fusion) | data formatting | bytes 18350080 | tf_op jit(solution)/shard_map/reshape | solution.py:55
  293.5 152.8 %all-to-all-done = bf16[32,20,7168]{2,1,0:T(8,128)(2,1)} async-done(((bf16[32,20,7168]{2,1,0:T(8,128)(2,1)}), bf16[32,20,7168]{2,1,0:T(8,128)(2,1)}, u32[]{:S(2)}, u32[]{:S(2)}) %all-to-all-start) | async-done | bytes 9175072 | tf_op jit(solution)/shard_map/all_to_all | solution.py:46
  446.3 17.0 %all-to-all-start.3 = ((bf16[32,20,7168]{2,1,0:T(8,128)(2,1)}), bf16[32,20,7168]{2,1,0:T(8,128)(2,1)}, u32[]{:S(2)}, u32[]{:S(2)}) async-start(bf16[32,20,7168]{2,1,0:T(8,128)(2,1)} %reshape.114), calls=%async_computation.3 | async-start | bytes 22020096 | tf_op jit(solution)/shard_map/all_to_all | solution.py:58
  463.3 13.4 %reshape.109 = bf16[640,7168]{1,0:T(8,128)(2,1)} reshape(bf16[32,20,7168]{2,1,0:T(8,128)(2,1)} %all-to-all-done) | data formatting | bytes 18350080 | tf_op jit(solution)/shard_map/reshape | solution.py:50
  476.7 7.2 fusion.8
  483.8 18.9 %convolution_convert_fusion.1 = bf16[640,7168]{1,0:T(8,128)(2,1)} fusion(bf16[1,2,256,7168]{3,2,1,0:T(8,128)(2,1)} %param.11, bf16[640,7168]{1,0:T(8,128)(2,1)} %reshape.109, bf16[1,2,7168,256]{3,2,1,0:T(8,128)(2,1)} %param.10, f32[640,256]{1,0:T(8,128)S(1)} %fusion.8), kind=kOutput, calls=%fused_computation.9 | convolution fusion | flops 4703191040 | bytes 26345472 | tf_op jit(solution)/shard_map/dot_general | solution.py:36
  502.7 13.3 %reshape.110 = bf16[32,20,7168]{2,1,0:T(8,128)(2,1)} reshape(bf16[640,7168]{1,0:T(8,128)(2,1)} %convolution_convert_fusion.1) | data formatting | bytes 18350080 | tf_op jit(solution)/shard_map/reshape | solution.py:55
  516.0 134.1 %all-to-all-done.3 = bf16[32,20,7168]{2,1,0:T(8,128)(2,1)} async-done(((bf16[32,20,7168]{2,1,0:T(8,128)(2,1)}), bf16[32,20,7168]{2,1,0:T(8,128)(2,1)}, u32[]{:S(2)}, u32[]{:S(2)}) %all-to-all-start.3) | async-done | bytes 9175072 | tf_op jit(solution)/shard_map/all_to_all | solution.py:58
  650.2 17.0 %all-to-all-start.1 = ((bf16[32,20,7168]{2,1,0:T(8,128)(2,1)}), bf16[32,20,7168]{2,1,0:T(8,128)(2,1)}, u32[]{:S(2)}, u32[]{:S(2)}) async-start(bf16[32,20,7168]{2,1,0:T(8,128)(2,1)} %reshape.110), calls=%async_computation.1 | async-start | bytes 22020096 | tf_op jit(solution)/shard_map/all_to_all | solution.py:58
  667.4 9.3 %convert_reduce_fusion = f32[8,20,7168]{2,1,0:T(8,128)} fusion(bf16[32,20,7168]{2,1,0:T(8,128)(2,1)} %all-to-all-done.3), kind=kLoop, calls=%fused_computation.6 | loop fusion | flops 8028160 | bytes 13762560 | tf_op jit(solution)/shard_map/reduce_sum | solution.py:59
  682.0 7.4 gather_fusion.3
  695.3 7.2 multiply_reduce_fusion
  702.8 8.6 collective-permute-start
  711.4 133.0 %all-to-all-done.1 = bf16[32,20,7168]{2,1,0:T(8,128)(2,1)} async-done(((bf16[32,20,7168]{2,1,0:T(8,128)(2,1)}), bf16[32,20,7168]{2,1,0:T(8,128)(2,1)}, u32[]{:S(2)}, u32[]{:S(2)}) %all-to-all-start.1) | async-done | bytes 9175072 | tf_op jit(solution)/shard_map/all_to_all | solution.py:58
  844.4 9.2 %convert_reduce_fusion.1 = f32[8,20,7168]{2,1,0:T(8,128)} fusion(bf16[32,20,7168]{2,1,0:T(8,128)(2,1)} %all-to-all-done.1), kind=kLoop, calls=%fused_computation.7 | loop fusion | flops 8028160 | bytes 13762560 | tf_op jit(solution)/shard_map/reduce_sum | solution.py:59
  859.2 7.3 gather_fusion.1
  872.0 7.1 multiply_reduce_fusion.1
  888.9 15.8 %collective-permute-done.1 = bf16[64,7168]{1,0:T(8,128)(2,1)S(1)} collective-permute-done((bf16[64,7168]{1,0:T(8,128)(2,1)}, bf16[64,7168]{1,0:T(8,128)(2,1)S(1)}, u32[]{:S(2)}, u32[]{:S(2)}) %collective-permute-start.1) | collective-permute-done | bytes 917536 | tf_op jit(solution)/shard_map/ppermute | solution.py:12
  (55 shorter events, 65.2 us)
Async XLA Ops:
  16.8 10.2 %copy-start.1 = (bf16[64,7168]{1,0:T(8,128)(2,1)S(1)}, bf16[64,7168]{1,0:T(8,128)(2,1)}, u32[]{:S(2)}) copy-start(bf16[64,7168]{1,0:T(8,128)(2,1)} %get-tuple-element.7) | copy-start | bytes 2752516
  16.8 201.3 %all-to-all-start.2 = ((bf16[32,20,7168]{2,1,0:T(8,128)(2,1)}), bf16[32,20,7168]{2,1,0:T(8,128)(2,1)}, u32[]{:S(2)}, u32[]{:S(2)}) async-start(bf16[32,20,7168]{2,1,0:T(8,128)(2,1)} %bitcast.81), calls=%async_computation.2 | async-start | bytes 22020096 | tf_op jit(solution)/shard_map/all_to_all | solution.py:46
  223.5 222.8 %all-to-all-start = ((bf16[32,20,7168]{2,1,0:T(8,128)(2,1)}), bf16[32,20,7168]{2,1,0:T(8,128)(2,1)}, u32[]{:S(2)}, u32[]{:S(2)}) async-start(bf16[32,20,7168]{2,1,0:T(8,128)(2,1)} %bitcast.82), calls=%async_computation | async-start | bytes 22020096 | tf_op jit(solution)/shard_map/all_to_all | solution.py:46
  446.3 203.9 %all-to-all-start.3 = ((bf16[32,20,7168]{2,1,0:T(8,128)(2,1)}), bf16[32,20,7168]{2,1,0:T(8,128)(2,1)}, u32[]{:S(2)}, u32[]{:S(2)}) async-start(bf16[32,20,7168]{2,1,0:T(8,128)(2,1)} %reshape.114), calls=%async_computation.3 | async-start | bytes 22020096 | tf_op jit(solution)/shard_map/all_to_all | solution.py:58
  516.0 151.2 %copy-start.2 = (f32[1,2,64,2]{2,3,1,0:T(2,128)S(1)}, f32[1,2,64,2]{2,3,1,0:T(2,128)}, u32[]{:S(2)}) copy-start(f32[1,2,64,2]{2,3,1,0:T(2,128)} %param.8) | copy-start | bytes 3076
  650.2 194.2 %all-to-all-start.1 = ((bf16[32,20,7168]{2,1,0:T(8,128)(2,1)}), bf16[32,20,7168]{2,1,0:T(8,128)(2,1)}, u32[]{:S(2)}, u32[]{:S(2)}) async-start(bf16[32,20,7168]{2,1,0:T(8,128)(2,1)} %reshape.110), calls=%async_computation.1 | async-start | bytes 22020096 | tf_op jit(solution)/shard_map/all_to_all | solution.py:58
  695.3 7.3 copy-start
  702.8 176.4 %collective-permute-start = (bf16[64,7168]{1,0:T(8,128)(2,1)S(1)}, bf16[64,7168]{1,0:T(8,128)(2,1)}, u32[]{:S(2)}, u32[]{:S(2)}) collective-permute-start(bf16[64,7168]{1,0:T(8,128)(2,1)S(1)} %add_convert_fusion), channel_id=1, source_target_pairs={{0,32},{32,64},{64,96},{1,33},{33,65},{65,97},{2,34},{34,66},{66,9... | collective-permute-start | bytes 2752520 | tf_op jit(solution)/shard_map/ppermute | solution.py:12
  882.0 22.7 %collective-permute-start.1 = (bf16[64,7168]{1,0:T(8,128)(2,1)}, bf16[64,7168]{1,0:T(8,128)(2,1)S(1)}, u32[]{:S(2)}, u32[]{:S(2)}) collective-permute-start(bf16[64,7168]{1,0:T(8,128)(2,1)} %get-tuple-element.6), channel_id=1, source_target_pairs={{32,0},{64,32},{96,64},{33,1},{65,33},{97,65},{34,2},{66,34},{98,6... | collective-permute-start | bytes 2752520 | tf_op jit(solution)/shard_map/ppermute | solution.py:12
where the time goes:
time: 924 us; the launch traced here: 908 us
  waiting for transfers between devices  619 us (67%)
  local copies, waits for them, and re-layouts  119 us (13%)
  starting transfers between devices  76.3 us (8%)
  matrix products  52.1 us (6%)
  other arithmetic  40.3 us (4%)
    all_to_all x2, waiting for transfers between devices, spread_all(): lax.all_to_all(sectioned, 'expert', split_axis=0, concat_axis=0, tiled=True)  337 us
    all_to_all x2, waiting for transfers between devices, spread_all(): lax.all_to_all(partial_value, 'expert', split_axis=0, concat_axis=0, tile...  267 us
    dot_general x2, matrix products, expert_hidden(): return jnp.dot(hidden, down_matrix, preferred_element_type=jnp.float32)  37.8 us
    all_to_all x2, starting transfers between devices, spread_all(): lax.all_to_all(partial_value, 'expert', split_axis=0, concat_axis=0, tile...  34 us
    all_to_all x2, starting transfers between devices, spread_all(): lax.all_to_all(sectioned, 'expert', split_axis=0, concat_axis=0, tiled=True)  26.8 us
    reshape x2, local copies, waits for them, and re-layouts, spread_all(): received.reshape(source_count * slot_count, model_width)  26.7 us
    reshape x2, local copies, waits for them, and re-layouts, spread_all(): partial_value.astype(jnp.bfloat16)  26.5 us
    gather x4, local copies, waits for them, and re-layouts, local(): summed[slot_index]  26.1 us
  transfers between devices with their start and end apart: 6, of which 5 were waited for; matrix products, arithmetic and copies ran while one was open for 20% of the time, Pallas kernels for 0%

commit v1 on v0

v1 whole, which is shorter than its diff:
```python
import jax
import jax.numpy as jnp
from jax import lax
from jax.sharding import Mesh, PartitionSpec as P

EXPERTS = 8
CAP = 20
BF = jnp.bfloat16
F32 = jnp.float32


def dot(a, b):
    return jnp.dot(a, b, preferred_element_type=F32)


def slots(ids):
    tokens = ids.shape[0]
    chose = jnp.any(ids[:, :, None] == jnp.arange(EXPERTS, dtype=jnp.int32), axis=1)
    before = jnp.tril(jnp.ones((tokens, tokens), BF), -1)
    rank = dot(before, chose.astype(BF)).astype(jnp.int32)
    return jnp.where(chose, rank, -1)


def dispatch_matrix(ids):
    slot = slots(ids)
    return (slot.T[:, None, :] == jnp.arange(CAP, dtype=jnp.int32)[None, :, None]).astype(BF)


def combine_matrix(ids, gates):
    slot = jax.vmap(slots)(ids)
    weight = jnp.sum(
        jnp.where(ids[..., None] == jnp.arange(EXPERTS, dtype=jnp.int32), gates[..., None], 0.0), axis=2
    )
    group = ids.shape[0]
    hit = slot[:, :, :, None, None] == jnp.arange(CAP, dtype=jnp.int32)
    same = jnp.arange(group)[:, None, None, None, None] == jnp.arange(group)[None, None, None, :, None]
    return jnp.where(hit & same, weight[:, :, :, None, None], 0.0)


def local(activations, expert_ids, gate_values, gate_weight, up_weight, down_weight):
    tokens, width = activations.shape[2:]
    group = lax.axis_size("y")
    part = width // group
    pipe_index = lax.axis_index("pipe")
    last = lax.axis_size("pipe") - 1

    routing = jnp.concatenate([expert_ids[0].astype(F32), gate_values[0]], axis=2)
    routing = lax.all_gather(routing, "y", axis=0)

    sums = []
    for s in range(2):
        rows = activations[0, s]
        outgoing = dot(dispatch_matrix(expert_ids[0, s]).reshape(EXPERTS * CAP, tokens), rows).astype(BF)
        arrived = lax.all_to_all(
            outgoing.reshape(EXPERTS, CAP, width), ("x", "z"), split_axis=0, concat_axis=0, tiled=True
        )
        gathered = lax.all_gather(arrived.reshape(EXPERTS * CAP, width), "y", axis=0, tiled=True)
        gate_out = dot(gathered, gate_weight[0, s])
        up_out = dot(gathered, up_weight[0, s])
        hidden = (jax.nn.silu(gate_out) * up_out).astype(BF)
        block = hidden.shape[1]
        hidden = hidden.reshape(group, EXPERTS, CAP, block).transpose(1, 0, 2, 3)
        hidden = lax.all_gather(hidden.reshape(-1, block), "y", axis=0)
        hidden = jnp.concatenate([hidden[j] for j in range(group)], axis=1)
        down = lax.all_to_all(
            down_weight[0, s].reshape(block, group, part).transpose(1, 0, 2),
            "y", split_axis=0, concat_axis=0, tiled=True,
        ).reshape(group * block, part)
        out = dot(hidden, down).astype(BF).reshape(EXPERTS, group * CAP, part)
        back = lax.all_to_all(out, ("x", "z"), split_axis=0, concat_axis=0, tiled=True)
        back = back.reshape(EXPERTS * group * CAP, part)
        mix = combine_matrix(routing[:, s, :, :2].astype(jnp.int32), routing[:, s, :, 2:])
        mix = mix.reshape(group * tokens, EXPERTS * group * CAP)
        high = lax.reduce_precision(mix, 8, 7)
        total = dot(high.astype(BF), back) + dot((mix - high).astype(BF), back)
        total = total.astype(BF).reshape(group, tokens, part)
        total = lax.all_to_all(total, "y", split_axis=0, concat_axis=0, tiled=True)
        total = total.transpose(1, 0, 2).reshape(tokens, width).astype(F32)
        sums.append((rows.astype(F32) + total).astype(BF))

    size = lax.axis_size("pipe")
    ahead = lax.ppermute(sums[0], "pipe", [(i, i + 1) for i in range(size - 1)])
    behind = lax.ppermute(sums[1], "pipe", [(i + 1, i) for i in range(size - 1)])
    first = jnp.where(pipe_index == 0, sums[1], ahead)
    second = jnp.where(pipe_index == last, sums[0], behind)
    return jnp.stack([first, second])[None]


def solution(mesh):
    pipe, expert = mesh.devices.shape
    group = 4
    split = Mesh(mesh.devices.reshape(pipe, 4, 2, group), ("pipe", "x", "z", "y"))
    wide = ("x", "z", "y")
    return jax.shard_map(
        local,
        mesh=split,
        in_specs=(
            P("pipe", None, wide, None),
            P("pipe", None, wide, None),
            P("pipe", None, wide, None),
            P("pipe", None, None, wide),
            P("pipe", None, None, wide),
            P("pipe", None, wide, None),
        ),
        out_specs=P("pipe", None, wide, None),
        check_vma=False,
    )
```

time: 924 us -> 485 us (0.52); the launches traced: 908 us -> 483 us
  waiting for transfers between devices: 619 us -> 226 us
  blocking collectives: 0 us -> 83.4 us
  local copies, waits for them, and re-layouts: 119 us -> 59.9 us
  starting transfers between devices: 76.3 us -> 38.9 us
  other arithmetic: 40.3 us -> 8.97 us
  between operations: 0.81 us -> 13.5 us
    all_to_all x4 -> x6, waiting for transfers between devices: 604 us -> 92.2 us  [the longest x2 61.5 us: local(): lax.all_to_all(down_weight[0, s].reshape(block, group, part).transpose(1,...]
    all_gather x0 -> x4, waiting for transfers between devices: none -> 110 us  [the longest x2 97.6 us: local(): lax.all_gather(arrived.reshape(EXPERTS * CAP, width), 'y', axis=0, tiled=...]
    all_to_all x0 -> x2, blocking collectives: none -> 73.7 us  [local(): lax.all_to_all(outgoing.reshape(EXPERTS, CAP, width), ('x', 'z'), split_a...]
    reshape x6, local copies, waits for them, and re-layouts: 64.1 us -> 13.7 us  [the longest x2 8.33 us: local(): arrived.reshape(EXPERTS * CAP, width)]
    reduce_sum x6 -> x1, other arithmetic: 33.3 us -> 0.02 us  [combine_matrix(): jnp.sum(jnp.where(ids[..., None] == jnp.arange(EXPERTS, dtype=jnp.int32),...]
    gather x6 -> x0, local copies, waits for them, and re-layouts: 32.9 us -> none  [the longest x4 26.1 us: local(): summed[slot_index]]
    all_to_all x4 -> x6, starting transfers between devices: 60.8 us -> 28.7 us  [the longest x2 9.69 us: local(): lax.all_to_all(out, ('x', 'z'), split_axis=0, concat_axis=0, tiled=True)]
    broadcast_in_dim x4 -> x0, local copies, waits for them, and re-layouts: 16.2 us -> none  [spread_all(): jnp.broadcast_to(outgoing.reshape(EXPERTS, 1, capacity, model_width), (EX...]
  transfers between devices with their start and end apart: 6 -> 12, of which waited for: 5 -> 9; matrix products, arithmetic and copies ran while one was open for 20% -> 21% of each run, Pallas kernels for 0% -> 0%
where the time goes in v1:
time: 485 us; the launch traced here: 483 us
  waiting for transfers between devices  226 us (47%)
  blocking collectives  83.4 us (17%)
  local copies, waits for them, and re-layouts  59.9 us (12%)
  matrix products  52.4 us (11%)
  starting transfers between devices  38.9 us (8%)
  between operations  13.5 us (3%)
  other arithmetic  8.97 us (2%)
    all_gather x2, waiting for transfers between devices, local(): lax.all_gather(arrived.reshape(EXPERTS * CAP, width), 'y', axis=0, tiled=...  97.6 us
    all_to_all x2, blocking collectives, local(): lax.all_to_all(outgoing.reshape(EXPERTS, CAP, width), ('x', 'z'), split_a...  73.7 us
    all_to_all x2, waiting for transfers between devices, local(): lax.all_to_all(down_weight[0, s].reshape(block, group, part).transpose(1,...  61.5 us
    dot_general x14, matrix products, dot(): return jnp.dot(a, b, preferred_element_type=F32)  52 us
    all_to_all x2, waiting for transfers between devices, local(): lax.all_to_all(out, ('x', 'z'), split_axis=0, concat_axis=0, tiled=True)  25.7 us
    ppermute x1, waiting for transfers between devices, local(): lax.ppermute(sums[1], 'pipe', [(i + 1, i) for i in range(size - 1)])  15.3 us
    unnamed x20, local copies, waits for them, and re-layouts  14.4 us
    all_to_all x2, local copies, waits for them, and re-layouts, local(): lax.all_to_all(down_weight[0, s].reshape(block, group, part).transpose(1,...  12.2 us
  transfers between devices with their start and end apart: 12, of which 9 were waited for; matrix products, arithmetic and copies ran while one was open for 21% of the time, Pallas kernels for 0%

profile of v1, /device:TPU:1, one launch (start us, length us, event | category | flops | bytes accessed | tf_op | source)
XLA Modules:
  0.0 483.1 jit_solution(3622445777055221089)
XLA Ops:
  13.5 38.9 %all_to_all.40 = bf16[8,20,7168]{2,1,0:T(8,128)(2,1)} all-to-all(bf16[8,20,7168]{2,1,0:T(8,128)(2,1)S(1)} %reshape.233), channel_id=1, replica_groups=mesh['pipe'=4,'x'=4,'z'=2,'y'=4] {'x','z'}, dimensions={0} | all-to-all | bytes 4587520 | tf_op jit(solution)/shard_map/all_to_all | solution.py:54
  62.8 34.7 %all_to_all.41 = bf16[8,20,7168]{2,1,0:T(8,128)(2,1)} all-to-all(bf16[8,20,7168]{2,1,0:T(8,128)(2,1)S(1)} %reshape.226), channel_id=1, replica_groups=mesh['pipe'=4,'x'=4,'z'=2,'y'=4] {'x','z'}, dimensions={0} | all-to-all | bytes 4587520 | tf_op jit(solution)/shard_map/all_to_all | solution.py:54
  101.7 6.8 %fusion.89 = (bf16[1,1,256,7168]{3,2,1,0:T(8,128)(2,1)}, bf16[1,1,256,7168]{3,2,1,0:T(8,128)(2,1)}) fusion(bf16[1,2,256,7168]{3,2,1,0:T(8,128)(2,1)} %param.11), kind=kLoop, calls=%fused_computation.127 | loop fusion | bytes 14680064 | tf_op jit(solution)/shard_map/slice | solution.py:66
  108.5 5.9 %copy.74 = bf16[1,1,256,7168]{2,3,1,0:T(8,128)(2,1)} copy(bf16[1,1,256,7168]{3,2,1,0:T(8,128)(2,1)} %get-tuple-element.8) | data formatting | bytes 7340032
  114.5 4.8 all-to-all-start.5
  119.3 5.9 %copy.73 = bf16[1,1,256,7168]{2,3,1,0:T(8,128)(2,1)} copy(bf16[1,1,256,7168]{3,2,1,0:T(8,128)(2,1)} %get-tuple-element.7) | data formatting | bytes 7340032
  125.2 61.5 %all-to-all-done.5 = bf16[4,256,1792]{1,2,0:T(8,128)(2,1)} async-done(((bf16[4,256,1792]{1,2,0:T(8,128)(2,1)}), bf16[4,256,1792]{1,2,0:T(8,128)(2,1)}, u32[]{:S(2)}, u32[]{:S(2)}) %all-to-all-start.5) | async-done | bytes 3670048 | tf_op jit(solution)/shard_map/all_to_all | solution.py:65
  191.5 6.2 %copy.71 = bf16[4,256,1792]{2,1,0:T(8,128)(2,1)} copy(bf16[4,256,1792]{1,2,0:T(8,128)(2,1)} %all-to-all-done.5) | data formatting | bytes 7340032 | tf_op jit(solution)/shard_map/all_to_all | solution.py:65
  197.7 7.8 %fusion.2 = f32[640,256]{1,0:T(8,128)S(1)} fusion(bf16[640,7168]{1,0:T(8,128)(2,1)} %all-gather.10.cloned.1.call-done, bf16[1,2,7168,256]{3,2,1,0:T(8,128)(2,1)} %param.9), kind=kOutput, calls=%fused_computation.4 | convolution fusion | flops 2348810240 | bytes 13500416 | tf_op jit(solution)/shard_map/dot_general | solution.py:13
  211.2 97.6 %all-gather.6.cloned.1.call-done = bf16[640,7168]{1,0:T(8,128)(2,1)} async-done(((bf16[160,7168]{1,0:T(8,128)(2,1)}), bf16[640,7168]{1,0:T(8,128)(2,1)}) %all-gather.6.cloned.1.call-update) | async-done | bytes 9175056 | tf_op jit(solution)/shard_map/all_gather | solution.py:57
  308.9 7.3 %fusion.6 = f32[640,256]{1,0:T(8,128)S(1)} fusion(bf16[640,7168]{1,0:T(8,128)(2,1)} %all-gather.6.cloned.1.call-done, bf16[1,2,7168,256]{3,2,1,0:T(8,128)(2,1)} %param.9), kind=kOutput, calls=%fused_computation.8 | convolution fusion | flops 2348810240 | bytes 13500416 | tf_op jit(solution)/shard_map/dot_general | solution.py:13
  321.8 12.1 %all-gather.12.cloned.1.call-done = bf16[4,640,256]{2,1,0:T(8,128)(2,1)} async-done(((bf16[1,640,256]{2,1,0:T(8,128)(2,1)}), bf16[4,640,256]{2,1,0:T(8,128)(2,1)}) %all-gather.12.cloned.1.call-update) | async-done | bytes 1310736 | tf_op jit(solution)/shard_map/all_gather | solution.py:63
  335.3 6.0 %convolution_convert_fusion.2 = bf16[640,1792]{1,0:T(8,128)(2,1)} fusion(bf16[1024,1792]{1,0:T(8,128)(2,1)} %bitcast.161, bf16[640,256]{1,0:T(8,128)(2,1)S(1)} %get-tuple-element.14, bf16[640,256]{1,0:T(8,128)(2,1)S(1)} %get-tuple-element.15, bf16[640,256]{1,0:T(8,128)(2,1)S(1)} %get-tuple-element.16, bf16[640,256]{1,0:T(8,128)(2,1)S(1)} %get-tuple-element.13), kind=kOutput, calls=%fused_computation.14 | convolution fusion | flops 2355200000 | bytes 7274496 | tf_op jit(solution)/shard_map/dot_general | solution.py:13
  341.3 5.1 %all-to-all-start.6 = ((bf16[8,80,1792]{2,1,0:T(8,128)(2,1)}), bf16[8,80,1792]{2,1,0:T(8,128)(2,1)S(1)}, u32[]{:S(2)}, u32[]{:S(2)}) async-start(bf16[8,80,1792]{2,1,0:T(8,128)(2,1)} %bitcast.164), calls=%async_computation.6 | async-start | bytes 4587520 | tf_op jit(solution)/shard_map/all_to_all | solution.py:70
  346.4 9.7 %all-gather = f32[8,64,4]{1,2,0:T(4,128)S(1)} all-gather(f32[2,64,4]{1,2,0:T(4,128)S(1)} %pad_maximum_fusion), channel_id=2, replica_groups=mesh['pipe'=4,'x'=4,'z'=2,'y'=4] {'y'}, dimensions={0}, use_global_device_ids=true | all-gather | bytes 10240 | tf_op jit(solution)/shard_map/all_gather | solution.py:48
  356.1 6.0 %copy.65 = bf16[4,256,1792]{2,1,0:T(8,128)(2,1)} copy(bf16[4,256,1792]{1,2,0:T(8,128)(2,1)} %all-to-all-done.1) | data formatting | bytes 7340032 | tf_op jit(solution)/shard_map/all_to_all | solution.py:65
  363.5 6.0 %convolution_convert_fusion.3 = bf16[640,1792]{1,0:T(8,128)(2,1)} fusion(bf16[1024,1792]{1,0:T(8,128)(2,1)} %bitcast.162, bf16[640,256]{1,0:T(8,128)(2,1)S(1)} %get-tuple-element.10, bf16[640,256]{1,0:T(8,128)(2,1)S(1)} %get-tuple-element.11, bf16[640,256]{1,0:T(8,128)(2,1)S(1)} %get-tuple-element.12, bf16[640,256]{1,0:T(8,128)(2,1)S(1)} %get-tuple-element.9), kind=kOutput, calls=%fused_computation.15 | convolution fusion | flops 2355200000 | bytes 7274496 | tf_op jit(solution)/shard_map/dot_general | solution.py:13
  369.5 8.6 %all-to-all-done.6 = bf16[8,80,1792]{2,1,0:T(8,128)(2,1)S(1)} async-done(((bf16[8,80,1792]{2,1,0:T(8,128)(2,1)}), bf16[8,80,1792]{2,1,0:T(8,128)(2,1)S(1)}, u32[]{:S(2)}, u32[]{:S(2)}) %all-to-all-start.6) | async-done | bytes 2293792 | tf_op jit(solution)/shard_map/all_to_all | solution.py:70
  397.2 17.0 %all-to-all-done.2 = bf16[8,80,1792]{2,1,0:T(8,128)(2,1)} async-done(((bf16[8,80,1792]{2,1,0:T(8,128)(2,1)}), bf16[8,80,1792]{2,1,0:T(8,128)(2,1)}, u32[]{:S(2)}, u32[]{:S(2)}) %all-to-all-start.2) | async-done | bytes 2293792 | tf_op jit(solution)/shard_map/all_to_all | solution.py:70
  414.3 5.2 %all-to-all-start.7 = ((bf16[4,64,1792]{2,1,0:T(8,128)(2,1)}), bf16[4,64,1792]{2,1,0:T(8,128)(2,1)S(1)}, u32[]{:S(2)}, u32[]{:S(2)}) async-start(bf16[4,64,1792]{2,1,0:T(8,128)(2,1)} %bitcast.47), calls=%async_computation.7 | async-start | bytes 1835008 | tf_op jit(solution)/shard_map/all_to_all | solution.py:77
  425.6 5.0 %all-to-all-done.7 = bf16[4,64,1792]{2,1,0:T(8,128)(2,1)S(1)} async-done(((bf16[4,64,1792]{2,1,0:T(8,128)(2,1)}), bf16[4,64,1792]{2,1,0:T(8,128)(2,1)S(1)}, u32[]{:S(2)}, u32[]{:S(2)}) %all-to-all-start.7) | async-done | bytes 917536 | tf_op jit(solution)/shard_map/all_to_all | solution.py:77
  436.7 7.9 %collective-permute-start = (bf16[64,7168]{1,0:T(8,128)(2,1)S(1)}, bf16[64,7168]{1,0:T(8,128)(2,1)}, u32[]{:S(2)}, u32[]{:S(2)}) collective-permute-start(bf16[64,7168]{1,0:T(8,128)(2,1)S(1)} %add_convert_fusion), channel_id=1, source_target_pairs={{0,32},{32,64},{64,96},{1,33},{33,65},{65,97},{2,34},{34,66},{66,9... | collective-permute-start | bytes 2752520 | tf_op jit(solution)/shard_map/ppermute | solution.py:82
  446.2 8.7 %collective-permute-done = bf16[64,7168]{1,0:T(8,128)(2,1)} collective-permute-done((bf16[64,7168]{1,0:T(8,128)(2,1)S(1)}, bf16[64,7168]{1,0:T(8,128)(2,1)}, u32[]{:S(2)}, u32[]{:S(2)}) %collective-permute-start) | collective-permute-done | bytes 917536 | tf_op jit(solution)/shard_map/ppermute | solution.py:82
  459.8 15.3 %collective-permute-done.1 = bf16[64,7168]{1,0:T(8,128)(2,1)S(1)} collective-permute-done((bf16[64,7168]{1,0:T(8,128)(2,1)}, bf16[64,7168]{1,0:T(8,128)(2,1)S(1)}, u32[]{:S(2)}, u32[]{:S(2)}) %collective-permute-start.1) | collective-permute-done | bytes 917536 | tf_op jit(solution)/shard_map/ppermute | solution.py:83
  (90 shorter events, 79.4 us)
Async XLA Ops:
  6.5 191.1 %all-gather.10.cloned.1.call-start = ((), (), s32[]{:S(2)}) async-start(), calls=%async_computation.10 | async-start | bytes 11468800 | tf_op jit(solution)/shard_map/all_gather | solution.py:57
  56.6 1.5 copy-start
  56.6 252.3 %all-gather.6.cloned.1.call-start = ((), (), s32[]{:S(2)}) async-start(), calls=%async_computation.8 | async-start | bytes 11468800 | tf_op jit(solution)/shard_map/all_gather | solution.py:57
  114.5 72.2 %all-to-all-start.5 = ((bf16[4,256,1792]{1,2,0:T(8,128)(2,1)}), bf16[4,256,1792]{1,2,0:T(8,128)(2,1)}, u32[]{:S(2)}, u32[]{:S(2)}) async-start(bf16[4,256,1792]{1,2,0:T(8,128)(2,1)} %bitcast.158), calls=%async_computation.5 | async-start | bytes 7340032 | tf_op jit(solution)/shard_map/all_to_all | solution.py:65
  186.7 154.6 %all-to-all-start.1 = ((bf16[4,256,1792]{1,2,0:T(8,128)(2,1)}), bf16[4,256,1792]{1,2,0:T(8,128)(2,1)}, u32[]{:S(2)}, u32[]{:S(2)}) async-start(bf16[4,256,1792]{1,2,0:T(8,128)(2,1)} %bitcast.157), calls=%async_computation.1 | async-start | bytes 7340032 | tf_op jit(solution)/shard_map/all_to_all | solution.py:65
  191.4 142.5 %all-gather.12.cloned.1.call-start = ((), (), s32[]{:S(2)}) async-start(), calls=%async_computation.11 | async-start | bytes 1638400 | tf_op jit(solution)/shard_map/all_gather | solution.py:63
  197.7 7.8 %copy-start.7 = (bf16[640,7168]{1,0:T(8,128)(2,1)S(1)}, bf16[640,7168]{1,0:T(8,128)(2,1)}, u32[]{:S(2)}) copy-start(bf16[640,7168]{1,0:T(8,128)(2,1)} %all-gather.10.cloned.1.call-done) | copy-start | bytes 27525124
  211.0 151.1 %all-gather.8.cloned.1.call-start = ((), (), s32[]{:S(2)}) async-start(), calls=%async_computation.9 | async-start | bytes 1638400 | tf_op jit(solution)/shard_map/all_gather | solution.py:63
  308.9 7.3 %copy-start.8 = (bf16[640,7168]{1,0:T(8,128)(2,1)S(1)}, bf16[640,7168]{1,0:T(8,128)(2,1)}, u32[]{:S(2)}) copy-start(bf16[640,7168]{1,0:T(8,128)(2,1)} %all-gather.6.cloned.1.call-done) | copy-start | bytes 27525124
  341.3 5.1 %copy-start.5 = (s32[1,2,64,2]{2,3,1,0:T(2,128)S(1)}, s32[1,2,64,2]{2,3,1,0:T(2,128)}, u32[]{:S(2)}) copy-start(s32[1,2,64,2]{2,3,1,0:T(2,128)} %param.7) | copy-start | bytes 3076
  341.3 5.1 %copy-start.6 = (f32[1,2,64,2]{2,3,1,0:T(2,128)S(1)}, f32[1,2,64,2]{2,3,1,0:T(2,128)}, u32[]{:S(2)}) copy-start(f32[1,2,64,2]{2,3,1,0:T(2,128)} %param.8) | copy-start | bytes 3076
  341.3 36.9 %all-to-all-start.6 = ((bf16[8,80,1792]{2,1,0:T(8,128)(2,1)}), bf16[8,80,1792]{2,1,0:T(8,128)(2,1)S(1)}, u32[]{:S(2)}, u32[]{:S(2)}) async-start(bf16[8,80,1792]{2,1,0:T(8,128)(2,1)} %bitcast.164), calls=%async_computation.6 | async-start | bytes 4587520 | tf_op jit(solution)/shard_map/all_to_all | solution.py:70
  378.1 36.1 %all-to-all-start.2 = ((bf16[8,80,1792]{2,1,0:T(8,128)(2,1)}), bf16[8,80,1792]{2,1,0:T(8,128)(2,1)}, u32[]{:S(2)}, u32[]{:S(2)}) async-start(bf16[8,80,1792]{2,1,0:T(8,128)(2,1)} %bitcast.163), calls=%async_computation.2 | async-start | bytes 4587520 | tf_op jit(solution)/shard_map/all_to_all | solution.py:70
  393.4 1.9 copy-start.4
  414.3 16.3 %all-to-all-start.7 = ((bf16[4,64,1792]{2,1,0:T(8,128)(2,1)}), bf16[4,64,1792]{2,1,0:T(8,128)(2,1)S(1)}, u32[]{:S(2)}, u32[]{:S(2)}) async-start(bf16[4,64,1792]{2,1,0:T(8,128)(2,1)} %bitcast.47), calls=%async_computation.7 | async-start | bytes 1835008 | tf_op jit(solution)/shard_map/all_to_all | solution.py:77
  419.5 2.6 copy-start.3
  430.6 14.2 %all-to-all-start.3 = ((bf16[4,64,1792]{2,1,0:T(8,128)(2,1)}), bf16[4,64,1792]{2,1,0:T(8,128)(2,1)}, u32[]{:S(2)}, u32[]{:S(2)}) async-start(bf16[4,64,1792]{2,1,0:T(8,128)(2,1)} %bitcast.24), calls=%async_computation.3 | async-start | bytes 1835008 | tf_op jit(solution)/shard_map/all_to_all | solution.py:77
  435.0 1.5 copy-start.1
  436.7 18.2 %collective-permute-start = (bf16[64,7168]{1,0:T(8,128)(2,1)S(1)}, bf16[64,7168]{1,0:T(8,128)(2,1)}, u32[]{:S(2)}, u32[]{:S(2)}) collective-permute-start(bf16[64,7168]{1,0:T(8,128)(2,1)S(1)} %add_convert_fusion), channel_id=1, source_target_pairs={{0,32},{32,64},{64,96},{1,33},{33,65},{65,97},{2,34},{34,66},{66,9... | collective-permute-start | bytes 2752520 | tf_op jit(solution)/shard_map/ppermute | solution.py:82
  457.7 17.5 %copy-start.2 = (bf16[1,64,7168]{2,1,0:T(8,128)(2,1)S(1)}, bf16[1,64,7168]{2,1,0:T(8,128)(2,1)}, u32[]{:S(2)}) copy-start(bf16[1,64,7168]{2,1,0:T(8,128)(2,1)} %get-tuple-element.5) | copy-start | bytes 2752516
  457.7 17.4 %collective-permute-start.1 = (bf16[64,7168]{1,0:T(8,128)(2,1)}, bf16[64,7168]{1,0:T(8,128)(2,1)S(1)}, u32[]{:S(2)}, u32[]{:S(2)}) collective-permute-start(bf16[64,7168]{1,0:T(8,128)(2,1)} %get-tuple-element.6), channel_id=1, source_target_pairs={{32,0},{64,32},{96,64},{33,1},{65,33},{97,65},{34,2},{66,34},{98,6... | collective-permute-start | bytes 2752520 | tf_op jit(solution)/shard_map/ppermute | solution.py:83
Sparse Core Ops, SparseCore 0:
  56.7 116.4 all-gather.9
  174.9 133.9 all-gather.5
  310.5 23.3 all-gather.11
  335.4 25.5 all-gather.7

commit v2 on v1

v2 whole, which is shorter than its diff:
```python
import jax
import jax.numpy as jnp
from jax import lax
from jax.sharding import Mesh, PartitionSpec as P

EXPERTS = 8
CAP = 20
GROUP = 4
BF = jnp.bfloat16
F32 = jnp.float32


def dot(a, b):
    return jnp.dot(a, b, preferred_element_type=F32)


def after(value, *earlier):
    return lax.optimization_barrier((value, *earlier))[0]


def shift(value, steps):
    return lax.ppermute(value, "y", [(i, (i + steps) % GROUP) for i in range(GROUP)])


def exchange(value):
    return lax.all_to_all(value, ("x", "z"), split_axis=0, concat_axis=0, tiled=True)


def slots(ids):
    tokens = ids.shape[0]
    chose = jnp.any(ids[:, :, None] == jnp.arange(EXPERTS, dtype=jnp.int32), axis=1)
    before = jnp.tril(jnp.ones((tokens, tokens), BF), -1)
    rank = dot(before, chose.astype(BF)).astype(jnp.int32)
    return jnp.where(chose, rank, -1)


def in_order(pieces, axis, y):
    size = pieces[0].shape[axis]
    joined = jnp.concatenate(pieces[::-1] + pieces[:0:-1], axis=axis)
    return lax.dynamic_slice_in_dim(joined, (GROUP - 1 - y) * size, GROUP * size, axis)


def down_parts(down, y):
    part = down.shape[1] // GROUP
    cut = [lax.dynamic_slice_in_dim(down, (y + k) % GROUP * part, part, 1) for k in range(GROUP)]
    return [cut[0]] + [shift(cut[k], k) for k in range(1, GROUP)]


def hidden_of(rows, gate, up):
    return (jax.nn.silu(dot(rows, gate)) * dot(rows, up)).astype(BF)


def finish(hidden, parts, slot, weight, y):
    units = [hidden] + [shift(hidden, k) for k in range(1, GROUP)]
    out = dot(jnp.concatenate(units, axis=1), jnp.concatenate(parts, axis=0)).astype(BF)
    part = out.shape[1]
    back = exchange(out.reshape(EXPERTS, GROUP * CAP, part)).reshape(EXPERTS * GROUP * CAP, part)
    tokens = slot.shape[1]
    hit = slot[:, :, :, None, None] == jnp.arange(CAP, dtype=jnp.int32)
    near = jnp.arange(GROUP)
    same = near[:, None, None, None, None] == near[None, None, None, :, None]
    mix = jnp.where(hit & same, weight[:, :, :, None, None], 0.0).reshape(GROUP * tokens, -1)
    high = lax.reduce_precision(mix, 8, 7)
    total = (dot(high.astype(BF), back) + dot((mix - high).astype(BF), back)).astype(BF)
    total = total.reshape(GROUP, tokens, part)
    mine = [lax.dynamic_index_in_dim(total, (y + k) % GROUP, 0, False) for k in range(GROUP)]
    return in_order([mine[0]] + [shift(mine[k], k) for k in range(1, GROUP)], 1, y)


def local(activations, expert_ids, gate_values, gate_weight, up_weight, down_weight):
    tokens, width = activations.shape[2:]
    half = width // 2
    y = lax.axis_index("y")
    pipe_index = lax.axis_index("pipe")
    last = lax.axis_size("pipe") - 1
    first_rows, second_rows = activations[0, 0], activations[0, 1]

    near = [second_rows] + [shift(second_rows, k) for k in range(1, GROUP)]

    slot = slots(expert_ids[0, 0])
    choose = (slot.T[:, None, :] == jnp.arange(CAP, dtype=jnp.int32)[None, :, None]).astype(BF)
    both = jnp.eye(2, dtype=BF)
    choose = (choose[:, None, :, None, :] * both[None, :, None, :, None]).reshape(EXPERTS * 2 * CAP, 2 * tokens)
    halves = jnp.concatenate([first_rows[:, :half], first_rows[:, half:]], axis=0)
    arrived = exchange(dot(choose, halves).astype(BF).reshape(EXPERTS, 2 * CAP, half))
    arrived = arrived.reshape(EXPERTS * 2 * CAP, half)
    order = jnp.arange(EXPERTS * CAP, dtype=jnp.int32)
    source = order // CAP * 2 * CAP + order % CAP
    pick = [
        (source[:, None] + h * CAP == jnp.arange(EXPERTS * 2 * CAP, dtype=jnp.int32)).astype(BF) for h in range(2)
    ]
    arrived = jnp.concatenate([dot(pick[h], arrived).astype(BF) for h in range(2)], axis=1)

    routing = jnp.concatenate([expert_ids[0].astype(F32), gate_values[0]], axis=2)
    routing = lax.all_gather(routing, "y", axis=0)
    ids = routing[..., :2].astype(jnp.int32)
    gates = routing[..., 2:]
    slot = jax.vmap(jax.vmap(slots))(ids)
    weight = jnp.sum(
        jnp.where(ids[..., None] == jnp.arange(EXPERTS, dtype=jnp.int32), gates[..., None], 0.0), axis=3
    )

    behind = jnp.concatenate(near, axis=0)
    slot_behind = jnp.stack([lax.dynamic_index_in_dim(slot[:, 1], (y - k) % GROUP, 0, False) for k in range(GROUP)])
    owner = (y - jnp.arange(GROUP, dtype=jnp.int32)) % GROUP
    hit = slot_behind.transpose(2, 0, 1)[:, None, None] == jnp.arange(CAP, dtype=jnp.int32)[:, None, None]
    same = jnp.arange(GROUP, dtype=jnp.int32)[:, None] == owner
    choose = (hit & same[None, :, None, :, None]).astype(BF).reshape(EXPERTS * GROUP * CAP, GROUP * tokens)
    chosen = dot(choose, behind).astype(BF).reshape(EXPERTS, GROUP * CAP, width)
    chosen = exchange(chosen).reshape(EXPERTS * GROUP * CAP, width)

    parts = [down_parts(after(down_weight[0, 0], behind), y)]

    ahead, back = shift(arrived, 1), shift(arrived, -1)
    middle = EXPERTS * CAP // 2
    far = [shift(ahead[:middle], 1), shift(back[middle:], -1)]
    parts.append(down_parts(after(down_weight[0, 1], ahead, back), y))
    gate, up = gate_weight[0, 0], up_weight[0, 0]
    pieces = [hidden_of(rows, gate, up) for rows in (arrived, ahead, jnp.concatenate(far, axis=0), back)]
    block = pieces[0].shape[1]
    hidden = in_order([piece[None] for piece in pieces], 0, y)
    hidden = hidden.reshape(GROUP, EXPERTS, CAP, block).transpose(1, 0, 2, 3).reshape(-1, block)
    sums = [finish(hidden, parts[0], slot[:, 0], weight[:, 0], y)]

    hidden = hidden_of(chosen, gate_weight[0, 1], up_weight[0, 1])
    sums.append(finish(hidden, parts[1], slot[:, 1], weight[:, 1], y))

    results = [
        (rows.astype(F32) + total.astype(F32)).astype(BF)
        for rows, total in zip((first_rows, second_rows), sums)
    ]
    size = lax.axis_size("pipe")
    ahead = lax.ppermute(results[0], "pipe", [(i, i + 1) for i in range(size - 1)])
    behind = lax.ppermute(results[1], "pipe", [(i + 1, i) for i in range(size - 1)])
    first = jnp.where(pipe_index == 0, results[1], ahead)
    second = jnp.where(pipe_index == last, results[0], behind)
    return jnp.stack([first, second])[None]


def solution(mesh):
    pipe = mesh.devices.shape[0]
    split = Mesh(mesh.devices.reshape(pipe, 4, 2, GROUP), ("pipe", "x", "z", "y"))
    wide = ("x", "z", "y")
    return jax.shard_map(
        local,
        mesh=split,
        in_specs=(
            P("pipe", None, wide, None),
            P("pipe", None, wide, None),
            P("pipe", None, wide, None),
            P("pipe", None, None, wide),
            P("pipe", None, None, wide),
            P("pipe", None, wide, None),
        ),
        out_specs=P("pipe", None, wide, None),
        check_vma=False,
    )
```

time: 485 us -> 497 us (1.025)
  local copies, waits for them, and re-layouts: 59.9 us -> 39.6 us
  waiting for transfers between devices: 226 us -> 245 us
  starting transfers between devices: 38.9 us -> 54.2 us
  between operations: 13.5 us -> 1.24 us
  matrix products: 52.4 us -> 59.8 us
    all_gather x4 -> x0, waiting for transfers between devices: 110 us -> none  [the longest x2 97.6 us: local(): lax.all_gather(arrived.reshape(EXPERTS * CAP, width), 'y', axis=0, tiled=...]
    all_to_all x2 -> x0, blocking collectives: 73.7 us -> none  [local(): lax.all_to_all(outgoing.reshape(EXPERTS, CAP, width), ('x', 'z'), split_a...]
    all_gather x1, blocking collectives: 9.68 us -> 81.1 us  [local(): routing = lax.all_gather(routing, 'y', axis=0)]
    ppermute x2 -> x27, waiting for transfers between devices: 24 us -> 91.5 us  [the longest x25 76.8 us: shift(): lax.ppermute(value, 'y', [(i, (i + steps) % GROUP) for i in range(GROUP)])]
    all_to_all x6 -> x4, waiting for transfers between devices: 92.2 us -> 153 us  [exchange(): lax.all_to_all(value, ('x', 'z'), split_axis=0, concat_axis=0, tiled=True)]
    ppermute x2 -> x27, starting transfers between devices: 9.96 us -> 31.6 us  [the longest x25 22.7 us: shift(): lax.ppermute(value, 'y', [(i, (i + steps) % GROUP) for i in range(GROUP)])]
    reshape x6 -> x1, local copies, waits for them, and re-layouts: 13.7 us -> 0.07 us  [local(): hidden.reshape(GROUP, EXPERTS, CAP, block).transpose(1, 0, 2, 3)]
    all_to_all x2 -> x0, local copies, waits for them, and re-layouts: 12.2 us -> none  [local(): lax.all_to_all(down_weight[0, s].reshape(block, group, part).transpose(1,...]
  transfers between devices with their start and end apart: 12 -> 31, of which waited for: 9 -> 18; matrix products, arithmetic and copies ran while one was open for 21% -> 18% of each run, Pallas kernels for 0% -> 0%
where the time goes in v2:
time: 497 us; the launch traced here: 491 us
  waiting for transfers between devices  245 us (49%)
  blocking collectives  81.1 us (16%)
  matrix products  59.8 us (12%)
  starting transfers between devices  54.2 us (11%)
  local copies, waits for them, and re-layouts  39.6 us (8%)
  other arithmetic  9.84 us (2%)
    all_to_all x4, waiting for transfers between devices, exchange(): lax.all_to_all(value, ('x', 'z'), split_axis=0, concat_axis=0, tiled=True)  153 us
    all_gather x1, blocking collectives, local(): routing = lax.all_gather(routing, 'y', axis=0)  81.1 us
    ppermute x25, waiting for transfers between devices, shift(): lax.ppermute(value, 'y', [(i, (i + steps) % GROUP) for i in range(GROUP)])  76.8 us
    dot_general x22, matrix products, dot(): return jnp.dot(a, b, preferred_element_type=F32)  59.8 us
    ppermute x25, starting transfers between devices, shift(): lax.ppermute(value, 'y', [(i, (i + steps) % GROUP) for i in range(GROUP)])  22.7 us
    all_to_all x4, starting transfers between devices, exchange(): lax.all_to_all(value, ('x', 'z'), split_axis=0, concat_axis=0, tiled=True)  22.6 us
    ppermute x1, waiting for transfers between devices, local(): lax.ppermute(results[1], 'pipe', [(i + 1, i) for i in range(size - 1)])  14.8 us
  transfers between devices with their start and end apart: 31, of which 18 were waited for; matrix products, arithmetic and copies ran while one was open for 18% of the time, Pallas kernels for 0%

profile of v2, /device:TPU:1, one launch (start us, length us, event | category | flops | bytes accessed | tf_op | source)
XLA Modules:
  0.0 490.8 jit_solution(2629253898504960997)
XLA Ops:
  6.0 6.2 %all-to-all-start.1 = ((bf16[8,40,3584]{2,1,0:T(8,128)(2,1)}), bf16[8,40,3584]{2,1,0:T(8,128)(2,1)S(1)}, u32[]{:S(2)}, u32[]{:S(2)}) async-start(bf16[8,40,3584]{2,1,0:T(8,128)(2,1)} %bitcast.170), calls=%async_computation.1 | async-start | bytes 4587520 | tf_op jit(solution)/shard_map/all_to_all | solution.py:26
  12.2 33.3 %all-to-all-done.1 = bf16[8,40,3584]{2,1,0:T(8,128)(2,1)S(1)} async-done(((bf16[8,40,3584]{2,1,0:T(8,128)(2,1)}), bf16[8,40,3584]{2,1,0:T(8,128)(2,1)S(1)}, u32[]{:S(2)}, u32[]{:S(2)}) %all-to-all-start.1) | async-done | bytes 2293792 | tf_op jit(solution)/shard_map/all_to_all | solution.py:26
  52.5 6.6 %slice_bitcast_fusion.1 = (bf16[256,7168]{1,0:T(8,128)(2,1)}, bf16[256,7168]{1,0:T(8,128)(2,1)}) fusion(bf16[1,2,256,7168]{3,2,1,0:T(8,128)(2,1)} %param.11), kind=kLoop, calls=%fused_computation.42 | loop fusion | bytes 14680064 | tf_op jit(solution)/shard_map/squeeze | solution.py:117
  59.1 4.0 constant_dynamic-slice_fusion.3
  66.4 81.1 %all-gather = f32[8,64,4]{1,2,0:T(4,128)S(1)} all-gather(f32[2,64,4]{1,2,0:T(4,128)S(1)} %pad_maximum_fusion.2), channel_id=2, replica_groups=mesh['pipe'=4,'x'=4,'z'=2,'y'=4] {'y'}, dimensions={0}, use_global_device_ids=true | all-gather | bytes 10240 | tf_op jit(solution)/shard_map/all_gather | solution.py:95
  166.1 9.1 %collective-permute-done.14 = bf16[80,7168]{1,0:T(8,128)(2,1)S(1)} collective-permute-done((bf16[80,7168]{1,0:T(8,128)(2,1)S(1)}, bf16[80,7168]{1,0:T(8,128)(2,1)S(1)}, u32[]{:S(2)}, u32[]{:S(2)}) %collective-permute-start.14) | collective-permute-done | bytes 1146912 | tf_op jit(solution)/shard_map/ppermute | solution.py:22
  192.6 3.8 collective-permute-done.16
  196.4 5.6 %fusion.38 = bf16[640,1792]{1,0:T(8,128)(2,1)} fusion(bf16[256,1792]{1,0:T(8,128)(2,1)} %collective-permute-done.21, bf16[256,1792]{1,0:T(8,128)(2,1)} %collective-permute-done.20, bf16[256,1792]{1,0:T(8,128)(2,1)} %collective-permute-done.19, bf16[256,1792]{1,0:T(8,128)(2,1)S(1)} %copy-done.7, bf16[640,256]{1,0:T(8,128)(2,1)S(1)} %collective-permute-done.18, ...), kind=kOutput, calls=%fused_computation.45 | convolution fusion | flops 2369880064 | bytes 7274496 | tf_op jit(solution)/shard_map/dot_general | solution.py:14
  202.1 7.4 %all-to-all-start.3 = ((bf16[8,80,1792]{2,1,0:T(8,128)(2,1)}), bf16[8,80,1792]{2,1,0:T(8,128)(2,1)S(1)}, u32[]{:S(2)}, u32[]{:S(2)}) async-start(bf16[8,80,1792]{2,1,0:T(8,128)(2,1)} %bitcast.176), calls=%async_computation.3 | async-start | bytes 4587520 | tf_op jit(solution)/shard_map/all_to_all | solution.py:26
  211.9 8.3 %collective-permute-done.2 = bf16[64,7168]{1,0:T(8,128)(2,1)} collective-permute-done((bf16[64,7168]{1,0:T(8,128)(2,1)S(1)}, bf16[64,7168]{1,0:T(8,128)(2,1)}, u32[]{:S(2)}, u32[]{:S(2)}) %collective-permute-start.2) | collective-permute-done | bytes 917536 | tf_op jit(solution)/shard_map/ppermute | solution.py:22
  220.2 18.8 %collective-permute-done = bf16[64,7168]{1,0:T(8,128)(2,1)} collective-permute-done((bf16[64,7168]{1,0:T(8,128)(2,1)S(1)}, bf16[64,7168]{1,0:T(8,128)(2,1)}, u32[]{:S(2)}, u32[]{:S(2)}) %collective-permute-start) | collective-permute-done | bytes 917536 | tf_op jit(solution)/shard_map/ppermute | solution.py:22
  239.0 6.3 %convolution_convert_fusion = bf16[640,7168]{1,0:T(8,128)(2,1)} fusion(pred[640,256]{1,0:T(32,128)(4,1)} %and.166, bf16[64,7168]{1,0:T(8,128)(2,1)} %collective-permute-done.2, bf16[64,7168]{1,0:T(8,128)(2,1)} %collective-permute-done.1, bf16[64,7168]{1,0:T(8,128)(2,1)} %collective-permute-done, bf16[64,7168]{1,0:T(8,128)(2,1)S(1)} %copy-done.6), kind=kOutput, calls=%fused_computation | convolution fusion | flops 2368077824 | bytes 13008896 | tf_op jit(solution)/shard_map/dot_general | solution.py:14
  245.3 5.4 %all-to-all-start = ((bf16[8,80,7168]{2,1,0:T(8,128)(2,1)}), bf16[8,80,7168]{2,1,0:T(8,128)(2,1)}, u32[]{:S(2)}, u32[]{:S(2)}) async-start(bf16[8,80,7168]{2,1,0:T(8,128)(2,1)} %bitcast.171), calls=%async_computation | async-start | bytes 18350080 | tf_op jit(solution)/shard_map/all_to_all | solution.py:26
  256.5 3.9 constant_dynamic-slice_fusion.8
  264.0 110.4 %all-to-all-done = bf16[8,80,7168]{2,1,0:T(8,128)(2,1)} async-done(((bf16[8,80,7168]{2,1,0:T(8,128)(2,1)}), bf16[8,80,7168]{2,1,0:T(8,128)(2,1)}, u32[]{:S(2)}, u32[]{:S(2)}) %all-to-all-start) | async-done | bytes 9175072 | tf_op jit(solution)/shard_map/all_to_all | solution.py:26
  374.4 7.7 %fusion.34 = f32[640,256]{0,1:T(8,128)S(1)} fusion(bf16[640,7168]{1,0:T(8,128)(2,1)} %bitcast.15, bf16[1,2,7168,256]{3,2,1,0:T(8,128)(2,1)} %param.9), kind=kOutput, calls=%fused_computation.39 | convolution fusion | flops 2348810240 | bytes 13500416 | tf_op jit(solution)/shard_map/dot_general | solution.py:14
  382.2 7.9 %fusion.73 = bf16[640,256]{0,1:T(8,128)(2,1)S(1)} fusion(bf16[640,7168]{1,0:T(8,128)(2,1)} %bitcast.15, bf16[1,2,7168,256]{3,2,1,0:T(8,128)(2,1)} %param.10, f32[640,256]{0,1:T(8,128)S(1)} %fusion.34), kind=kOutput, calls=%fused_computation.84 | convolution fusion | flops 2349793280 | bytes 13828096 | tf_op jit(solution)/shard_map/dot_general | solution.py:14
  397.7 9.5 %collective-permute-done.3 = bf16[640,256]{0,1:T(8,128)(2,1)S(1)} collective-permute-done((bf16[640,256]{0,1:T(8,128)(2,1)S(1)}, bf16[640,256]{0,1:T(8,128)(2,1)S(1)}, u32[]{:S(2)}, u32[]{:S(2)}) %collective-permute-start.3) | collective-permute-done | bytes 327712 | tf_op jit(solution)/shard_map/ppermute | solution.py:22
  407.3 5.7 %fusion.41 = bf16[640,1792]{1,0:T(8,128)(2,1)} fusion(bf16[256,1792]{1,0:T(8,128)(2,1)} %collective-permute-done.10, bf16[256,1792]{1,0:T(8,128)(2,1)} %collective-permute-done.9, bf16[256,1792]{1,0:T(8,128)(2,1)} %collective-permute-done.8, bf16[256,1792]{1,0:T(8,128)(2,1)S(1)} %copy-done.8, bf16[640,256]{0,1:T(8,128)(2,1)S(1)} %collective-permute-done.5, ...), kind=kOutput, calls=%fused_computation.46 | convolution fusion | flops 2369880064 | bytes 7274496 | tf_op jit(solution)/shard_map/dot_general | solution.py:14
  429.0 5.8 %collective-permute-done.24 = bf16[64,1792]{1,0:T(8,128)(2,1)S(1)} collective-permute-done((bf16[64,1792]{1,0:T(8,128)(2,1)}, bf16[64,1792]{1,0:T(8,128)(2,1)S(1)}, u32[]{:S(2)}, u32[]{:S(2)}) %collective-permute-start.24) | collective-permute-done | bytes 229408 | tf_op jit(solution)/shard_map/ppermute | solution.py:22
  439.2 9.8 %all-to-all-done.2 = bf16[8,80,1792]{2,1,0:T(8,128)(2,1)S(1)} async-done(((bf16[8,80,1792]{2,1,0:T(8,128)(2,1)}), bf16[8,80,1792]{2,1,0:T(8,128)(2,1)S(1)}, u32[]{:S(2)}, u32[]{:S(2)}) %all-to-all-start.2) | async-done | bytes 2293792 | tf_op jit(solution)/shard_map/all_to_all | solution.py:26
  452.8 7.1 %collective-permute-start.25 = (bf16[64,7168]{1,0:T(8,128)(2,1)S(1)}, bf16[64,7168]{1,0:T(8,128)(2,1)S(1)}, u32[]{:S(2)}, u32[]{:S(2)}) collective-permute-start(bf16[64,7168]{1,0:T(8,128)(2,1)S(1)} %add_convert_fusion), channel_id=1, source_target_pairs={{0,32},{32,64},{64,96},{1,33},{33,65},{65,97},{2,34},{34,66},{66,9... | collective-permute-start | bytes 2752520 | tf_op jit(solution)/shard_map/ppermute | solution.py:133
  461.4 6.7 %collective-permute-done.12 = bf16[64,1792]{1,0:T(8,128)(2,1)S(1)} collective-permute-done((bf16[64,1792]{1,0:T(8,128)(2,1)S(1)}, bf16[64,1792]{1,0:T(8,128)(2,1)S(1)}, u32[]{:S(2)}, u32[]{:S(2)}) %collective-permute-start.12) | collective-permute-done | bytes 229408 | tf_op jit(solution)/shard_map/ppermute | solution.py:22
  472.9 14.8 %collective-permute-done.26 = bf16[64,7168]{1,0:T(8,128)(2,1)} collective-permute-done((bf16[64,7168]{1,0:T(8,128)(2,1)S(1)}, bf16[64,7168]{1,0:T(8,128)(2,1)}, u32[]{:S(2)}, u32[]{:S(2)}) %collective-permute-start.26) | collective-permute-done | bytes 917536 | tf_op jit(solution)/shard_map/ppermute | solution.py:134
  (171 shorter events, 104.5 us)
Async XLA Ops:
  6.0 39.5 %all-to-all-start.1 = ((bf16[8,40,3584]{2,1,0:T(8,128)(2,1)}), bf16[8,40,3584]{2,1,0:T(8,128)(2,1)S(1)}, u32[]{:S(2)}, u32[]{:S(2)}) async-start(bf16[8,40,3584]{2,1,0:T(8,128)(2,1)} %bitcast.170), calls=%async_computation.1 | async-start | bytes 4587520 | tf_op jit(solution)/shard_map/all_to_all | solution.py:26
  49.8 102.0 %collective-permute-start.7 = (bf16[160,7168]{1,0:T(8,128)(2,1)}, bf16[160,7168]{1,0:T(8,128)(2,1)}, u32[]{:S(2)}, u32[]{:S(2)}) collective-permute-start(bf16[160,7168]{1,0:T(8,128)(2,1)} %pad_maximum_fusion.1), channel_id=1, source_target_pairs={{0,3},{1,0},{2,1},{3,2},{4,7},{5,4},{6,5},{7,6},{8,11},{9,8},{10,9... | collective-permute-start | bytes 6881288 | tf_op jit(solution)/shard_map/ppermute | solution.py:22
  52.5 97.8 %collective-permute-start.6 = (bf16[160,7168]{1,0:T(8,128)(2,1)}, bf16[160,7168]{1,0:T(8,128)(2,1)}, u32[]{:S(2)}, u32[]{:S(2)}) collective-permute-start(bf16[160,7168]{1,0:T(8,128)(2,1)} %pad_maximum_fusion.1), channel_id=1, source_target_pairs={{0,1},{1,2},{2,3},{3,0},{4,5},{5,6},{6,7},{7,4},{8,9},{9,10},{10,1... | collective-permute-start | bytes 6881288 | tf_op jit(solution)/shard_map/ppermute | solution.py:22
  63.2 121.5 %collective-permute-start.21 = (bf16[256,1792]{1,0:T(8,128)(2,1)}, bf16[256,1792]{1,0:T(8,128)(2,1)}, u32[]{:S(2)}, u32[]{:S(2)}) collective-permute-start(bf16[256,1792]{1,0:T(8,128)(2,1)} %get-tuple-element.24), channel_id=1, source_target_pairs={{0,3},{1,0},{2,1},{3,2},{4,7},{5,4},{6,5},{7,6},{8,11},{9,8},{10,9... | collective-permute-start | bytes 2752520 | tf_op jit(solution)/shard_map/ppermute | solution.py:22
  65.8 119.7 %collective-permute-start.20 = (bf16[256,1792]{1,0:T(8,128)(2,1)}, bf16[256,1792]{1,0:T(8,128)(2,1)}, u32[]{:S(2)}, u32[]{:S(2)}) collective-permute-start(bf16[256,1792]{1,0:T(8,128)(2,1)} %get-tuple-element.25), channel_id=1, source_target_pairs={{0,2},{1,3},{2,0},{3,1},{4,6},{5,7},{6,4},{7,5},{8,10},{9,11},{10,... | collective-permute-start | bytes 2752520 | tf_op jit(solution)/shard_map/ppermute | solution.py:22
  65.8 121.8 %collective-permute-start.19 = (bf16[256,1792]{1,0:T(8,128)(2,1)}, bf16[256,1792]{1,0:T(8,128)(2,1)}, u32[]{:S(2)}, u32[]{:S(2)}) collective-permute-start(bf16[256,1792]{1,0:T(8,128)(2,1)} %get-tuple-element.26), channel_id=1, source_target_pairs={{0,1},{1,2},{2,3},{3,0},{4,5},{5,6},{6,7},{7,4},{8,9},{9,10},{10,1... | collective-permute-start | bytes 2752520 | tf_op jit(solution)/shard_map/ppermute | solution.py:22
  151.7 23.4 %collective-permute-start.14 = (bf16[80,7168]{1,0:T(8,128)(2,1)S(1)}, bf16[80,7168]{1,0:T(8,128)(2,1)S(1)}, u32[]{:S(2)}, u32[]{:S(2)}) collective-permute-start(bf16[80,7168]{1,0:T(8,128)(2,1)S(1)} %slice.88), channel_id=1, source_target_pairs={{0,1},{1,2},{2,3},{3,0},{4,5},{5,6},{6,7},{7,4},{8,9},{9,10},{10,1... | collective-permute-start | bytes 3440648 | tf_op jit(solution)/shard_map/ppermute | solution.py:22
  153.1 22.6 %collective-permute-start.15 = (bf16[80,7168]{1,0:T(8,128)(2,1)S(1)}, bf16[80,7168]{1,0:T(8,128)(2,1)S(1)}, u32[]{:S(2)}, u32[]{:S(2)}) collective-permute-start(bf16[80,7168]{1,0:T(8,128)(2,1)S(1)} %slice.89), channel_id=1, source_target_pairs={{0,3},{1,0},{2,1},{3,2},{4,7},{5,4},{6,5},{7,6},{8,11},{9,8},{10,9... | collective-permute-start | bytes 3440648 | tf_op jit(solution)/shard_map/ppermute | solution.py:22
  181.7 11.0 %collective-permute-start.18 = (bf16[640,256]{1,0:T(8,128)(2,1)S(1)}, bf16[640,256]{1,0:T(8,128)(2,1)S(1)}, u32[]{:S(2)}, u32[]{:S(2)}) collective-permute-start(bf16[640,256]{1,0:T(8,128)(2,1)S(1)} %reshape.235), channel_id=1, source_target_pairs={{0,3},{1,0},{2,1},{3,2},{4,7},{5,4},{6,5},{7,6},{8,11},{9,8},{10,9... | collective-permute-start | bytes 983048 | tf_op jit(solution)/shard_map/ppermute | solution.py:22
  184.6 11.8 %collective-permute-start.16 = (bf16[640,256]{1,0:T(8,128)(2,1)S(1)}, bf16[640,256]{1,0:T(8,128)(2,1)S(1)}, u32[]{:S(2)}, u32[]{:S(2)}) collective-permute-start(bf16[640,256]{1,0:T(8,128)(2,1)S(1)} %reshape.235), channel_id=1, source_target_pairs={{0,1},{1,2},{2,3},{3,0},{4,5},{5,6},{6,7},{7,4},{8,9},{9,10},{10,1... | collective-permute-start | bytes 983048 | tf_op jit(solution)/shard_map/ppermute | solution.py:22
  185.5 34.7 %collective-permute-start.2 = (bf16[64,7168]{1,0:T(8,128)(2,1)S(1)}, bf16[64,7168]{1,0:T(8,128)(2,1)}, u32[]{:S(2)}, u32[]{:S(2)}) collective-permute-start(bf16[64,7168]{1,0:T(8,128)(2,1)S(1)} %copy-done.6), channel_id=1, source_target_pairs={{0,3},{1,0},{2,1},{3,2},{4,7},{5,4},{6,5},{7,6},{8,11},{9,8},{10,9... | collective-permute-start | bytes 2752520 | tf_op jit(solution)/shard_map/ppermute | solution.py:22
  187.6 32.6 %collective-permute-start.1 = (bf16[64,7168]{1,0:T(8,128)(2,1)S(1)}, bf16[64,7168]{1,0:T(8,128)(2,1)}, u32[]{:S(2)}, u32[]{:S(2)}) collective-permute-start(bf16[64,7168]{1,0:T(8,128)(2,1)S(1)} %copy-done.6), channel_id=1, source_target_pairs={{0,2},{1,3},{2,0},{3,1},{4,6},{5,7},{6,4},{7,5},{8,10},{9,11},{10,... | collective-permute-start | bytes 2752520 | tf_op jit(solution)/shard_map/ppermute | solution.py:22
  192.6 46.4 %collective-permute-start = (bf16[64,7168]{1,0:T(8,128)(2,1)S(1)}, bf16[64,7168]{1,0:T(8,128)(2,1)}, u32[]{:S(2)}, u32[]{:S(2)}) collective-permute-start(bf16[64,7168]{1,0:T(8,128)(2,1)S(1)} %copy-done.6), channel_id=1, source_target_pairs={{0,1},{1,2},{2,3},{3,0},{4,5},{5,6},{6,7},{7,4},{8,9},{9,10},{10,1... | collective-permute-start | bytes 2752520 | tf_op jit(solution)/shard_map/ppermute | solution.py:22
  202.1 43.3 %all-to-all-start.3 = ((bf16[8,80,1792]{2,1,0:T(8,128)(2,1)}), bf16[8,80,1792]{2,1,0:T(8,128)(2,1)S(1)}, u32[]{:S(2)}, u32[]{:S(2)}) async-start(bf16[8,80,1792]{2,1,0:T(8,128)(2,1)} %bitcast.176), calls=%async_computation.3 | async-start | bytes 4587520 | tf_op jit(solution)/shard_map/all_to_all | solution.py:26
  245.3 129.1 %all-to-all-start = ((bf16[8,80,7168]{2,1,0:T(8,128)(2,1)}), bf16[8,80,7168]{2,1,0:T(8,128)(2,1)}, u32[]{:S(2)}, u32[]{:S(2)}) async-start(bf16[8,80,7168]{2,1,0:T(8,128)(2,1)} %bitcast.171), calls=%async_computation | async-start | bytes 18350080 | tf_op jit(solution)/shard_map/all_to_all | solution.py:26
  260.4 129.8 %collective-permute-start.10 = (bf16[256,1792]{1,0:T(8,128)(2,1)}, bf16[256,1792]{1,0:T(8,128)(2,1)}, u32[]{:S(2)}, u32[]{:S(2)}) collective-permute-start(bf16[256,1792]{1,0:T(8,128)(2,1)} %get-tuple-element.20), channel_id=1, source_target_pairs={{0,3},{1,0},{2,1},{3,2},{4,7},{5,4},{6,5},{7,6},{8,11},{9,8},{10,9... | collective-permute-start | bytes 2752520 | tf_op jit(solution)/shard_map/ppermute | solution.py:22
  260.4 132.3 %collective-permute-start.9 = (bf16[256,1792]{1,0:T(8,128)(2,1)}, bf16[256,1792]{1,0:T(8,128)(2,1)}, u32[]{:S(2)}, u32[]{:S(2)}) collective-permute-start(bf16[256,1792]{1,0:T(8,128)(2,1)} %get-tuple-element.21), channel_id=1, source_target_pairs={{0,2},{1,3},{2,0},{3,1},{4,6},{5,7},{6,4},{7,5},{8,10},{9,11},{10,... | collective-permute-start | bytes 2752520 | tf_op jit(solution)/shard_map/ppermute | solution.py:22
  260.4 132.3 %collective-permute-start.8 = (bf16[256,1792]{1,0:T(8,128)(2,1)}, bf16[256,1792]{1,0:T(8,128)(2,1)}, u32[]{:S(2)}, u32[]{:S(2)}) collective-permute-start(bf16[256,1792]{1,0:T(8,128)(2,1)} %get-tuple-element.22), channel_id=1, source_target_pairs={{0,1},{1,2},{2,3},{3,0},{4,5},{5,6},{6,7},{7,4},{8,9},{9,10},{10,1... | collective-permute-start | bytes 2752520 | tf_op jit(solution)/shard_map/ppermute | solution.py:22
  390.2 17.0 %collective-permute-start.3 = (bf16[640,256]{0,1:T(8,128)(2,1)S(1)}, bf16[640,256]{0,1:T(8,128)(2,1)S(1)}, u32[]{:S(2)}, u32[]{:S(2)}) collective-permute-start(bf16[640,256]{0,1:T(8,128)(2,1)S(1)} %fusion.73), channel_id=1, source_target_pairs={{0,1},{1,2},{2,3},{3,0},{4,5},{5,6},{6,7},{7,4},{8,9},{9,10},{10,1... | collective-permute-start | bytes 983048 | tf_op jit(solution)/shard_map/ppermute | solution.py:22
  413.0 36.0 %all-to-all-start.2 = ((bf16[8,80,1792]{2,1,0:T(8,128)(2,1)}), bf16[8,80,1792]{2,1,0:T(8,128)(2,1)S(1)}, u32[]{:S(2)}, u32[]{:S(2)}) async-start(bf16[8,80,1792]{2,1,0:T(8,128)(2,1)} %bitcast.177), calls=%async_computation.2 | async-start | bytes 4587520 | tf_op jit(solution)/shard_map/all_to_all | solution.py:26
  421.4 13.4 %collective-permute-start.24 = (bf16[64,1792]{1,0:T(8,128)(2,1)}, bf16[64,1792]{1,0:T(8,128)(2,1)S(1)}, u32[]{:S(2)}, u32[]{:S(2)}) collective-permute-start(bf16[64,1792]{1,0:T(8,128)(2,1)} %get-tuple-element.32), channel_id=1, source_target_pairs={{0,1},{1,2},{2,3},{3,0},{4,5},{5,6},{6,7},{7,4},{8,9},{9,10},{10,1... | collective-permute-start | bytes 688136 | tf_op jit(solution)/shard_map/ppermute | solution.py:22
  452.8 17.7 %collective-permute-start.25 = (bf16[64,7168]{1,0:T(8,128)(2,1)S(1)}, bf16[64,7168]{1,0:T(8,128)(2,1)S(1)}, u32[]{:S(2)}, u32[]{:S(2)}) collective-permute-start(bf16[64,7168]{1,0:T(8,128)(2,1)S(1)} %add_convert_fusion), channel_id=1, source_target_pairs={{0,32},{32,64},{64,96},{1,33},{33,65},{65,97},{2,34},{34,66},{66,9... | collective-permute-start | bytes 2752520 | tf_op jit(solution)/shard_map/ppermute | solution.py:133
  460.0 10.4 %collective-permute-start.13 = (bf16[64,1792]{1,0:T(8,128)(2,1)S(1)}, bf16[64,1792]{1,0:T(8,128)(2,1)S(1)}, u32[]{:S(2)}, u32[]{:S(2)}) collective-permute-start(bf16[64,1792]{1,0:T(8,128)(2,1)S(1)} %get-tuple-element.29), channel_id=1, source_target_pairs={{0,1},{1,2},{2,3},{3,0},{4,5},{5,6},{6,7},{7,4},{8,9},{9,10},{10,1... | collective-permute-start | bytes 688136 | tf_op jit(solution)/shard_map/ppermute | solution.py:22
  471.0 16.7 %collective-permute-start.26 = (bf16[64,7168]{1,0:T(8,128)(2,1)S(1)}, bf16[64,7168]{1,0:T(8,128)(2,1)}, u32[]{:S(2)}, u32[]{:S(2)}) collective-permute-start(bf16[64,7168]{1,0:T(8,128)(2,1)S(1)} %get-tuple-element.10), channel_id=1, source_target_pairs={{32,0},{64,32},{96,64},{33,1},{65,33},{97,65},{34,2},{66,34},{98,6... | collective-permute-start | bytes 2752520 | tf_op jit(solution)/shard_map/ppermute | solution.py:134
  (26 other events, 267.4 us)

commit v3 on v1

v3 whole, which is shorter than its diff:
```python
import functools

import jax
import jax.numpy as jnp
import numpy as np
from jax import lax
from jax.experimental import pallas as pl
from jax.experimental.pallas import tpu as pltpu
from jax.sharding import Mesh, PartitionSpec as P

EXPERTS = 8
CAP = 20
GROUP = 4
PAIR = 2
LANES = 128
STRIDE = 64
BF = jnp.bfloat16
F32 = jnp.float32


def dot(a, b):
    return jnp.dot(a, b, preferred_element_type=F32)


def dot_t(a, b):
    return lax.dot_general(a, b, (((1,), (1,)), ((), ())), preferred_element_type=F32)


def tie(*values):
    anywhere = [pl.BlockSpec(memory_space=pl.ANY)] * len(values)
    return pl.pallas_call(
        lambda *refs: None,
        out_shape=[jax.ShapeDtypeStruct(value.shape, value.dtype) for value in values],
        in_specs=anywhere,
        out_specs=anywhere,
        input_output_aliases={i: i for i in range(len(values))},
    )(*values)


def call(kernel, out_shape, grid, in_specs, out_specs, scratch=(), moved=0):
    return pl.pallas_call(
        kernel,
        cost_estimate=pl.CostEstimate(flops=0, transcendentals=0, bytes_accessed=moved),
        out_shape=out_shape,
        grid_spec=pltpu.PrefetchScalarGridSpec(
            num_scalar_prefetch=1, grid=grid, in_specs=in_specs, out_specs=out_specs, scratch_shapes=scratch
        ),
        compiler_params=pltpu.CompilerParams(vmem_limit_bytes=48 * 1024 * 1024),
    )


def shape(*dims):
    return jax.ShapeDtypeStruct(dims, BF)


def whole(value):
    return pl.BlockSpec(value.shape, lambda *_: (0,) * len(value.shape))


def columns_of(rows, tile):
    return pl.BlockSpec((rows, tile), lambda j, y: (0, j))


def shift(value, steps):
    return lax.ppermute(value, "y", [(i, (i + steps) % GROUP) for i in range(GROUP)])


def shifts(pieces):
    return [shift(pieces[k - 1], k) for k in range(1, GROUP)]


def spread(value):
    return [shift(value, k) for k in range(1, GROUP)]


def exchange(value):
    return lax.all_to_all(value, ("x", "z"), split_axis=0, concat_axis=0, tiled=True)


def packed(ids, gates):
    high = lax.reduce_precision(gates, 8, 7)
    middle = lax.reduce_precision(gates - high, 8, 7)
    return jnp.concatenate([ids.astype(F32), high, middle, gates - high - middle], axis=-1).astype(BF)


def unpacked(columns):
    top = columns.shape[-1] // 4
    columns = [columns[:, i * top : (i + 1) * top].astype(F32) for i in range(4)]
    return columns[0].astype(jnp.int32), (columns[1] + columns[2]) + columns[3]


def keys(ids, before, place):
    named = [ids[:, k : k + 1] == jnp.arange(LANES, dtype=jnp.int32) for k in range(ids.shape[1])]
    chose = functools.reduce(jnp.logical_or, named)
    rank = dot(before, chose.astype(BF))
    return jnp.where(chose, rank + place, -1.0).astype(BF), named


def expert_rows(per_expert):
    return np.asarray(np.arange(EXPERTS * per_expert)[:, None] // per_expert == np.arange(LANES), dtype=BF)


def codes(places):
    return np.asarray([STRIDE * place + c for _ in range(EXPERTS) for place in places for c in range(CAP)], np.float32)


def unfold(y, pick, value):
    rows, half = pick.shape[1], value.shape[1]

    def kernel(y_ref, pick_ref, value_ref, out_ref):
        out_ref[...] = dot(pick_ref[0], value_ref[...]).astype(BF)

    return call(
        kernel,
        shape(rows, 2 * half),
        (2,),
        [pl.BlockSpec((1,) + pick.shape[1:], lambda h, y: (h, 0, 0)), whole(value)],
        columns_of(rows, half),
    )(y, pick, value)


def quarters(y, down, section, runs):
    depth, part = down.shape[2], down.shape[3] // GROUP // runs
    count = (GROUP - 1) * runs

    def kernel(y_ref, down_ref, *refs):
        for i in range(count):

            @pl.when(pl.program_id(0) == i)
            def _():
                refs[i][...] = down_ref[0, 0]

    def column(i, y):
        return (0, section, 0, lax.rem(y[0] + i // runs + 1, GROUP) * runs + lax.rem(i, runs))

    cuts = call(
        kernel,
        [shape(depth, part)] * count,
        (count,),
        [pl.BlockSpec((1, 1, depth, part), column)],
        [pl.BlockSpec((depth, part), lambda k, y: (0, 0))] * count,
    )(y, down)
    return [cuts[run::runs] for run in range(runs)]


def hidden_of(y, rows, gate, up, section):
    width, block = gate.shape[2:]
    total = sum(run.shape[0] for run in rows)
    tile = 1024
    steps = width // tile

    def kernel(y_ref, gate_ref, up_ref, *refs):
        *runs, out_ref, gate_sum, up_sum = refs
        step = pl.program_id(0)

        @pl.when(step == 0)
        def _():
            gate_sum[...] = jnp.zeros_like(gate_sum)
            up_sum[...] = jnp.zeros_like(up_sum)

        value = jnp.concatenate([run[...] for run in runs], axis=0) if len(runs) > 1 else runs[0][...]
        gate_sum[...] += dot(value, gate_ref[0, 0])
        up_sum[...] += dot(value, up_ref[0, 0])

        @pl.when(step == steps - 1)
        def _():
            out_ref[...] = (jax.nn.silu(gate_sum[...]) * up_sum[...]).astype(BF)

    weights = pl.BlockSpec((1, 1, tile, block), lambda j, y: (0, section, j, 0))
    return call(
        kernel,
        shape(total, block),
        (steps,),
        [weights, weights] + [columns_of(run.shape[0], tile) for run in rows],
        pl.BlockSpec((total, block), lambda j, y: (0, 0)),
        [pltpu.VMEM((total, block), F32)] * 2,
        moved=20 * 2**20,
    )(y, gate, up, *rows)


def arrange(y, target, pieces):
    block = pieces[0].shape[1]
    rows = target.shape[1]

    def kernel(y_ref, target_ref, *refs):
        stacked = jnp.concatenate([ref[...] for ref in refs[:-1]], axis=0)
        moved = lax.broadcasted_iota(jnp.int32, (rows, rows), 0) == target_ref[...]
        refs[-1][...] = dot(moved.astype(F32).astype(BF), stacked).astype(BF)

    return call(
        kernel,
        shape(rows, block),
        (1,),
        [whole(target)] + [whole(piece) for piece in pieces],
        pl.BlockSpec((rows, block), lambda j, y: (0, 0)),
    )(y, target, *pieces)


def project(y, units, parts, down, section):
    rows, depth = units[0].shape
    part = sum(group[0].shape[1] for group in parts)
    tile = part // 2
    runs = len(parts)
    flat = [value for group in parts for value in group]

    def kernel(y_ref, *refs):
        *refs, out_ref, joined = refs
        step = pl.program_id(0)

        @pl.when(step == 0)
        def _():
            for k in range(GROUP):
                joined[:, k * depth : (k + 1) * depth] = refs[k][...]

        own, others = refs[GROUP], refs[GROUP + 1 :]
        for run in range(runs):

            @pl.when(step // (2 // runs) == run)
            def _():
                mine = others[run * (GROUP - 1) : (run + 1) * (GROUP - 1)]
                matrix = jnp.concatenate([own[0, 0], *(ref[...] for ref in mine)], axis=0)
                out_ref[...] = dot(joined[...], matrix).astype(BF)

    own = pl.BlockSpec((1, 1, depth, tile), lambda j, y: (0, section, 0, y[0] * 2 + j))
    others = [columns_of(depth, tile) if runs == 1 else whole(value) for value in flat]
    out = call(
        kernel,
        shape(rows, part),
        (2,),
        [whole(unit) for unit in units] + [own] + others,
        columns_of(rows, tile),
        [pltpu.VMEM((rows, GROUP * depth), BF)],
        moved=20 * 2**20,
    )(y, *units, down, *flat)
    return out.reshape(EXPERTS, GROUP * CAP, part)


def combine(y, back, key, weight):
    part, tile = back.shape[2], 896
    back = back.reshape(-1, part)
    tokens = key.shape[0] // GROUP
    onehot = expert_rows(GROUP * CAP)
    code = codes(range(GROUP))[None]
    high = lax.reduce_precision(weight, 8, 7)
    weights = [high.astype(BF), (weight - high).astype(BF)]

    def kernel(y_ref, key_ref, high_ref, low_ref, onehot_ref, code_ref, back_ref, *refs):
        expand = onehot_ref[...]
        hit = dot_t(key_ref[...], expand) == code_ref[...]
        total = 0.0
        for ref in (high_ref, low_ref):
            mix = jnp.where(hit, dot_t(ref[...], expand), 0.0).astype(BF)
            total += dot(mix, back_ref[...])
        total = total.astype(BF)
        for k in range(GROUP):
            refs[k][...] = total[k * tokens : (k + 1) * tokens]

    return call(
        kernel,
        [shape(tokens, part)] * GROUP,
        (part // tile,),
        [whole(value) for value in (key, *weights, onehot, code)] + [columns_of(back.shape[0], tile)],
        [columns_of(tokens, tile)] * GROUP,
    )(y, key, *weights, onehot, code, back)


def home(y, totals, rows):
    pieces = [totals[0], *shifts(totals[1:])]
    tokens, part = totals[0].shape

    def kernel(y_ref, rows_ref, *refs):
        for k in range(GROUP):

            @pl.when(pl.program_id(0) == k)
            def _():
                refs[-1][...] = (rows_ref[...].astype(F32) + refs[k][...].astype(F32)).astype(BF)

    quarter = pl.BlockSpec((tokens, part), lambda k, y: (0, lax.rem(y[0] + GROUP - k, GROUP)))
    return call(
        kernel,
        shape(*rows.shape),
        (GROUP,),
        [quarter] + [whole(piece) for piece in pieces],
        quarter,
    )(y, rows, *pieces)


def local(activations, expert_ids, gate_values, gate_weight, up_weight, down_weight):
    tokens, width = activations.shape[2:]
    top = expert_ids.shape[3]
    half = width // 2
    index = lax.axis_index("y").astype(jnp.int32)
    y = index.reshape(1)
    pipe_index = lax.axis_index("pipe")
    last = lax.axis_size("pipe") - 1
    first_rows, second_rows = activations[0, 0], activations[0, 1]

    before = np.asarray(np.tril(np.ones((tokens, tokens)), -1), dtype=BF)
    key, _ = keys(expert_ids[0, 0], before, 0.0)
    key = jnp.concatenate([key, jnp.where(key < 0, key, key + STRIDE)], axis=0)
    choose = (dot_t(expert_rows(2 * CAP), key) == codes(range(2))[:, None]).astype(BF)
    halves = jnp.concatenate([first_rows[:, :half], first_rows[:, half:]], axis=0)
    outgoing = dot(choose, halves).astype(BF).reshape(EXPERTS, 2 * CAP, half)
    routing = [packed(expert_ids[0, s], gate_values[0, s]) for s in range(2)]
    routing = jnp.concatenate([*routing, jnp.zeros((tokens, LANES - 8 * top), BF)], axis=1)
    arrived = exchange(outgoing)

    near = spread(second_rows)
    routing = jnp.concatenate([routing, *spread(routing)], axis=0)
    order = np.arange(EXPERTS * CAP)
    source = order // CAP * 2 * CAP + order % CAP + np.arange(2)[:, None] * CAP
    pick = np.asarray(source[:, :, None] == np.arange(EXPERTS * 2 * CAP), dtype=BF)
    arrived = unfold(y, pick, arrived.reshape(EXPERTS * 2 * CAP, half))
    (cuts0,), (cuts1,) = [quarters(y, down_weight, s, 1) for s in range(2)]

    owner = jnp.bitwise_and(index - np.arange(GROUP * tokens, dtype=np.int32)[:, None] // tokens, GROUP - 1)
    before = np.asarray(np.kron(np.eye(GROUP), np.tril(np.ones((tokens, tokens)), -1)), dtype=BF)
    key, weight = [], []
    for s in range(2):
        ids, gates = unpacked(routing[:, 4 * top * s : 4 * top * (s + 1)])
        found, named = keys(ids, before, (owner * STRIDE).astype(F32))
        key.append(found)
        weight.append(sum(jnp.where(named[k], gates[:, k : k + 1], 0.0) for k in range(top)))
    onehot = expert_rows(GROUP * CAP)
    choose = (dot_t(onehot, key[1]) == codes(range(GROUP))[:, None]).astype(BF)
    turned = [slice(k * tokens, (k + 1) * tokens) for k in (0, 3, 2, 1)]
    key, weight = [[jnp.concatenate([value[cut] for cut in turned]) for value in group] for group in (key, weight)]
    arrived, choose, key0, key1, weight0, weight1, *rest = tie(
        arrived, choose, *key, *weight, *near, *cuts0, *cuts1
    )
    near, cuts0, cuts1 = rest[:3], rest[3:6], rest[6:]

    chosen = dot(choose, jnp.concatenate([second_rows, *near], axis=0)).astype(BF)
    chosen = exchange(chosen.reshape(EXPERTS, GROUP * CAP, width))

    ahead, back = shift(arrived, 1), shift(arrived, -1)
    weights = (gate_weight, up_weight)
    piece = hidden_of(y, [arrived], *weights, 0)
    middle = EXPERTS * CAP // 2
    ahead, back, piece, *rest = tie(ahead, back, piece, *cuts0, *cuts1)
    cuts0, cuts1 = rest[:3], rest[3:]
    far = [shift(ahead[:middle], 1), shift(back[middle:], -1)]
    both = hidden_of(y, [ahead, back], *weights, 0)
    far0, far1, both, *rest = tie(*far, both, *cuts0, *cuts1)
    cuts0, cuts1 = rest[:3], rest[3:]

    parts0 = shifts(cuts0)
    rows = np.arange(EXPERTS * CAP)
    target = np.tile((rows // CAP * GROUP * CAP + rows % CAP).astype(np.int32), GROUP)[None]
    step = np.repeat(np.asarray([0, 1, 3, 2], np.int32), EXPERTS * CAP)[None]
    far_piece = hidden_of(y, [far0, far1], *weights, 0)
    hidden = arrange(y, target + jnp.bitwise_and(index - step + GROUP, GROUP - 1) * CAP, [piece, both, far_piece])
    units = spread(hidden)
    hidden_second = hidden_of(y, [chosen.reshape(-1, width)], *weights, 1)
    hidden_second, *rest = tie(hidden_second, *units, *parts0, *cuts1)
    units, parts0, cuts1 = [hidden, *rest[:3]], rest[3:6], rest[6:]

    parts1 = shifts(cuts1)
    units_second = [hidden_second, *spread(hidden_second)]
    back0 = exchange(project(y, units, [parts0], down_weight, 0))
    out = project(y, units_second, [parts1], down_weight, 1)
    out, key0 = tie(out, key0)
    back1 = exchange(out)
    results = [
        home(y, combine(y, back0, key0, weight0), first_rows),
        home(y, combine(y, back1, key1, weight1), second_rows),
    ]
    size = lax.axis_size("pipe")
    ahead = lax.ppermute(results[0], "pipe", [(i, i + 1) for i in range(size - 1)])
    behind = lax.ppermute(results[1], "pipe", [(i + 1, i) for i in range(size - 1)])
    first = jnp.where(pipe_index == 0, results[1], ahead)
    second = jnp.where(pipe_index == last, results[0], behind)
    return jnp.stack([first, second])[None]


def solution(mesh):
    pipe = mesh.devices.shape[0]
    split = Mesh(mesh.devices.reshape(pipe, 4, 2, GROUP), ("pipe", "x", "z", "y"))
    wide = ("x", "z", "y")
    return jax.shard_map(
        local,
        mesh=split,
        in_specs=(
            P("pipe", None, wide, None),
            P("pipe", None, wide, None),
            P("pipe", None, wide, None),
            P("pipe", None, None, wide),
            P("pipe", None, None, wide),
            P("pipe", None, wide, None),
        ),
        out_specs=P("pipe", None, wide, None),
        check_vma=False,
    )
```

time: 485 us -> 362 us (0.75)
  blocking collectives: 83.4 us -> 0 us
  Pallas kernels: 0 us -> 58.1 us
  waiting for transfers between devices: 226 us -> 168 us
  starting transfers between devices: 38.9 us -> 82.1 us
  matrix products: 52.4 us -> 12.1 us
  local copies, waits for them, and re-layouts: 59.9 us -> 30.2 us
  between operations: 13.5 us -> 0.62 us
    ppermute x2 -> x30, waiting for transfers between devices: 24 us -> 154 us  [the longest x28 141 us: shift(): lax.ppermute(value, 'y', [(i, (i + steps) % GROUP) for i in range(GROUP)])]
    all_gather x4 -> x0, waiting for transfers between devices: 110 us -> none  [the longest x2 97.6 us: local(): lax.all_gather(arrived.reshape(EXPERTS * CAP, width), 'y', axis=0, tiled=...]
    all_to_all x6 -> x4, waiting for transfers between devices: 92.2 us -> 14.3 us  [exchange(): lax.all_to_all(value, ('x', 'z'), split_axis=0, concat_axis=0, tiled=True)]
    all_to_all x2 -> x0, blocking collectives: 73.7 us -> none  [local(): lax.all_to_all(outgoing.reshape(EXPERTS, CAP, width), ('x', 'z'), split_a...]
    pallas_call x0 -> x19, Pallas kernels: none -> 58.1 us  [the longest x4 30 us: hidden_of(): call(kernel, shape(total, block), (steps,), [weights, weights] + [columns...]
    ppermute x2 -> x30, starting transfers between devices: 9.96 us -> 61.7 us  [the longest x28 38.7 us: shift(): lax.ppermute(value, 'y', [(i, (i + steps) % GROUP) for i in range(GROUP)])]
    dot_general x14 -> x5, matrix products: 52 us -> 11.2 us  [dot(): return jnp.dot(a, b, preferred_element_type=F32)]
    reshape x6 -> x0, local copies, waits for them, and re-layouts: 13.7 us -> none  [the longest x2 8.33 us: local(): arrived.reshape(EXPERTS * CAP, width)]
  transfers between devices with their start and end apart: 12 -> 34, of which waited for: 9 -> 14; matrix products, arithmetic and copies ran while one was open for 21% -> 3% of each run, Pallas kernels for 0% -> 15%
where the time goes in v3:
time: 362 us; the launch traced here: 360 us
  waiting for transfers between devices  168 us (46%)
  starting transfers between devices  82.1 us (23%)
  Pallas kernels  58.1 us (16%)
  local copies, waits for them, and re-layouts  30.2 us (8%)
  matrix products  12.1 us (3%)
  other arithmetic  8.07 us (2%)
    ppermute x28, waiting for transfers between devices, shift(): lax.ppermute(value, 'y', [(i, (i + steps) % GROUP) for i in range(GROUP)])  141 us
    ppermute x28, starting transfers between devices, shift(): lax.ppermute(value, 'y', [(i, (i + steps) % GROUP) for i in range(GROUP)])  38.7 us
    pallas_call x4, Pallas kernels, hidden_of(): call(kernel, shape(total, block), (steps,), [weights, weights] + [columns...  30 us
    unnamed x110, local copies, waits for them, and re-layouts  26.9 us
    ppermute x1, starting transfers between devices, local(): lax.ppermute(results[0], 'pipe', [(i, i + 1) for i in range(size - 1)])  21.1 us
    all_to_all x4, starting transfers between devices, exchange(): lax.all_to_all(value, ('x', 'z'), split_axis=0, concat_axis=0, tiled=True)  20.4 us
    all_to_all x4, waiting for transfers between devices, exchange(): lax.all_to_all(value, ('x', 'z'), split_axis=0, concat_axis=0, tiled=True)  14.3 us
    ppermute x1, waiting for transfers between devices, local(): lax.ppermute(results[1], 'pipe', [(i + 1, i) for i in range(size - 1)])  13 us
  transfers between devices with their start and end apart: 34, of which 14 were waited for; matrix products, arithmetic and copies ran while one was open for 3% of the time, Pallas kernels for 15%

profile of v3, /device:TPU:1, one launch (start us, length us, event | category | flops | bytes accessed | tf_op | source)
XLA Modules:
  0.0 359.7 jit_solution(9413689531862796787)
XLA Ops:
  13.9 5.5 %all-to-all-start = ((bf16[8,40,3584]{2,1,0:T(8,128)(2,1)}), bf16[8,40,3584]{2,1,0:T(8,128)(2,1)S(1)}, u32[]{:S(2)}, u32[]{:S(2)}) async-start(bf16[8,40,3584]{2,1,0:T(8,128)(2,1)} %bitcast.77), calls=%async_computation | async-start | bytes 4587520 | tf_op jit(solution)/shard_map/all_to_all | solution.py:77
  36.9 14.3 %all-to-all-done = bf16[8,40,3584]{2,1,0:T(8,128)(2,1)S(1)} async-done(((bf16[8,40,3584]{2,1,0:T(8,128)(2,1)}), bf16[8,40,3584]{2,1,0:T(8,128)(2,1)S(1)}, u32[]{:S(2)}, u32[]{:S(2)}) %all-to-all-start) | async-done | bytes 2293792 | tf_op jit(solution)/shard_map/all_to_all | solution.py:77
  55.3 8.0 %convolution_convert_fusion = bf16[640,7168]{1,0:T(8,128)(2,1)} fusion(bf16[640,256]{1,0:T(8,128)(2,1)} %get-tuple-element.72, bf16[64,7168]{1,0:T(8,128)(2,1)} %get-tuple-element.75, bf16[64,7168]{1,0:T(8,128)(2,1)} %get-tuple-element.74, bf16[64,7168]{1,0:T(8,128)(2,1)} %get-tuple-element.73, bf16[64,7168]{1,0:T(8,128)(2,1)S(1)} %get-tuple-element.123.rows_ref), kind=kOutput, calls=%fused_computation | convolution fusion | flops 2368077824 | bytes 13172736 | tf_op jit(solution)/shard_map/dot_general | solution.py:22
  63.3 5.2 %all-to-all-start.1 = ((bf16[8,80,7168]{2,1,0:T(8,128)(2,1)}), bf16[8,80,7168]{2,1,0:T(8,128)(2,1)}, u32[]{:S(2)}, u32[]{:S(2)}) async-start(bf16[8,80,7168]{2,1,0:T(8,128)(2,1)} %bitcast.76), calls=%async_computation.1 | async-start | bytes 18350080 | tf_op jit(solution)/shard_map/all_to_all | solution.py:77
  71.2 6.3 %shard_map.195.refs_2_ = bf16[160,256]{1,0:T(8,128)(2,1)S(1)} custom-call(s32[1]{0:T(128)} %bitcast.y_ref, bf16[1,2,7168,256]{3,2,1,0:T(8,128)(2,1)} %gate_ref.7, bf16[1,2,7168,256]{3,2,1,0:T(8,128)(2,1)} %up_ref.7, bf16[160,7168]{1,0:T(8,128)(2,1)S(1)} %copy-done.1), custom_call_target="tpu_custom_call" | custom-call | bytes 20971520 | tf_op jit(solution)/shard_map/pallas_call | solution.py:170
  78.2 40.8 %collective-permute-done.6.refs_0_ = bf16[160,7168]{1,0:T(8,128)(2,1)S(1)} collective-permute-done((bf16[160,7168]{1,0:T(8,128)(2,1)S(1)}, bf16[160,7168]{1,0:T(8,128)(2,1)S(1)}, u32[]{:S(2)}, u32[]{:S(2)}) %collective-permute-start.6) | collective-permute-done | bytes 2293792 | tf_op jit(solution)/shard_map/ppermute | solution.py:65
  126.2 7.0 %shard_map.197.refs_2_ = bf16[320,256]{1,0:T(8,128)(2,1)S(1)} custom-call(s32[1]{0:T(128)} %bitcast.y_ref, bf16[1,2,7168,256]{3,2,1,0:T(8,128)(2,1)} %gate_ref.7, bf16[1,2,7168,256]{3,2,1,0:T(8,128)(2,1)} %up_ref.7, bf16[160,7168]{1,0:T(8,128)(2,1)S(1)} %copy-done.9, bf16[160,7168]{1,0:T(8,128)(2,1)S(1)} %copy-done.11), custom_call_target="tpu_custom_call" | custom-call | bytes 20971520 | tf_op jit(solution)/shard_map/pallas_call | solution.py:170
  133.9 14.5 %collective-permute-done.8.refs_0_ = bf16[80,7168]{1,0:T(8,128)(2,1)S(1)} collective-permute-done((bf16[80,7168]{1,0:T(8,128)(2,1)S(1)}, bf16[80,7168]{1,0:T(8,128)(2,1)S(1)}, u32[]{:S(2)}, u32[]{:S(2)}) %collective-permute-start.8) | collective-permute-done | bytes 1146912 | tf_op jit(solution)/shard_map/ppermute | solution.py:65
  155.8 6.4 %shard_map.199.refs_2_ = bf16[160,256]{1,0:T(8,128)(2,1)S(1)} custom-call(s32[1]{0:T(128)} %bitcast.y_ref, bf16[1,2,7168,256]{3,2,1,0:T(8,128)(2,1)} %gate_ref.7, bf16[1,2,7168,256]{3,2,1,0:T(8,128)(2,1)} %up_ref.7, bf16[80,7168]{1,0:T(8,128)(2,1)S(1)} %copy-done.18, bf16[80,7168]{1,0:T(8,128)(2,1)S(1)} %copy-done.20), custom_call_target="tpu_custom_call" | custom-call | bytes 20971520 | tf_op jit(solution)/shard_map/pallas_call | solution.py:170
  164.4 28.9 %collective-permute-done.10.refs_1_ = bf16[640,256]{1,0:T(8,128)(2,1)S(1)} collective-permute-done((bf16[640,256]{1,0:T(8,128)(2,1)S(1)}, bf16[640,256]{1,0:T(8,128)(2,1)S(1)}, u32[]{:S(2)}, u32[]{:S(2)}) %collective-permute-start.10) | collective-permute-done | bytes 327712 | tf_op jit(solution)/shard_map/ppermute | solution.py:65
  194.1 3.4 collective-permute-start.12
  197.5 10.3 %shard_map.194.refs_0_ = bf16[640,256]{1,0:T(8,128)(2,1)S(1)} custom-call(s32[1]{0:T(128)} %bitcast.y_ref, bf16[1,2,7168,256]{3,2,1,0:T(8,128)(2,1)} %gate_ref.7, bf16[1,2,7168,256]{3,2,1,0:T(8,128)(2,1)} %up_ref.7, bf16[640,7168]{1,0:T(8,128)(2,1)} %bitcast.24.refs_0_), custom_call_target="tpu_custom_call" | custom-call | bytes 20971520 | tf_op jit(solution)/shard_map/pallas_call | solution.py:170
  214.6 5.6 %shard_map.206 = bf16[640,1792]{1,0:T(8,128)(2,1)} custom-call(s32[1]{0:T(128)} %bitcast.y_ref, bf16[640,256]{1,0:T(8,128)(2,1)S(1)} %shard_map.200.refs_0_, bf16[640,256]{1,0:T(8,128)(2,1)S(1)} %copy-done.35, bf16[640,256]{1,0:T(8,128)(2,1)} %get-tuple-element.114.refs_2_, bf16[640,256]{1,0:T(8,128)(2,1)} %get-tuple-element.115.refs_3_, ...), custom_call_target="tpu_custom_call" | custom-call | bytes 20971520 | tf_op jit(solution)/shard_map/pallas_call | solution.py:226
  220.2 4.6 %all-to-all-start.3 = ((bf16[8,80,1792]{2,1,0:T(8,128)(2,1)}), bf16[8,80,1792]{2,1,0:T(8,128)(2,1)}, u32[]{:S(2)}, u32[]{:S(2)}) async-start(bf16[8,80,1792]{2,1,0:T(8,128)(2,1)} %bitcast.78), calls=%async_computation.3 | async-start | bytes 4587520 | tf_op jit(solution)/shard_map/all_to_all | solution.py:77
  230.0 32.0 %collective-permute-done.16.refs_1_ = bf16[640,256]{1,0:T(8,128)(2,1)S(1)} collective-permute-done((bf16[640,256]{1,0:T(8,128)(2,1)S(1)}, bf16[640,256]{1,0:T(8,128)(2,1)S(1)}, u32[]{:S(2)}, u32[]{:S(2)}) %collective-permute-start.16) | collective-permute-done | bytes 327712 | tf_op jit(solution)/shard_map/ppermute | solution.py:65
  265.0 6.7 %collective-permute-done.17.refs_2_ = bf16[640,256]{1,0:T(8,128)(2,1)S(1)} collective-permute-done((bf16[640,256]{1,0:T(8,128)(2,1)S(1)}, bf16[640,256]{1,0:T(8,128)(2,1)S(1)}, u32[]{:S(2)}, u32[]{:S(2)}) %collective-permute-start.17) | collective-permute-done | bytes 327712 | tf_op jit(solution)/shard_map/ppermute | solution.py:65
  274.6 5.4 %shard_map.202 = bf16[640,1792]{1,0:T(8,128)(2,1)} custom-call(s32[1]{0:T(128)} %bitcast.y_ref, bf16[640,256]{1,0:T(8,128)(2,1)S(1)} %copy-done.30, bf16[640,256]{1,0:T(8,128)(2,1)S(1)} %collective-permute-done.16.refs_1_, bf16[640,256]{1,0:T(8,128)(2,1)S(1)} %collective-permute-done.17.refs_2_, bf16[640,256]{1,0:T(8,128)(2,1)S(1)} %collective-permute-done.18.refs_3_, ...), custom_call_target="tpu_custom_call" | custom-call | bytes 20971520 | tf_op jit(solution)/shard_map/pallas_call | solution.py:226
  280.0 5.1 %all-to-all-start.2 = ((bf16[8,80,1792]{2,1,0:T(8,128)(2,1)}), bf16[8,80,1792]{2,1,0:T(8,128)(2,1)S(1)}, u32[]{:S(2)}, u32[]{:S(2)}) async-start(bf16[8,80,1792]{2,1,0:T(8,128)(2,1)} %get-tuple-element.106), calls=%async_computation.2 | async-start | bytes 4587520 | tf_op jit(solution)/shard_map/all_to_all | solution.py:77
  285.2 4.0 %shard_map.207 = (bf16[64,1792]{1,0:T(8,128)(2,1)S(1)}, bf16[64,1792]{1,0:T(8,128)(2,1)S(1)}, bf16[64,1792]{1,0:T(8,128)(2,1)S(1)}, bf16[64,1792]{1,0:T(8,128)(2,1)S(1)}) custom-call(s32[1]{0:T(128)} %bitcast.y_ref, bf16[256,128]{1,0:T(8,128)(2,1)S(1)} %copy-done.36, bf16[256,128]{1,0:T(8,128)(2,1)S(1)} %get-tuple-element.130.high_ref, ...), custom_call_target="tpu_custom_call" | custom-call | tf_op jit(solution)/shard_map/pallas_call | solution.py:258
  295.8 3.6 %collective-permute-done.26.refs_2_ = bf16[64,1792]{1,0:T(8,128)(2,1)S(1)} collective-permute-done((bf16[64,1792]{1,0:T(8,128)(2,1)S(1)}, bf16[64,1792]{1,0:T(8,128)(2,1)S(1)}, u32[]{:S(2)}, u32[]{:S(2)}) %collective-permute-start.26) | collective-permute-done | bytes 229408 | tf_op jit(solution)/shard_map/ppermute | solution.py:65
  301.1 21.1 %collective-permute-start.28 = (bf16[64,7168]{1,0:T(8,128)(2,1)}, bf16[64,7168]{1,0:T(8,128)(2,1)}, u32[]{:S(2)}, u32[]{:S(2)}) collective-permute-start(bf16[64,7168]{1,0:T(8,128)(2,1)} %shard_map.208), channel_id=1, source_target_pairs={{0,32},{32,64},{64,96},{1,33},{33,65},{65,97},{2,34},{34,66},{66,9... | collective-permute-start | bytes 2752520 | tf_op jit(solution)/shard_map/ppermute | solution.py:369
  323.8 3.6 shard_map.204
  331.3 5.8 %collective-permute-done.22.refs_1_ = bf16[64,1792]{1,0:T(8,128)(2,1)S(1)} collective-permute-done((bf16[64,1792]{1,0:T(8,128)(2,1)}, bf16[64,1792]{1,0:T(8,128)(2,1)S(1)}, u32[]{:S(2)}, u32[]{:S(2)}) %collective-permute-start.22) | collective-permute-done | bytes 229408 | tf_op jit(solution)/shard_map/ppermute | solution.py:65
  345.2 13.0 %collective-permute-done.29 = bf16[64,7168]{1,0:T(8,128)(2,1)S(1)} collective-permute-done((bf16[64,7168]{1,0:T(8,128)(2,1)S(1)}, bf16[64,7168]{1,0:T(8,128)(2,1)S(1)}, u32[]{:S(2)}, u32[]{:S(2)}) %collective-permute-start.29) | collective-permute-done | bytes 917536 | tf_op jit(solution)/shard_map/ppermute | solution.py:370
  (211 shorter events, 97.8 us)
Async XLA Ops:
  1.5 28.7 %collective-permute-start = (bf16[64,128]{0,1:T(8,128)(2,1)S(1)}, bf16[64,128]{0,1:T(8,128)(2,1)S(1)}, u32[]{:S(2)}, u32[]{:S(2)}) collective-permute-start(bf16[64,128]{0,1:T(8,128)(2,1)S(1)} %concatenate.34), channel_id=1, source_target_pairs={{0,1},{1,2},{2,3},{3,0},{4,5},{5,6},{6,7},{7,4},{8,9},{9,10},{10,1... | collective-permute-start | bytes 49160 | tf_op jit(solution)/shard_map/ppermute | solution.py:65
  3.7 28.3 %collective-permute-start.1 = (bf16[64,128]{0,1:T(8,128)(2,1)S(1)}, bf16[64,128]{0,1:T(8,128)(2,1)S(1)}, u32[]{:S(2)}, u32[]{:S(2)}) collective-permute-start(bf16[64,128]{0,1:T(8,128)(2,1)S(1)} %concatenate.34), channel_id=1, source_target_pairs={{0,2},{1,3},{2,0},{3,1},{4,6},{5,7},{6,4},{7,5},{8,10},{9,11},{10,... | collective-permute-start | bytes 49160 | tf_op jit(solution)/shard_map/ppermute | solution.py:65
  6.3 25.6 %collective-permute-start.2 = (bf16[64,128]{0,1:T(8,128)(2,1)S(1)}, bf16[64,128]{0,1:T(8,128)(2,1)S(1)}, u32[]{:S(2)}, u32[]{:S(2)}) collective-permute-start(bf16[64,128]{0,1:T(8,128)(2,1)S(1)} %concatenate.34), channel_id=1, source_target_pairs={{0,3},{1,0},{2,1},{3,2},{4,7},{5,4},{6,5},{7,6},{8,11},{9,8},{10,9... | collective-permute-start | bytes 49160 | tf_op jit(solution)/shard_map/ppermute | solution.py:65
  9.0 46.3 %collective-permute-start.3 = (bf16[64,7168]{1,0:T(8,128)(2,1)S(1)}, bf16[64,7168]{1,0:T(8,128)(2,1)}, u32[]{:S(2)}, u32[]{:S(2)}) collective-permute-start(bf16[64,7168]{1,0:T(8,128)(2,1)S(1)} %get-tuple-element.123.rows_ref), channel_id=1, source_target_pairs={{0,1},{1,2},{2,3},{3,0},{4,5},{5,6},{6,7},{7,4},{8,9},{9,10},{10,1... | collective-permute-start | bytes 2752520 | tf_op jit(solution)/shard_map/ppermute | solution.py:65
  9.5 45.8 %collective-permute-start.4 = (bf16[64,7168]{1,0:T(8,128)(2,1)S(1)}, bf16[64,7168]{1,0:T(8,128)(2,1)}, u32[]{:S(2)}, u32[]{:S(2)}) collective-permute-start(bf16[64,7168]{1,0:T(8,128)(2,1)S(1)} %get-tuple-element.123.rows_ref), channel_id=1, source_target_pairs={{0,2},{1,3},{2,0},{3,1},{4,6},{5,7},{6,4},{7,5},{8,10},{9,11},{10,... | collective-permute-start | bytes 2752520 | tf_op jit(solution)/shard_map/ppermute | solution.py:65
  13.9 37.3 %all-to-all-start = ((bf16[8,40,3584]{2,1,0:T(8,128)(2,1)}), bf16[8,40,3584]{2,1,0:T(8,128)(2,1)S(1)}, u32[]{:S(2)}, u32[]{:S(2)}) async-start(bf16[8,40,3584]{2,1,0:T(8,128)(2,1)} %bitcast.77), calls=%async_computation | async-start | bytes 4587520 | tf_op jit(solution)/shard_map/all_to_all | solution.py:77
  30.3 25.0 %collective-permute-start.5 = (bf16[64,7168]{1,0:T(8,128)(2,1)S(1)}, bf16[64,7168]{1,0:T(8,128)(2,1)}, u32[]{:S(2)}, u32[]{:S(2)}) collective-permute-start(bf16[64,7168]{1,0:T(8,128)(2,1)S(1)} %get-tuple-element.123.rows_ref), channel_id=1, source_target_pairs={{0,3},{1,0},{2,1},{3,2},{4,7},{5,4},{6,5},{7,6},{8,11},{9,8},{10,9... | collective-permute-start | bytes 2752520 | tf_op jit(solution)/shard_map/ppermute | solution.py:65
  63.3 134.2 %all-to-all-start.1 = ((bf16[8,80,7168]{2,1,0:T(8,128)(2,1)}), bf16[8,80,7168]{2,1,0:T(8,128)(2,1)}, u32[]{:S(2)}, u32[]{:S(2)}) async-start(bf16[8,80,7168]{2,1,0:T(8,128)(2,1)} %bitcast.76), calls=%async_computation.1 | async-start | bytes 18350080 | tf_op jit(solution)/shard_map/all_to_all | solution.py:77
  68.5 50.5 %collective-permute-start.6 = (bf16[160,7168]{1,0:T(8,128)(2,1)S(1)}, bf16[160,7168]{1,0:T(8,128)(2,1)S(1)}, u32[]{:S(2)}, u32[]{:S(2)}) collective-permute-start(bf16[160,7168]{1,0:T(8,128)(2,1)S(1)} %copy-done.1), channel_id=1, source_target_pairs={{0,1},{1,2},{2,3},{3,0},{4,5},{5,6},{6,7},{7,4},{8,9},{9,10},{10,1... | collective-permute-start | bytes 6881288 | tf_op jit(solution)/shard_map/ppermute | solution.py:65
  70.3 48.8 %collective-permute-start.7 = (bf16[160,7168]{1,0:T(8,128)(2,1)S(1)}, bf16[160,7168]{1,0:T(8,128)(2,1)S(1)}, u32[]{:S(2)}, u32[]{:S(2)}) collective-permute-start(bf16[160,7168]{1,0:T(8,128)(2,1)S(1)} %copy-done.1), channel_id=1, source_target_pairs={{0,3},{1,0},{2,1},{3,2},{4,7},{5,4},{6,5},{7,6},{8,11},{9,8},{10,9... | collective-permute-start | bytes 6881288 | tf_op jit(solution)/shard_map/ppermute | solution.py:65
  123.3 25.1 %collective-permute-start.8 = (bf16[80,7168]{1,0:T(8,128)(2,1)S(1)}, bf16[80,7168]{1,0:T(8,128)(2,1)S(1)}, u32[]{:S(2)}, u32[]{:S(2)}) collective-permute-start(bf16[80,7168]{1,0:T(8,128)(2,1)S(1)} %slice.185), channel_id=1, source_target_pairs={{0,1},{1,2},{2,3},{3,0},{4,5},{5,6},{6,7},{7,4},{8,9},{9,10},{10,1... | collective-permute-start | bytes 3440648 | tf_op jit(solution)/shard_map/ppermute | solution.py:65
  149.8 58.7 %collective-permute-start.13 = (bf16[256,1792]{1,0:T(8,128)(2,1)}, bf16[256,1792]{1,0:T(8,128)(2,1)S(1)}, u32[]{:S(2)}, u32[]{:S(2)}) collective-permute-start(bf16[256,1792]{1,0:T(8,128)(2,1)} %get-tuple-element.95), channel_id=1, source_target_pairs={{0,1},{1,2},{2,3},{3,0},{4,5},{5,6},{6,7},{7,4},{8,9},{9,10},{10,1... | collective-permute-start | bytes 2752520 | tf_op jit(solution)/shard_map/ppermute | solution.py:65
  149.9 58.7 %collective-permute-start.14 = (bf16[256,1792]{1,0:T(8,128)(2,1)}, bf16[256,1792]{1,0:T(8,128)(2,1)S(1)}, u32[]{:S(2)}, u32[]{:S(2)}) collective-permute-start(bf16[256,1792]{1,0:T(8,128)(2,1)} %get-tuple-element.96), channel_id=1, source_target_pairs={{0,2},{1,3},{2,0},{3,1},{4,6},{5,7},{6,4},{7,5},{8,10},{9,11},{10,... | collective-permute-start | bytes 2752520 | tf_op jit(solution)/shard_map/ppermute | solution.py:65
  153.2 55.4 %collective-permute-start.15 = (bf16[256,1792]{1,0:T(8,128)(2,1)}, bf16[256,1792]{1,0:T(8,128)(2,1)S(1)}, u32[]{:S(2)}, u32[]{:S(2)}) collective-permute-start(bf16[256,1792]{1,0:T(8,128)(2,1)} %get-tuple-element.97), channel_id=1, source_target_pairs={{0,3},{1,0},{2,1},{3,2},{4,7},{5,4},{6,5},{7,6},{8,11},{9,8},{10,9... | collective-permute-start | bytes 2752520 | tf_op jit(solution)/shard_map/ppermute | solution.py:65
  162.6 30.8 %collective-permute-start.10 = (bf16[640,256]{1,0:T(8,128)(2,1)S(1)}, bf16[640,256]{1,0:T(8,128)(2,1)S(1)}, u32[]{:S(2)}, u32[]{:S(2)}) collective-permute-start(bf16[640,256]{1,0:T(8,128)(2,1)S(1)} %shard_map.200.refs_0_), channel_id=1, source_target_pairs={{0,1},{1,2},{2,3},{3,0},{4,5},{5,6},{6,7},{7,4},{8,9},{9,10},{10,1... | collective-permute-start | bytes 983048 | tf_op jit(solution)/shard_map/ppermute | solution.py:65
  164.1 44.5 %collective-permute-start.11 = (bf16[640,256]{1,0:T(8,128)(2,1)S(1)}, bf16[640,256]{1,0:T(8,128)(2,1)}, u32[]{:S(2)}, u32[]{:S(2)}) collective-permute-start(bf16[640,256]{1,0:T(8,128)(2,1)S(1)} %shard_map.200.refs_0_), channel_id=1, source_target_pairs={{0,2},{1,3},{2,0},{3,1},{4,6},{5,7},{6,4},{7,5},{8,10},{9,11},{10,... | collective-permute-start | bytes 983048 | tf_op jit(solution)/shard_map/ppermute | solution.py:65
  220.2 59.7 %all-to-all-start.3 = ((bf16[8,80,1792]{2,1,0:T(8,128)(2,1)}), bf16[8,80,1792]{2,1,0:T(8,128)(2,1)}, u32[]{:S(2)}, u32[]{:S(2)}) async-start(bf16[8,80,1792]{2,1,0:T(8,128)(2,1)} %bitcast.78), calls=%async_computation.3 | async-start | bytes 4587520 | tf_op jit(solution)/shard_map/all_to_all | solution.py:77
  224.9 49.7 %collective-permute-start.19 = (bf16[256,1792]{1,0:T(8,128)(2,1)S(1)}, bf16[256,1792]{1,0:T(8,128)(2,1)S(1)}, u32[]{:S(2)}, u32[]{:S(2)}) collective-permute-start(bf16[256,1792]{1,0:T(8,128)(2,1)S(1)} %copy-done.3), channel_id=1, source_target_pairs={{0,1},{1,2},{2,3},{3,0},{4,5},{5,6},{6,7},{7,4},{8,9},{9,10},{10,1... | collective-permute-start | bytes 2752520 | tf_op jit(solution)/shard_map/ppermute | solution.py:65
  225.0 49.6 %collective-permute-start.20 = (bf16[256,1792]{1,0:T(8,128)(2,1)S(1)}, bf16[256,1792]{1,0:T(8,128)(2,1)S(1)}, u32[]{:S(2)}, u32[]{:S(2)}) collective-permute-start(bf16[256,1792]{1,0:T(8,128)(2,1)S(1)} %copy-done.5), channel_id=1, source_target_pairs={{0,2},{1,3},{2,0},{3,1},{4,6},{5,7},{6,4},{7,5},{8,10},{9,11},{10,... | collective-permute-start | bytes 2752520 | tf_op jit(solution)/shard_map/ppermute | solution.py:65
  226.1 48.4 %collective-permute-start.21 = (bf16[256,1792]{1,0:T(8,128)(2,1)S(1)}, bf16[256,1792]{1,0:T(8,128)(2,1)S(1)}, u32[]{:S(2)}, u32[]{:S(2)}) collective-permute-start(bf16[256,1792]{1,0:T(8,128)(2,1)S(1)} %copy-done.7), channel_id=1, source_target_pairs={{0,3},{1,0},{2,1},{3,2},{4,7},{5,4},{6,5},{7,6},{8,11},{9,8},{10,9... | collective-permute-start | bytes 2752520 | tf_op jit(solution)/shard_map/ppermute | solution.py:65
  227.7 34.3 %collective-permute-start.16 = (bf16[640,256]{1,0:T(8,128)(2,1)S(1)}, bf16[640,256]{1,0:T(8,128)(2,1)S(1)}, u32[]{:S(2)}, u32[]{:S(2)}) collective-permute-start(bf16[640,256]{1,0:T(8,128)(2,1)S(1)} %copy-done.30), channel_id=1, source_target_pairs={{0,1},{1,2},{2,3},{3,0},{4,5},{5,6},{6,7},{7,4},{8,9},{9,10},{10,1... | collective-permute-start | bytes 983048 | tf_op jit(solution)/shard_map/ppermute | solution.py:65
  228.3 43.4 %collective-permute-start.17 = (bf16[640,256]{1,0:T(8,128)(2,1)S(1)}, bf16[640,256]{1,0:T(8,128)(2,1)S(1)}, u32[]{:S(2)}, u32[]{:S(2)}) collective-permute-start(bf16[640,256]{1,0:T(8,128)(2,1)S(1)} %copy-done.30), channel_id=1, source_target_pairs={{0,2},{1,3},{2,0},{3,1},{4,6},{5,7},{6,4},{7,5},{8,10},{9,11},{10,... | collective-permute-start | bytes 983048 | tf_op jit(solution)/shard_map/ppermute | solution.py:65
  280.0 43.0 %all-to-all-start.2 = ((bf16[8,80,1792]{2,1,0:T(8,128)(2,1)}), bf16[8,80,1792]{2,1,0:T(8,128)(2,1)S(1)}, u32[]{:S(2)}, u32[]{:S(2)}) async-start(bf16[8,80,1792]{2,1,0:T(8,128)(2,1)} %get-tuple-element.106), calls=%async_computation.2 | async-start | bytes 4587520 | tf_op jit(solution)/shard_map/all_to_all | solution.py:77
  301.1 42.8 %collective-permute-start.28 = (bf16[64,7168]{1,0:T(8,128)(2,1)}, bf16[64,7168]{1,0:T(8,128)(2,1)}, u32[]{:S(2)}, u32[]{:S(2)}) collective-permute-start(bf16[64,7168]{1,0:T(8,128)(2,1)} %shard_map.208), channel_id=1, source_target_pairs={{0,32},{32,64},{64,96},{1,33},{33,65},{65,97},{2,34},{34,66},{66,9... | collective-permute-start | bytes 2752520 | tf_op jit(solution)/shard_map/ppermute | solution.py:369
  (65 other events, 449.3 us)

commit v4 on v3

--- a/solution.py
+++ b/solution.py
@@ -26,21 +26,23 @@
     return lax.dot_general(a, b, (((1,), (1,)), ((), ())), preferred_element_type=F32)
 
 
-def tie(*values):
-    anywhere = [pl.BlockSpec(memory_space=pl.ANY)] * len(values)
+def tie(values, earlier):
+    anywhere = pl.BlockSpec(memory_space=pl.ANY)
+    corner = pl.BlockSpec((16, LANES), lambda i: (0, 0))
     return pl.pallas_call(
         lambda *refs: None,
         out_shape=[jax.ShapeDtypeStruct(value.shape, value.dtype) for value in values],
-        in_specs=anywhere,
-        out_specs=anywhere,
+        in_specs=[anywhere] * len(values) + [corner] * len(earlier),
+        out_specs=[anywhere] * len(values),
+        grid=(1,),
         input_output_aliases={i: i for i in range(len(values))},
-    )(*values)
+    )(*values, *earlier)
 
 
 def call(kernel, out_shape, grid, in_specs, out_specs, scratch=(), moved=0):
     return pl.pallas_call(
         kernel,
-        cost_estimate=pl.CostEstimate(flops=0, transcendentals=0, bytes_accessed=moved),
+        cost_estimate=pl.CostEstimate(flops=moved * 500, transcendentals=0, bytes_accessed=moved),
         out_shape=out_shape,
         grid_spec=pltpu.PrefetchScalarGridSpec(
             num_scalar_prefetch=1, grid=grid, in_specs=in_specs, out_specs=out_specs, scratch_shapes=scratch
@@ -174,7 +176,7 @@
         [weights, weights] + [columns_of(run.shape[0], tile) for run in rows],
         pl.BlockSpec((total, block), lambda j, y: (0, 0)),
         [pltpu.VMEM((total, block), F32)] * 2,
-        moved=20 * 2**20,
+        moved=400 * 2**20,
     )(y, gate, up, *rows)
 
 
@@ -196,7 +198,7 @@
     )(y, target, *pieces)
 
 
-def project(y, units, parts, down, section):
+def project(y, units, parts, down, section, moved):
     rows, depth = units[0].shape
     part = sum(group[0].shape[1] for group in parts)
     tile = part // 2
@@ -230,12 +232,12 @@
         [whole(unit) for unit in units] + [own] + others,
         columns_of(rows, tile),
         [pltpu.VMEM((rows, GROUP * depth), BF)],
-        moved=20 * 2**20,
+        moved=moved,
     )(y, *units, down, *flat)
     return out.reshape(EXPERTS, GROUP * CAP, part)
 
 
-def combine(y, back, key, weight):
+def combine(here, back, key, weight, others=()):
     part, tile = back.shape[2], 896
     back = back.reshape(-1, part)
     tokens = key.shape[0] // GROUP
@@ -243,8 +245,9 @@
     code = codes(range(GROUP))[None]
     high = lax.reduce_precision(weight, 8, 7)
     weights = [high.astype(BF), (weight - high).astype(BF)]
-
-    def kernel(y_ref, key_ref, high_ref, low_ref, onehot_ref, code_ref, back_ref, *refs):
+    given = len(others)
+
+    def kernel(here_ref, key_ref, high_ref, low_ref, onehot_ref, code_ref, back_ref, *refs):
         expand = onehot_ref[...]
         hit = dot_t(key_ref[...], expand) == code_ref[...]
         total = 0.0
@@ -253,36 +256,66 @@
             total += dot(mix, back_ref[...])
         total = total.astype(BF)
         for k in range(GROUP):
-            refs[k][...] = total[k * tokens : (k + 1) * tokens]
-
+            piece = total[k * tokens : (k + 1) * tokens]
+            refs[given + k][...] = piece
+            if given:
+                first = here_ref[1] == 0
+
+                @pl.when(first)
+                def _():
+                    refs[given + GROUP + k][...] = piece
+
+                @pl.when(jnp.logical_not(first))
+                def _():
+                    refs[given + GROUP + k][...] = refs[k][...]
+
+    count = GROUP + given
     return call(
         kernel,
-        [shape(tokens, part)] * GROUP,
+        [shape(tokens, part)] * count,
         (part // tile,),
-        [whole(value) for value in (key, *weights, onehot, code)] + [columns_of(back.shape[0], tile)],
-        [columns_of(tokens, tile)] * GROUP,
-    )(y, key, *weights, onehot, code, back)
-
-
-def home(y, totals, rows):
-    pieces = [totals[0], *shifts(totals[1:])]
-    tokens, part = totals[0].shape
-
-    def kernel(y_ref, rows_ref, *refs):
+        [whole(value) for value in (key, *weights, onehot, code)]
+        + [columns_of(back.shape[0], tile)]
+        + [columns_of(tokens, tile)] * given,
+        [columns_of(tokens, tile)] * count,
+    )(here, key, *weights, onehot, code, back, *others)
+
+
+def send(pieces, ranks, size):
+    return [
+        lax.ppermute(
+            pieces[k],
+            ("pipe", "y"),
+            [(p * GROUP + i, q * GROUP + (i + k) % GROUP) for p, q in ranks for i in range(GROUP)],
+        )
+        for k in range(size)
+    ]
+
+
+def settle(here, last, rows, ahead, behind, kept):
+    tokens, part = kept[0].shape
+    pieces = [*ahead, *behind, *kept]
+
+    def kernel(here_ref, rows_ref, *refs):
+        *refs, out_ref = refs
+        sums = [refs[i * GROUP : (i + 1) * GROUP] for i in range(3)]
         for k in range(GROUP):
 
             @pl.when(pl.program_id(0) == k)
             def _():
-                refs[-1][...] = (rows_ref[...].astype(F32) + refs[k][...].astype(F32)).astype(BF)
-
-    quarter = pl.BlockSpec((tokens, part), lambda k, y: (0, lax.rem(y[0] + GROUP - k, GROUP)))
+                for slot, edge in ((0, 0), (1, last)):
+                    at_edge = here_ref[1] == edge
+                    value = jnp.where(at_edge, sums[2][k][...].astype(F32), sums[slot][k][...].astype(F32))
+                    out_ref[slot] = (rows_ref[slot].astype(F32) + value).astype(BF)
+
+    quarter = pl.BlockSpec((2, tokens, part), lambda k, here: (0, 0, lax.rem(here[0] + GROUP - k, GROUP)))
     return call(
         kernel,
         shape(*rows.shape),
         (GROUP,),
         [quarter] + [whole(piece) for piece in pieces],
         quarter,
-    )(y, rows, *pieces)
+    )(here, rows, *pieces)
 
 
 def local(activations, expert_ids, gate_values, gate_weight, up_weight, down_weight):
@@ -290,8 +323,7 @@
     top = expert_ids.shape[3]
     half = width // 2
     index = lax.axis_index("y").astype(jnp.int32)
-    y = index.reshape(1)
-    pipe_index = lax.axis_index("pipe")
+    y = jnp.stack([index, lax.axis_index("pipe").astype(jnp.int32)])
     last = lax.axis_size("pipe") - 1
     first_rows, second_rows = activations[0, 0], activations[0, 1]
 
@@ -325,52 +357,51 @@
     choose = (dot_t(onehot, key[1]) == codes(range(GROUP))[:, None]).astype(BF)
     turned = [slice(k * tokens, (k + 1) * tokens) for k in (0, 3, 2, 1)]
     key, weight = [[jnp.concatenate([value[cut] for cut in turned]) for value in group] for group in (key, weight)]
-    arrived, choose, key0, key1, weight0, weight1, *rest = tie(
-        arrived, choose, *key, *weight, *near, *cuts0, *cuts1
-    )
-    near, cuts0, cuts1 = rest[:3], rest[3:6], rest[6:]
+    choose, key0, key1, weight0, weight1 = tie([choose, *key, *weight], [arrived, *near])
 
     chosen = dot(choose, jnp.concatenate([second_rows, *near], axis=0)).astype(BF)
     chosen = exchange(chosen.reshape(EXPERTS, GROUP * CAP, width))
 
     ahead, back = shift(arrived, 1), shift(arrived, -1)
     weights = (gate_weight, up_weight)
-    piece = hidden_of(y, [arrived], *weights, 0)
     middle = EXPERTS * CAP // 2
-    ahead, back, piece, *rest = tie(ahead, back, piece, *cuts0, *cuts1)
-    cuts0, cuts1 = rest[:3], rest[3:]
     far = [shift(ahead[:middle], 1), shift(back[middle:], -1)]
-    both = hidden_of(y, [ahead, back], *weights, 0)
-    far0, far1, both, *rest = tie(*far, both, *cuts0, *cuts1)
-    cuts0, cuts1 = rest[:3], rest[3:]
+    both = hidden_of(y, [arrived, ahead, back], *weights, 0)
+    up_one, down_one = [(p, p + 1) for p in range(last)], [(p + 1, p) for p in range(last)]
+    before_rows = lax.ppermute(first_rows, "pipe", up_one)
+    after_rows = lax.ppermute(second_rows, "pipe", down_one)
+    rows = jnp.stack(
+        [jnp.where(y[1] == 0, second_rows, before_rows), jnp.where(y[1] == last, first_rows, after_rows)]
+    )
+    rest = tie([*cuts0, *cuts1, rows], [*far, both])
+    cuts0, cuts1, own_rows = rest[:3], rest[3:6], rest[6]
 
     parts0 = shifts(cuts0)
     rows = np.arange(EXPERTS * CAP)
     target = np.tile((rows // CAP * GROUP * CAP + rows % CAP).astype(np.int32), GROUP)[None]
     step = np.repeat(np.asarray([0, 1, 3, 2], np.int32), EXPERTS * CAP)[None]
-    far_piece = hidden_of(y, [far0, far1], *weights, 0)
-    hidden = arrange(y, target + jnp.bitwise_and(index - step + GROUP, GROUP - 1) * CAP, [piece, both, far_piece])
+    far_piece = hidden_of(y, far, *weights, 0)
+    hidden = arrange(y, target + jnp.bitwise_and(index - step + GROUP, GROUP - 1) * CAP, [both, far_piece])
     units = spread(hidden)
+    cuts1 = tie(cuts1, [*units, *parts0])
+    units = [hidden, *units]
+
+    parts1 = shifts(cuts1)
     hidden_second = hidden_of(y, [chosen.reshape(-1, width)], *weights, 1)
-    hidden_second, *rest = tie(hidden_second, *units, *parts0, *cuts1)
-    units, parts0, cuts1 = [hidden, *rest[:3]], rest[3:6], rest[6:]
-
-    parts1 = shifts(cuts1)
-    units_second = [hidden_second, *spread(hidden_second)]
-    back0 = exchange(project(y, units, [parts0], down_weight, 0))
-    out = project(y, units_second, [parts1], down_weight, 1)
-    out, key0 = tie(out, key0)
+    out = project(y, units, [parts0], down_weight, 0, 0)
+    (later,) = tie([hidden_second], [out.reshape(-1, out.shape[2])])
+    units_second = [hidden_second, shift(hidden_second, 1), shift(later, 2), shift(hidden_second, 3)]
+    back0 = exchange(out)
+    out = project(y, units_second, [parts1], down_weight, 1, 400 * 2**20)
+    out, key0 = tie([out, key0], [])
     back1 = exchange(out)
-    results = [
-        home(y, combine(y, back0, key0, weight0), first_rows),
-        home(y, combine(y, back1, key1, weight1), second_rows),
-    ]
-    size = lax.axis_size("pipe")
-    ahead = lax.ppermute(results[0], "pipe", [(i, i + 1) for i in range(size - 1)])
-    behind = lax.ppermute(results[1], "pipe", [(i + 1, i) for i in range(size - 1)])
-    first = jnp.where(pipe_index == 0, results[1], ahead)
-    second = jnp.where(pipe_index == last, results[0], behind)
-    return jnp.stack([first, second])[None]
+    sums0 = combine(y, back0, key0, weight0)
+    ahead = send(sums0, up_one, GROUP)
+    sums1 = combine(y, back1, key1, weight1, sums0)
+    sums1, kept = sums1[:GROUP], sums1[GROUP:]
+    behind = send(sums1, down_one, GROUP)
+    kept = [kept[0], *send(kept, [(0, 0), (last, last)], GROUP)[1:]]
+    return settle(y, last, own_rows, ahead, behind, kept)[None]
 
 
 def solution(mesh):

time: 362 us -> 360 us (level)
  waiting for transfers between devices: 168 us -> 147 us
  starting transfers between devices: 82.1 us -> 100 us
  local copies, waits for them, and re-layouts: 30.2 us -> 22.8 us
  Pallas kernels: 58.1 us -> 65.2 us
    ppermute x2 -> x13, starting transfers between devices: 23 us -> 51.5 us  [the longest x11 42.7 us: send(): lax.ppermute(pieces[k], ('pipe', 'y'), [(p * GROUP + i, q * GROUP + (i +...]
    ppermute x28 -> x22, waiting for transfers between devices: 141 us -> 122 us  [shift(): lax.ppermute(value, 'y', [(i, (i + steps) % GROUP) for i in range(GROUP)])]
    all_to_all x4, waiting for transfers between devices: 14.3 us -> 0.01 us  [exchange(): lax.all_to_all(value, ('x', 'z'), split_axis=0, concat_axis=0, tiled=True)]
    unnamed x110 -> x75, local copies, waits for them, and re-layouts: 26.9 us -> 13.9 us
    ppermute x2 -> x13, waiting for transfers between devices: 13 us -> 24.4 us  [the longest x1 12.4 us: local(): after_rows = lax.ppermute(second_rows, 'pipe', down_one)]
    ppermute x28 -> x22, starting transfers between devices: 38.7 us -> 28.6 us  [shift(): lax.ppermute(value, 'y', [(i, (i + steps) % GROUP) for i in range(GROUP)])]
    pallas_call x4 -> x3, Pallas kernels: 9.9 us -> 13.3 us  [the longest x2 9.22 us: combine(): call(kernel, [shape(tokens, part)] * count, (part // tile,), [whole(value...]
    pallas_call x4 -> x3, Pallas kernels: 30 us -> 27.2 us  [hidden_of(): call(kernel, shape(total, block), (steps,), [weights, weights] + [columns...]
  transfers between devices with their start and end apart: 34 -> 39, of which waited for: 14 -> 16; matrix products, arithmetic and copies ran while one was open for 3% -> 8% of each run, Pallas kernels for 15% -> 17%
where the time goes in v4:
time: 360 us; the launch traced here: 357 us
  waiting for transfers between devices  147 us (41%)
  starting transfers between devices  100 us (28%)
  Pallas kernels  65.2 us (18%)
  local copies, waits for them, and re-layouts  22.8 us (6%)
  matrix products  12.4 us (3%)
  other arithmetic  9.2 us (3%)
    ppermute x22, waiting for transfers between devices, shift(): lax.ppermute(value, 'y', [(i, (i + steps) % GROUP) for i in range(GROUP)])  122 us
    ppermute x11, starting transfers between devices, send(): lax.ppermute(pieces[k], ('pipe', 'y'), [(p * GROUP + i, q * GROUP + (i +...  42.7 us
    ppermute x22, starting transfers between devices, shift(): lax.ppermute(value, 'y', [(i, (i + steps) % GROUP) for i in range(GROUP)])  28.6 us
    pallas_call x3, Pallas kernels, hidden_of(): call(kernel, shape(total, block), (steps,), [weights, weights] + [columns...  27.2 us
    all_to_all x4, starting transfers between devices, exchange(): lax.all_to_all(value, ('x', 'z'), split_axis=0, concat_axis=0, tiled=True)  20 us
    unnamed x75, local copies, waits for them, and re-layouts  13.9 us
    pallas_call x2, Pallas kernels, project(): call(kernel, shape(rows, part), (2,), [whole(unit) for unit in units] + [...  12.6 us
    ppermute x1, waiting for transfers between devices, local(): after_rows = lax.ppermute(second_rows, 'pipe', down_one)  12.4 us
  transfers between devices with their start and end apart: 39, of which 16 were waited for; matrix products, arithmetic and copies ran while one was open for 8% of the time, Pallas kernels for 17%

profile of v4, /device:TPU:1, one launch (start us, length us, event | category | flops | bytes accessed | tf_op | source)
XLA Modules:
  0.0 357.2 jit_solution(14134377298068173870)
XLA Ops:
  10.2 6.9 %collective-permute-start = (bf16[64,7168]{1,0:T(8,128)(2,1)}, bf16[64,7168]{1,0:T(8,128)(2,1)}, u32[]{:S(2)}, u32[]{:S(2)}) collective-permute-start(bf16[64,7168]{1,0:T(8,128)(2,1)} %get-tuple-element.77), channel_id=1, source_target_pairs={{0,32},{32,64},{64,96},{1,33},{33,65},{65,97},{2,34},{34,66},{66,9... | collective-permute-start | bytes 2752520 | tf_op jit(solution)/shard_map/ppermute | solution.py:371
  20.9 4.6 %all-to-all-start = ((bf16[8,40,3584]{2,1,0:T(8,128)(2,1)}), bf16[8,40,3584]{2,1,0:T(8,128)(2,1)S(1)}, u32[]{:S(2)}, u32[]{:S(2)}) async-start(bf16[8,40,3584]{2,1,0:T(8,128)(2,1)} %bitcast.80), calls=%async_computation | async-start | bytes 4587520 | tf_op jit(solution)/shard_map/all_to_all | solution.py:79
  47.4 12.4 %collective-permute-done.1 = bf16[64,7168]{1,0:T(8,128)(2,1)} collective-permute-done((bf16[64,7168]{1,0:T(8,128)(2,1)}, bf16[64,7168]{1,0:T(8,128)(2,1)}, u32[]{:S(2)}, u32[]{:S(2)}) %collective-permute-start.1) | collective-permute-done | bytes 917536 | tf_op jit(solution)/shard_map/ppermute | solution.py:372
  72.2 8.8 %collective-permute-done.11.refs_8_ = bf16[64,7168]{1,0:T(8,128)(2,1)} collective-permute-done((bf16[64,7168]{1,0:T(8,128)(2,1)}, bf16[64,7168]{1,0:T(8,128)(2,1)}, u32[]{:S(2)}, u32[]{:S(2)}) %collective-permute-start.11) | collective-permute-done | bytes 917536 | tf_op jit(solution)/shard_map/ppermute | solution.py:67
  82.1 8.3 %convolution_convert_fusion = bf16[640,7168]{1,0:T(8,128)(2,1)} fusion(bf16[640,256]{1,0:T(8,128)(2,1)} %get-tuple-element.47, bf16[64,7168]{1,0:T(8,128)(2,1)} %collective-permute-done.11.refs_8_, bf16[64,7168]{1,0:T(8,128)(2,1)} %collective-permute-done.10.refs_7_, bf16[64,7168]{1,0:T(8,128)(2,1)} %collective-permute-done.9.refs_6_, ...), kind=kOutput, calls=%fused_computation | convolution fusion | flops 2368077824 | bytes 13172736 | tf_op jit(solution)/shard_map/dot_general | solution.py:22
  90.4 5.4 %all-to-all-start.1 = ((bf16[8,80,7168]{2,1,0:T(8,128)(2,1)}), bf16[8,80,7168]{2,1,0:T(8,128)(2,1)}, u32[]{:S(2)}, u32[]{:S(2)}) async-start(bf16[8,80,7168]{2,1,0:T(8,128)(2,1)} %bitcast.79), calls=%async_computation.1 | async-start | bytes 18350080 | tf_op jit(solution)/shard_map/all_to_all | solution.py:79
  95.8 34.5 %collective-permute-done.2.refs_1_ = bf16[160,7168]{1,0:T(8,128)(2,1)} collective-permute-done((bf16[160,7168]{1,0:T(8,128)(2,1)S(1)}, bf16[160,7168]{1,0:T(8,128)(2,1)}, u32[]{:S(2)}, u32[]{:S(2)}) %collective-permute-start.2) | collective-permute-done | bytes 2293792 | tf_op jit(solution)/shard_map/ppermute | solution.py:67
  137.8 9.1 %shard_map.193.refs_9_.refs_0_ = bf16[480,256]{1,0:T(8,128)(2,1)S(1)} custom-call(s32[2]{0:T(128)S(1)} %pad_add_fusion.y_ref.here_ref, bf16[1,2,7168,256]{3,2,1,0:T(8,128)(2,1)} %gate_ref.5, bf16[1,2,7168,256]{3,2,1,0:T(8,128)(2,1)} %up_ref.5, bf16[160,7168]{1,0:T(8,128)(2,1)S(1)} %copy-done.2, bf16[160,7168]{1,0:T(8,128)(2,1)} %collective-permute-done.2.refs_1_, ...), custom_call_target="tpu_custom_call" | custom-call | flops 209715200000 | bytes 419430400 | tf_op jit(solution)/shard_map/pallas_call | solution.py:172
  147.6 13.2 %collective-permute-done.3.refs_7_.refs_0_ = bf16[80,7168]{1,0:T(8,128)(2,1)} collective-permute-done((bf16[80,7168]{1,0:T(8,128)(2,1)}, bf16[80,7168]{1,0:T(8,128)(2,1)}, u32[]{:S(2)}, u32[]{:S(2)}) %collective-permute-start.3) | collective-permute-done | bytes 1146912 | tf_op jit(solution)/shard_map/ppermute | solution.py:67
  162.7 4.6 %collective-permute-start.17 = (bf16[256,1792]{1,0:T(8,128)(2,1)}, bf16[256,1792]{1,0:T(8,128)(2,1)}, u32[]{:S(2)}, u32[]{:S(2)}) collective-permute-start(bf16[256,1792]{1,0:T(8,128)(2,1)} %get-tuple-element.49), channel_id=1, source_target_pairs={{0,2},{1,3},{2,0},{3,1},{4,6},{5,7},{6,4},{7,5},{8,10},{9,11},{10,... | collective-permute-start | bytes 2752520 | tf_op jit(solution)/shard_map/ppermute | solution.py:67
  167.3 7.3 %shard_map.197.refs_1_ = bf16[160,256]{1,0:T(8,128)(2,1)S(1)} custom-call(s32[2]{0:T(128)S(1)} %pad_add_fusion.y_ref.here_ref, bf16[1,2,7168,256]{3,2,1,0:T(8,128)(2,1)} %gate_ref.5, bf16[1,2,7168,256]{3,2,1,0:T(8,128)(2,1)} %up_ref.5, bf16[80,7168]{1,0:T(8,128)(2,1)} %collective-permute-done.3.refs_7_.refs_0_, ...), custom_call_target="tpu_custom_call" | custom-call | flops 209715200000 | bytes 419430400 | tf_op jit(solution)/shard_map/pallas_call | solution.py:172
  177.1 35.1 %collective-permute-done.13.refs_1_.refs_3_ = bf16[640,256]{1,0:T(8,128)(2,1)S(1)} collective-permute-done((bf16[640,256]{1,0:T(8,128)(2,1)S(1)}, bf16[640,256]{1,0:T(8,128)(2,1)S(1)}, u32[]{:S(2)}, u32[]{:S(2)}) %collective-permute-start.13) | collective-permute-done | bytes 327712 | tf_op jit(solution)/shard_map/ppermute | solution.py:67
  213.5 6.7 %collective-permute-done.14.refs_2_.refs_4_ = bf16[640,256]{1,0:T(8,128)(2,1)S(1)} collective-permute-done((bf16[640,256]{1,0:T(8,128)(2,1)S(1)}, bf16[640,256]{1,0:T(8,128)(2,1)S(1)}, u32[]{:S(2)}, u32[]{:S(2)}) %collective-permute-start.14) | collective-permute-done | bytes 327712 | tf_op jit(solution)/shard_map/ppermute | solution.py:67
  227.4 6.3 %shard_map.199.refs_1_ = bf16[640,1792]{1,0:T(8,128)(2,1)} custom-call(s32[2]{0:T(128)S(1)} %pad_add_fusion.y_ref.here_ref, bf16[640,256]{1,0:T(8,128)(2,1)S(1)} %shard_map.198.refs_0_, bf16[640,256]{1,0:T(8,128)(2,1)S(1)} %copy-done.10, bf16[640,256]{1,0:T(8,128)(2,1)S(1)} %copy-done.12, bf16[640,256]{1,0:T(8,128)(2,1)S(1)} %copy-done.14, ...), custom_call_target="tpu_custom_call" | custom-call | tf_op jit(solution)/shard_map/pallas_call | solution.py:228
  233.7 10.8 %shard_map.196.refs_0_ = bf16[640,256]{1,0:T(8,128)(2,1)S(1)} custom-call(s32[2]{0:T(128)S(1)} %pad_add_fusion.y_ref.here_ref, bf16[1,2,7168,256]{3,2,1,0:T(8,128)(2,1)} %gate_ref.5, bf16[1,2,7168,256]{3,2,1,0:T(8,128)(2,1)} %up_ref.5, bf16[640,7168]{1,0:T(8,128)(2,1)} %bitcast.27.refs_0_), custom_call_target="tpu_custom_call" | custom-call | flops 209715200000 | bytes 419430400 | tf_op jit(solution)/shard_map/pallas_call | solution.py:172
  250.4 5.5 %all-to-all-start.2 = ((bf16[8,80,1792]{2,1,0:T(8,128)(2,1)}), bf16[8,80,1792]{2,1,0:T(8,128)(2,1)}, u32[]{:S(2)}, u32[]{:S(2)}) async-start(bf16[8,80,1792]{2,1,0:T(8,128)(2,1)} %bitcast.78), calls=%async_computation.2 | async-start | bytes 4587520 | tf_op jit(solution)/shard_map/all_to_all | solution.py:79
  256.6 11.0 %collective-permute-done.23.refs_7_ = bf16[256,1792]{1,0:T(8,128)(2,1)} collective-permute-done((bf16[256,1792]{1,0:T(8,128)(2,1)}, bf16[256,1792]{1,0:T(8,128)(2,1)}, u32[]{:S(2)}, u32[]{:S(2)}) %collective-permute-start.23) | collective-permute-done | bytes 917536 | tf_op jit(solution)/shard_map/ppermute | solution.py:67
  273.2 4.8 %collective-permute-done.20.refs_3_ = bf16[640,256]{1,0:T(8,128)(2,1)S(1)} collective-permute-done((bf16[640,256]{1,0:T(8,128)(2,1)S(1)}, bf16[640,256]{1,0:T(8,128)(2,1)S(1)}, u32[]{:S(2)}, u32[]{:S(2)}) %collective-permute-start.20) | collective-permute-done | bytes 327712 | tf_op jit(solution)/shard_map/ppermute | solution.py:67
  278.1 6.3 %shard_map.202 = bf16[640,1792]{1,0:T(8,128)(2,1)} custom-call(s32[2]{0:T(128)S(1)} %pad_add_fusion.y_ref.here_ref, bf16[640,256]{1,0:T(8,128)(2,1)S(1)} %shard_map.196.refs_0_, bf16[640,256]{1,0:T(8,128)(2,1)S(1)} %collective-permute-done.12.refs_1_, bf16[640,256]{1,0:T(8,128)(2,1)S(1)} %collective-permute-done.19.refs_2_, ...), custom_call_target="tpu_custom_call" | custom-call | flops 209715200000 | bytes 419430400 | tf_op jit(solution)/shard_map/pallas_call | solution.py:228
  284.4 4.5 %all-to-all-start.3 = ((bf16[8,80,1792]{2,1,0:T(8,128)(2,1)}), bf16[8,80,1792]{2,1,0:T(8,128)(2,1)}, u32[]{:S(2)}, u32[]{:S(2)}) async-start(bf16[8,80,1792]{2,1,0:T(8,128)(2,1)} %get-tuple-element.66), calls=%async_computation.3 | async-start | bytes 4587520 | tf_op jit(solution)/shard_map/all_to_all | solution.py:79
  293.5 23.3 %collective-permute-start.24 = (bf16[64,1792]{1,0:T(8,128)(2,1)S(1)}, bf16[64,1792]{1,0:T(8,128)(2,1)S(1)}, u32[]{:S(2)}, u32[]{:S(2)}) collective-permute-start(bf16[64,1792]{1,0:T(8,128)(2,1)S(1)} %get-tuple-element.60.refs_0_), channel_id=1, source_target_pairs={{0,32},{1,33},{2,34},{3,35},{32,64},{33,65},{34,66},{35,67},{64,96... | collective-permute-start | bytes 688136 | tf_op jit(solution)/shard_map/ppermute | solution.py:286
  323.2 4.8 %shard_map.205 = (bf16[64,1792]{1,0:T(8,128)(2,1)S(1)}, bf16[64,1792]{1,0:T(8,128)(2,1)S(1)}, bf16[64,1792]{1,0:T(8,128)(2,1)S(1)}, bf16[64,1792]{1,0:T(8,128)(2...) custom-call(s32[2]{0:T(128)S(1)} %pad_add_fusion.y_ref.here_ref, ...), custom_call_target="tpu_custom_call" | custom-call | tf_op jit(solution)/shard_map/pallas_call | solution.py:273
  327.9 5.4 %collective-permute-start.28 = (bf16[64,1792]{1,0:T(8,128)(2,1)S(1)}, bf16[64,1792]{1,0:T(8,128)(2,1)S(1)}, u32[]{:S(2)}, u32[]{:S(2)}) collective-permute-start(bf16[64,1792]{1,0:T(8,128)(2,1)S(1)} %get-tuple-element.67), channel_id=1, source_target_pairs={{32,0},{33,1},{34,2},{35,3},{64,32},{65,33},{66,34},{67,35},{96,64... | collective-permute-start | bytes 688136 | tf_op jit(solution)/shard_map/ppermute | solution.py:286
  341.5 10.0 %collective-permute-done.29.refs_5_ = bf16[64,1792]{1,0:T(8,128)(2,1)S(1)} collective-permute-done((bf16[64,1792]{1,0:T(8,128)(2,1)S(1)}, bf16[64,1792]{1,0:T(8,128)(2,1)S(1)}, u32[]{:S(2)}, u32[]{:S(2)}) %collective-permute-start.29) | collective-permute-done | bytes 229408 | tf_op jit(solution)/shard_map/ppermute | solution.py:286
  (184 shorter events, 106.9 us)
Async XLA Ops:
  1.5 38.0 %collective-permute-start.6 = (bf16[64,128]{0,1:T(8,128)(2,1)S(1)}, bf16[64,128]{0,1:T(8,128)(2,1)S(1)}, u32[]{:S(2)}, u32[]{:S(2)}) collective-permute-start(bf16[64,128]{0,1:T(8,128)(2,1)S(1)} %concatenate.34), channel_id=1, source_target_pairs={{0,1},{1,2},{2,3},{3,0},{4,5},{5,6},{6,7},{7,4},{8,9},{9,10},{10,1... | collective-permute-start | bytes 49160 | tf_op jit(solution)/shard_map/ppermute | solution.py:67
  3.7 36.0 %collective-permute-start.7 = (bf16[64,128]{0,1:T(8,128)(2,1)S(1)}, bf16[64,128]{0,1:T(8,128)(2,1)S(1)}, u32[]{:S(2)}, u32[]{:S(2)}) collective-permute-start(bf16[64,128]{0,1:T(8,128)(2,1)S(1)} %concatenate.34), channel_id=1, source_target_pairs={{0,2},{1,3},{2,0},{3,1},{4,6},{5,7},{6,4},{7,5},{8,10},{9,11},{10,... | collective-permute-start | bytes 49160 | tf_op jit(solution)/shard_map/ppermute | solution.py:67
  6.3 36.1 %collective-permute-start.8 = (bf16[64,128]{0,1:T(8,128)(2,1)S(1)}, bf16[64,128]{0,1:T(8,128)(2,1)S(1)}, u32[]{:S(2)}, u32[]{:S(2)}) collective-permute-start(bf16[64,128]{0,1:T(8,128)(2,1)S(1)} %concatenate.34), channel_id=1, source_target_pairs={{0,3},{1,0},{2,1},{3,2},{4,7},{5,4},{6,5},{7,6},{8,11},{9,8},{10,9... | collective-permute-start | bytes 49160 | tf_op jit(solution)/shard_map/ppermute | solution.py:67
  10.2 49.6 %collective-permute-start = (bf16[64,7168]{1,0:T(8,128)(2,1)}, bf16[64,7168]{1,0:T(8,128)(2,1)}, u32[]{:S(2)}, u32[]{:S(2)}) collective-permute-start(bf16[64,7168]{1,0:T(8,128)(2,1)} %get-tuple-element.77), channel_id=1, source_target_pairs={{0,32},{32,64},{64,96},{1,33},{33,65},{65,97},{2,34},{34,66},{66,9... | collective-permute-start | bytes 2752520 | tf_op jit(solution)/shard_map/ppermute | solution.py:371
  20.9 41.9 %all-to-all-start = ((bf16[8,40,3584]{2,1,0:T(8,128)(2,1)}), bf16[8,40,3584]{2,1,0:T(8,128)(2,1)S(1)}, u32[]{:S(2)}, u32[]{:S(2)}) async-start(bf16[8,40,3584]{2,1,0:T(8,128)(2,1)} %bitcast.80), calls=%async_computation | async-start | bytes 4587520 | tf_op jit(solution)/shard_map/all_to_all | solution.py:79
  25.5 34.3 %collective-permute-start.1 = (bf16[64,7168]{1,0:T(8,128)(2,1)}, bf16[64,7168]{1,0:T(8,128)(2,1)}, u32[]{:S(2)}, u32[]{:S(2)}) collective-permute-start(bf16[64,7168]{1,0:T(8,128)(2,1)} %get-tuple-element.78), channel_id=1, source_target_pairs={{32,0},{64,32},{96,64},{33,1},{65,33},{97,65},{34,2},{66,34},{98,6... | collective-permute-start | bytes 2752520 | tf_op jit(solution)/shard_map/ppermute | solution.py:372
  39.5 32.7 %collective-permute-start.10 = (bf16[64,7168]{1,0:T(8,128)(2,1)}, bf16[64,7168]{1,0:T(8,128)(2,1)}, u32[]{:S(2)}, u32[]{:S(2)}) collective-permute-start(bf16[64,7168]{1,0:T(8,128)(2,1)} %get-tuple-element.78), channel_id=1, source_target_pairs={{0,2},{1,3},{2,0},{3,1},{4,6},{5,7},{6,4},{7,5},{8,10},{9,11},{10,... | collective-permute-start | bytes 2752520 | tf_op jit(solution)/shard_map/ppermute | solution.py:67
  39.7 41.3 %collective-permute-start.11 = (bf16[64,7168]{1,0:T(8,128)(2,1)}, bf16[64,7168]{1,0:T(8,128)(2,1)}, u32[]{:S(2)}, u32[]{:S(2)}) collective-permute-start(bf16[64,7168]{1,0:T(8,128)(2,1)} %get-tuple-element.78), channel_id=1, source_target_pairs={{0,3},{1,0},{2,1},{3,2},{4,7},{5,4},{6,5},{7,6},{8,11},{9,8},{10,9... | collective-permute-start | bytes 2752520 | tf_op jit(solution)/shard_map/ppermute | solution.py:67
  42.4 39.0 %collective-permute-start.9 = (bf16[64,7168]{1,0:T(8,128)(2,1)}, bf16[64,7168]{1,0:T(8,128)(2,1)}, u32[]{:S(2)}, u32[]{:S(2)}) collective-permute-start(bf16[64,7168]{1,0:T(8,128)(2,1)} %get-tuple-element.78), channel_id=1, source_target_pairs={{0,1},{1,2},{2,3},{3,0},{4,5},{5,6},{6,7},{7,4},{8,9},{9,10},{10,1... | collective-permute-start | bytes 2752520 | tf_op jit(solution)/shard_map/ppermute | solution.py:67
  68.1 62.3 %collective-permute-start.2 = (bf16[160,7168]{1,0:T(8,128)(2,1)S(1)}, bf16[160,7168]{1,0:T(8,128)(2,1)}, u32[]{:S(2)}, u32[]{:S(2)}) collective-permute-start(bf16[160,7168]{1,0:T(8,128)(2,1)S(1)} %shard_map.192.refs_0_.refs_5_), channel_id=1, source_target_pairs={{0,1},{1,2},{2,3},{3,0},{4,5},{5,6},{6,7},{7,4},{8,9},{9,10},{10,1... | collective-permute-start | bytes 6881288 | tf_op jit(solution)/shard_map/ppermute | solution.py:67
  68.5 64.2 %collective-permute-start.4 = (bf16[160,7168]{1,0:T(8,128)(2,1)S(1)}, bf16[160,7168]{1,0:T(8,128)(2,1)}, u32[]{:S(2)}, u32[]{:S(2)}) collective-permute-start(bf16[160,7168]{1,0:T(8,128)(2,1)S(1)} %shard_map.192.refs_0_.refs_5_), channel_id=1, source_target_pairs={{0,3},{1,0},{2,1},{3,2},{4,7},{5,4},{6,5},{7,6},{8,11},{9,8},{10,9... | collective-permute-start | bytes 6881288 | tf_op jit(solution)/shard_map/ppermute | solution.py:67
  90.4 143.3 %all-to-all-start.1 = ((bf16[8,80,7168]{2,1,0:T(8,128)(2,1)}), bf16[8,80,7168]{2,1,0:T(8,128)(2,1)}, u32[]{:S(2)}, u32[]{:S(2)}) async-start(bf16[8,80,7168]{2,1,0:T(8,128)(2,1)} %bitcast.79), calls=%async_computation.1 | async-start | bytes 18350080 | tf_op jit(solution)/shard_map/all_to_all | solution.py:79
  162.7 57.5 %collective-permute-start.16 = (bf16[256,1792]{1,0:T(8,128)(2,1)}, bf16[256,1792]{1,0:T(8,128)(2,1)}, u32[]{:S(2)}, u32[]{:S(2)}) collective-permute-start(bf16[256,1792]{1,0:T(8,128)(2,1)} %get-tuple-element.48), channel_id=1, source_target_pairs={{0,1},{1,2},{2,3},{3,0},{4,5},{5,6},{6,7},{7,4},{8,9},{9,10},{10,1... | collective-permute-start | bytes 2752520 | tf_op jit(solution)/shard_map/ppermute | solution.py:67
  162.7 57.5 %collective-permute-start.17 = (bf16[256,1792]{1,0:T(8,128)(2,1)}, bf16[256,1792]{1,0:T(8,128)(2,1)}, u32[]{:S(2)}, u32[]{:S(2)}) collective-permute-start(bf16[256,1792]{1,0:T(8,128)(2,1)} %get-tuple-element.49), channel_id=1, source_target_pairs={{0,2},{1,3},{2,0},{3,1},{4,6},{5,7},{6,4},{7,5},{8,10},{9,11},{10,... | collective-permute-start | bytes 2752520 | tf_op jit(solution)/shard_map/ppermute | solution.py:67
  167.3 52.9 %collective-permute-start.18 = (bf16[256,1792]{1,0:T(8,128)(2,1)}, bf16[256,1792]{1,0:T(8,128)(2,1)}, u32[]{:S(2)}, u32[]{:S(2)}) collective-permute-start(bf16[256,1792]{1,0:T(8,128)(2,1)} %get-tuple-element.50), channel_id=1, source_target_pairs={{0,3},{1,0},{2,1},{3,2},{4,7},{5,4},{6,5},{7,6},{8,11},{9,8},{10,9... | collective-permute-start | bytes 2752520 | tf_op jit(solution)/shard_map/ppermute | solution.py:67
  175.6 36.7 %collective-permute-start.13 = (bf16[640,256]{1,0:T(8,128)(2,1)S(1)}, bf16[640,256]{1,0:T(8,128)(2,1)S(1)}, u32[]{:S(2)}, u32[]{:S(2)}) collective-permute-start(bf16[640,256]{1,0:T(8,128)(2,1)S(1)} %shard_map.198.refs_0_), channel_id=1, source_target_pairs={{0,1},{1,2},{2,3},{3,0},{4,5},{5,6},{6,7},{7,4},{8,9},{9,10},{10,1... | collective-permute-start | bytes 983048 | tf_op jit(solution)/shard_map/ppermute | solution.py:67
  177.1 43.1 %collective-permute-start.14 = (bf16[640,256]{1,0:T(8,128)(2,1)S(1)}, bf16[640,256]{1,0:T(8,128)(2,1)S(1)}, u32[]{:S(2)}, u32[]{:S(2)}) collective-permute-start(bf16[640,256]{1,0:T(8,128)(2,1)S(1)} %shard_map.198.refs_0_), channel_id=1, source_target_pairs={{0,2},{1,3},{2,0},{3,1},{4,6},{5,7},{6,4},{7,5},{8,10},{9,11},{10,... | collective-permute-start | bytes 983048 | tf_op jit(solution)/shard_map/ppermute | solution.py:67
  221.8 34.8 %collective-permute-start.22 = (bf16[256,1792]{1,0:T(8,128)(2,1)}, bf16[256,1792]{1,0:T(8,128)(2,1)}, u32[]{:S(2)}, u32[]{:S(2)}) collective-permute-start(bf16[256,1792]{1,0:T(8,128)(2,1)} %get-tuple-element.55), channel_id=1, source_target_pairs={{0,2},{1,3},{2,0},{3,1},{4,6},{5,7},{6,4},{7,5},{8,10},{9,11},{10,... | collective-permute-start | bytes 2752520 | tf_op jit(solution)/shard_map/ppermute | solution.py:67
  223.6 44.0 %collective-permute-start.23 = (bf16[256,1792]{1,0:T(8,128)(2,1)}, bf16[256,1792]{1,0:T(8,128)(2,1)}, u32[]{:S(2)}, u32[]{:S(2)}) collective-permute-start(bf16[256,1792]{1,0:T(8,128)(2,1)} %get-tuple-element.56), channel_id=1, source_target_pairs={{0,3},{1,0},{2,1},{3,2},{4,7},{5,4},{6,5},{7,6},{8,11},{9,8},{10,9... | collective-permute-start | bytes 2752520 | tf_op jit(solution)/shard_map/ppermute | solution.py:67
  245.3 28.0 %collective-permute-start.12 = (bf16[640,256]{1,0:T(8,128)(2,1)S(1)}, bf16[640,256]{1,0:T(8,128)(2,1)S(1)}, u32[]{:S(2)}, u32[]{:S(2)}) collective-permute-start(bf16[640,256]{1,0:T(8,128)(2,1)S(1)} %shard_map.196.refs_0_), channel_id=1, source_target_pairs={{0,1},{1,2},{2,3},{3,0},{4,5},{5,6},{6,7},{7,4},{8,9},{9,10},{10,1... | collective-permute-start | bytes 983048 | tf_op jit(solution)/shard_map/ppermute | solution.py:67
  248.3 29.8 %collective-permute-start.20 = (bf16[640,256]{1,0:T(8,128)(2,1)S(1)}, bf16[640,256]{1,0:T(8,128)(2,1)S(1)}, u32[]{:S(2)}, u32[]{:S(2)}) collective-permute-start(bf16[640,256]{1,0:T(8,128)(2,1)S(1)} %shard_map.196.refs_0_), channel_id=1, source_target_pairs={{0,3},{1,0},{2,1},{3,2},{4,7},{5,4},{6,5},{7,6},{8,11},{9,8},{10,9... | collective-permute-start | bytes 983048 | tf_op jit(solution)/shard_map/ppermute | solution.py:67
  250.4 34.0 %all-to-all-start.2 = ((bf16[8,80,1792]{2,1,0:T(8,128)(2,1)}), bf16[8,80,1792]{2,1,0:T(8,128)(2,1)}, u32[]{:S(2)}, u32[]{:S(2)}) async-start(bf16[8,80,1792]{2,1,0:T(8,128)(2,1)} %bitcast.78), calls=%async_computation.2 | async-start | bytes 4587520 | tf_op jit(solution)/shard_map/all_to_all | solution.py:79
  284.4 38.7 %all-to-all-start.3 = ((bf16[8,80,1792]{2,1,0:T(8,128)(2,1)}), bf16[8,80,1792]{2,1,0:T(8,128)(2,1)}, u32[]{:S(2)}, u32[]{:S(2)}) async-start(bf16[8,80,1792]{2,1,0:T(8,128)(2,1)} %get-tuple-element.66), calls=%async_computation.3 | async-start | bytes 4587520 | tf_op jit(solution)/shard_map/all_to_all | solution.py:79
  293.5 39.8 %collective-permute-start.24 = (bf16[64,1792]{1,0:T(8,128)(2,1)S(1)}, bf16[64,1792]{1,0:T(8,128)(2,1)S(1)}, u32[]{:S(2)}, u32[]{:S(2)}) collective-permute-start(bf16[64,1792]{1,0:T(8,128)(2,1)S(1)} %get-tuple-element.60.refs_0_), channel_id=1, source_target_pairs={{0,32},{1,33},{2,34},{3,35},{32,64},{33,65},{34,66},{35,67},{64,96... | collective-permute-start | bytes 688136 | tf_op jit(solution)/shard_map/ppermute | solution.py:286
  (52 other events, 620.4 us)

commit v5 on v4

--- a/solution.py
+++ b/solution.py
@@ -107,17 +107,19 @@
 
 
 def unfold(y, pick, value):
-    rows, half = pick.shape[1], value.shape[1]
-
-    def kernel(y_ref, pick_ref, value_ref, out_ref):
-        out_ref[...] = dot(pick_ref[0], value_ref[...]).astype(BF)
-
-    return call(
-        kernel,
-        shape(rows, 2 * half),
+    rows, half = pick.shape[1] // 2, value.shape[1]
+
+    def kernel(y_ref, pick_ref, value_ref, *refs):
+        joined = dot(pick_ref[0], value_ref[...]).astype(BF)
+        for i in range(2):
+            refs[i][...] = joined[i * rows : (i + 1) * rows]
+
+    return call(
+        kernel,
+        [shape(rows, 2 * half)] * 2,
         (2,),
         [pl.BlockSpec((1,) + pick.shape[1:], lambda h, y: (h, 0, 0)), whole(value)],
-        columns_of(rows, half),
+        [columns_of(rows, half)] * 2,
     )(y, pick, value)
 
 
@@ -237,7 +239,7 @@
     return out.reshape(EXPERTS, GROUP * CAP, part)
 
 
-def combine(here, back, key, weight, others=()):
+def combine(here, back, key, weight, rows=()):
     part, tile = back.shape[2], 896
     back = back.reshape(-1, part)
     tokens = key.shape[0] // GROUP
@@ -245,7 +247,7 @@
     code = codes(range(GROUP))[None]
     high = lax.reduce_precision(weight, 8, 7)
     weights = [high.astype(BF), (weight - high).astype(BF)]
-    given = len(others)
+    given = len(rows)
 
     def kernel(here_ref, key_ref, high_ref, low_ref, onehot_ref, code_ref, back_ref, *refs):
         expand = onehot_ref[...]
@@ -254,31 +256,41 @@
         for ref in (high_ref, low_ref):
             mix = jnp.where(hit, dot_t(ref[...], expand), 0.0).astype(BF)
             total += dot(mix, back_ref[...])
-        total = total.astype(BF)
         for k in range(GROUP):
             piece = total[k * tokens : (k + 1) * tokens]
-            refs[given + k][...] = piece
             if given:
-                first = here_ref[1] == 0
-
-                @pl.when(first)
-                def _():
-                    refs[given + GROUP + k][...] = piece
-
-                @pl.when(jnp.logical_not(first))
-                def _():
-                    refs[given + GROUP + k][...] = refs[k][...]
-
-    count = GROUP + given
-    return call(
-        kernel,
-        [shape(tokens, part)] * count,
+                piece = piece + refs[k][...].astype(F32)
+            refs[given + k][...] = piece.astype(BF)
+
+    own = pl.BlockSpec((tokens, tile), lambda j, here: (0, here[0] * (part // tile) + j))
+    return call(
+        kernel,
+        [shape(tokens, part)] * GROUP,
         (part // tile,),
-        [whole(value) for value in (key, *weights, onehot, code)]
-        + [columns_of(back.shape[0], tile)]
-        + [columns_of(tokens, tile)] * given,
-        [columns_of(tokens, tile)] * count,
-    )(here, key, *weights, onehot, code, back, *others)
+        [whole(value) for value in (key, *weights, onehot, code)] + [columns_of(back.shape[0], tile)] + [own] * given,
+        [columns_of(tokens, tile)] * GROUP,
+    )(here, key, *weights, onehot, code, back, *rows)
+
+
+def home(here, totals, rows):
+    pieces = [totals[0], *shifts(totals[1:])]
+    tokens, part = totals[0].shape
+
+    def kernel(here_ref, rows_ref, *refs):
+        for k in range(GROUP):
+
+            @pl.when(pl.program_id(0) == k)
+            def _():
+                refs[-1][...] = (rows_ref[...].astype(F32) + refs[k][...].astype(F32)).astype(BF)
+
+    quarter = pl.BlockSpec((tokens, part), lambda k, here: (0, lax.rem(here[0] + GROUP - k, GROUP)))
+    return call(
+        kernel,
+        shape(*rows.shape),
+        (GROUP,),
+        [quarter] + [whole(piece) for piece in pieces],
+        quarter,
+    )(here, rows, *pieces)
 
 
 def send(pieces, ranks, size):
@@ -292,30 +304,30 @@
     ]
 
 
-def settle(here, last, rows, ahead, behind, kept):
+def settle(here, last, ahead, own, behind, kept):
     tokens, part = kept[0].shape
-    pieces = [*ahead, *behind, *kept]
-
-    def kernel(here_ref, rows_ref, *refs):
+
+    def kernel(here_ref, ahead_ref, own_ref, *refs):
         *refs, out_ref = refs
-        sums = [refs[i * GROUP : (i + 1) * GROUP] for i in range(3)]
         for k in range(GROUP):
 
             @pl.when(pl.program_id(0) == k)
             def _():
-                for slot, edge in ((0, 0), (1, last)):
-                    at_edge = here_ref[1] == edge
-                    value = jnp.where(at_edge, sums[2][k][...].astype(F32), sums[slot][k][...].astype(F32))
-                    out_ref[slot] = (rows_ref[slot].astype(F32) + value).astype(BF)
-
-    quarter = pl.BlockSpec((2, tokens, part), lambda k, here: (0, 0, lax.rem(here[0] + GROUP - k, GROUP)))
-    return call(
-        kernel,
-        shape(*rows.shape),
+                first, final = here_ref[1] == 0, here_ref[1] == last
+                out_ref[0] = jnp.where(first, refs[GROUP + k][...], ahead_ref[...])
+                out_ref[1] = jnp.where(final, own_ref[...], refs[k][...])
+
+    def column(k, here):
+        return lax.rem(here[0] + GROUP - k, GROUP)
+
+    quarter = pl.BlockSpec((tokens, part), lambda k, here: (0, column(k, here)))
+    return call(
+        kernel,
+        shape(2, *own.shape),
         (GROUP,),
-        [quarter] + [whole(piece) for piece in pieces],
-        quarter,
-    )(here, rows, *pieces)
+        [quarter] * 2 + [whole(piece) for piece in (*behind, *kept)],
+        pl.BlockSpec((2, tokens, part), lambda k, here: (0, 0, column(k, here))),
+    )(here, ahead, own, *behind, *kept)
 
 
 def local(activations, expert_ids, gate_values, gate_weight, up_weight, down_weight):
@@ -357,24 +369,18 @@
     choose = (dot_t(onehot, key[1]) == codes(range(GROUP))[:, None]).astype(BF)
     turned = [slice(k * tokens, (k + 1) * tokens) for k in (0, 3, 2, 1)]
     key, weight = [[jnp.concatenate([value[cut] for cut in turned]) for value in group] for group in (key, weight)]
-    choose, key0, key1, weight0, weight1 = tie([choose, *key, *weight], [arrived, *near])
+    choose, key0, key1, weight0, weight1 = tie([choose, *key, *weight], [*arrived, *near])
 
     chosen = dot(choose, jnp.concatenate([second_rows, *near], axis=0)).astype(BF)
     chosen = exchange(chosen.reshape(EXPERTS, GROUP * CAP, width))
 
-    ahead, back = shift(arrived, 1), shift(arrived, -1)
+    ahead, back = [[shift(run, steps) for run in arrived] for steps in (1, -1)]
     weights = (gate_weight, up_weight)
-    middle = EXPERTS * CAP // 2
-    far = [shift(ahead[:middle], 1), shift(back[middle:], -1)]
-    both = hidden_of(y, [arrived, ahead, back], *weights, 0)
+    far = [shift(ahead[0], 1), shift(back[1], -1)]
+    both = hidden_of(y, [*arrived, *ahead, *back], *weights, 0)
     up_one, down_one = [(p, p + 1) for p in range(last)], [(p + 1, p) for p in range(last)]
-    before_rows = lax.ppermute(first_rows, "pipe", up_one)
-    after_rows = lax.ppermute(second_rows, "pipe", down_one)
-    rows = jnp.stack(
-        [jnp.where(y[1] == 0, second_rows, before_rows), jnp.where(y[1] == last, first_rows, after_rows)]
-    )
-    rest = tie([*cuts0, *cuts1, rows], [*far, both])
-    cuts0, cuts1, own_rows = rest[:3], rest[3:6], rest[6]
+    rest = tie([*cuts0, *cuts1], [*far, both])
+    cuts0, cuts1 = rest[:3], rest[3:]
 
     parts0 = shifts(cuts0)
     rows = np.arange(EXPERTS * CAP)
@@ -387,21 +393,21 @@
     units = [hidden, *units]
 
     parts1 = shifts(cuts1)
-    hidden_second = hidden_of(y, [chosen.reshape(-1, width)], *weights, 1)
     out = project(y, units, [parts0], down_weight, 0, 0)
-    (later,) = tie([hidden_second], [out.reshape(-1, out.shape[2])])
-    units_second = [hidden_second, shift(hidden_second, 1), shift(later, 2), shift(hidden_second, 3)]
+    (here,) = tie([y], [out.reshape(-1, out.shape[2])])
+    hidden_second = hidden_of(here, [chosen.reshape(-1, width)], *weights, 1)
+    units_second = [hidden_second, *spread(hidden_second)]
     back0 = exchange(out)
-    out = project(y, units_second, [parts1], down_weight, 1, 400 * 2**20)
+    out = project(y, units_second, [parts1], down_weight, 1, 0)
     out, key0 = tie([out, key0], [])
     back1 = exchange(out)
-    sums0 = combine(y, back0, key0, weight0)
-    ahead = send(sums0, up_one, GROUP)
-    sums1 = combine(y, back1, key1, weight1, sums0)
-    sums1, kept = sums1[:GROUP], sums1[GROUP:]
+    result0 = home(y, combine(y, back0, key0, weight0), first_rows)
+    ahead = lax.ppermute(result0, "pipe", up_one)
+    turned = [second_rows, near[2], near[1], near[0]]
+    sums1 = combine(y, back1, key1, weight1, turned)
     behind = send(sums1, down_one, GROUP)
-    kept = [kept[0], *send(kept, [(0, 0), (last, last)], GROUP)[1:]]
-    return settle(y, last, own_rows, ahead, behind, kept)[None]
+    kept = [sums1[0], *send(sums1, [(0, 0)], GROUP)[1:]]
+    return settle(y, last, ahead, result0, behind, kept)[None]
 
 
 def solution(mesh):

time: 360 us -> 332 us (0.922)
  starting transfers between devices: 100 us -> 74.1 us
  waiting for transfers between devices: 147 us -> 160 us
  local copies, waits for them, and re-layouts: 22.8 us -> 10.5 us
    ppermute x11 -> x7, starting transfers between devices: 42.7 us -> 16.6 us  [send(): lax.ppermute(pieces[k], ('pipe', 'y'), [(p * GROUP + i, q * GROUP + (i +...]
    all_to_all x4, waiting for transfers between devices: 0.01 us -> 22.3 us  [exchange(): lax.all_to_all(value, ('x', 'z'), split_axis=0, concat_axis=0, tiled=True)]
    ppermute x2 -> x1, waiting for transfers between devices: 12.4 us -> 0.01 us  [local(): ahead = lax.ppermute(result0, 'pipe', up_one)]
    ppermute x22 -> x27, waiting for transfers between devices: 122 us -> 129 us  [shift(): lax.ppermute(value, 'y', [(i, (i + steps) % GROUP) for i in range(GROUP)])]
    unnamed x75 -> x67, local copies, waits for them, and re-layouts: 13.9 us -> 8.71 us
    slice x2 -> x0, local copies, waits for them, and re-layouts: 4.76 us -> none  [local(): far = [shift(ahead[:middle], 1), shift(back[middle:], -1)]]
    another operation x3 -> x1, other arithmetic: 5.12 us -> 0.7 us  [the longest x2 4.42 us: local(): jnp.stack([jnp.where(y[1] == 0, second_rows, before_rows), jnp.where(y[1]...]
    ppermute x11 -> x7, waiting for transfers between devices: 12 us -> 9.07 us  [send(): lax.ppermute(pieces[k], ('pipe', 'y'), [(p * GROUP + i, q * GROUP + (i +...]
  transfers between devices with their start and end apart: 39 -> 39, of which waited for: 16 -> 14; matrix products, arithmetic and copies ran while one was open for 8% -> 6% of each run, Pallas kernels for 17% -> 19%
where the time goes in v5:
time: 332 us; the launch traced here: 331 us
  waiting for transfers between devices  160 us (48%)
  starting transfers between devices  74.1 us (22%)
  Pallas kernels  65.8 us (20%)
  matrix products  12 us (4%)
  local copies, waits for them, and re-layouts  10.5 us (3%)
  other arithmetic  7.56 us (2%)
    ppermute x27, waiting for transfers between devices, shift(): lax.ppermute(value, 'y', [(i, (i + steps) % GROUP) for i in range(GROUP)])  129 us
    ppermute x27, starting transfers between devices, shift(): lax.ppermute(value, 'y', [(i, (i + steps) % GROUP) for i in range(GROUP)])  31.4 us
    pallas_call x3, Pallas kernels, hidden_of(): call(kernel, shape(total, block), (steps,), [weights, weights] + [columns...  27.2 us
    all_to_all x4, waiting for transfers between devices, exchange(): lax.all_to_all(value, ('x', 'z'), split_axis=0, concat_axis=0, tiled=True)  22.3 us
    all_to_all x4, starting transfers between devices, exchange(): lax.all_to_all(value, ('x', 'z'), split_axis=0, concat_axis=0, tiled=True)  19.5 us
    ppermute x7, starting transfers between devices, send(): lax.ppermute(pieces[k], ('pipe', 'y'), [(p * GROUP + i, q * GROUP + (i +...  16.6 us
    pallas_call x2, Pallas kernels, project(): call(kernel, shape(rows, part), (2,), [whole(unit) for unit in units] + [...  12.6 us
    dot_general x5, matrix products, dot(): return jnp.dot(a, b, preferred_element_type=F32)  11.1 us
  transfers between devices with their start and end apart: 39, of which 14 were waited for; matrix products, arithmetic and copies ran while one was open for 6% of the time, Pallas kernels for 19%

profile of v5, /device:TPU:1, one launch (start us, length us, event | category | flops | bytes accessed | tf_op | source)
XLA Modules:
  0.0 331.0 jit_solution(14255392048923261331)
XLA Ops:
  14.8 5.5 %all-to-all-start = ((bf16[8,40,3584]{2,1,0:T(8,128)(2,1)}), bf16[8,40,3584]{2,1,0:T(8,128)(2,1)S(1)}, u32[]{:S(2)}, u32[]{:S(2)}) async-start(bf16[8,40,3584]{2,1,0:T(8,128)(2,1)} %bitcast.72), calls=%async_computation | async-start | bytes 4587520 | tf_op jit(solution)/shard_map/all_to_all | solution.py:79
  37.5 14.3 %all-to-all-done = bf16[8,40,3584]{2,1,0:T(8,128)(2,1)S(1)} async-done(((bf16[8,40,3584]{2,1,0:T(8,128)(2,1)}), bf16[8,40,3584]{2,1,0:T(8,128)(2,1)S(1)}, u32[]{:S(2)}, u32[]{:S(2)}) %all-to-all-start) | async-done | bytes 2293792 | tf_op jit(solution)/shard_map/all_to_all | solution.py:79
  59.3 7.9 %convolution_convert_fusion = bf16[640,7168]{1,0:T(8,128)(2,1)} fusion(bf16[640,256]{1,0:T(8,128)(2,1)} %get-tuple-element.48, bf16[64,7168]{1,0:T(8,128)(2,1)} %collective-permute-done.17.refs_9_.refs_1_, bf16[64,7168]{1,0:T(8,128)(2,1)} %collective-permute-done.16.refs_8_.refs_2_, bf16[64,7168]{1,0:T(8,128)(2,1)} %collective-permute-done.15.refs_7_.refs_3_, ...), kind=kOutput, calls=%fused_computation | convolution fusion | flops 2368077824 | bytes 13172736 | tf_op jit(solution)/shard_map/dot_general | solution.py:22
  67.2 5.0 %all-to-all-start.1 = ((bf16[8,80,7168]{2,1,0:T(8,128)(2,1)}), bf16[8,80,7168]{2,1,0:T(8,128)(2,1)}, u32[]{:S(2)}, u32[]{:S(2)}) async-start(bf16[8,80,7168]{2,1,0:T(8,128)(2,1)} %bitcast.71), calls=%async_computation.1 | async-start | bytes 18350080 | tf_op jit(solution)/shard_map/all_to_all | solution.py:79
  72.3 9.4 %collective-permute-done.refs_2_ = bf16[80,7168]{1,0:T(8,128)(2,1)} collective-permute-done((bf16[80,7168]{1,0:T(8,128)(2,1)}, bf16[80,7168]{1,0:T(8,128)(2,1)}, u32[]{:S(2)}, u32[]{:S(2)}) %collective-permute-start) | collective-permute-done | bytes 1146912 | tf_op jit(solution)/shard_map/ppermute | solution.py:67
  81.7 22.5 %collective-permute-done.3.refs_5_ = bf16[80,7168]{1,0:T(8,128)(2,1)} collective-permute-done((bf16[80,7168]{1,0:T(8,128)(2,1)}, bf16[80,7168]{1,0:T(8,128)(2,1)}, u32[]{:S(2)}, u32[]{:S(2)}) %collective-permute-start.3) | collective-permute-done | bytes 1146912 | tf_op jit(solution)/shard_map/ppermute | solution.py:67
  106.5 9.1 %shard_map.191.refs_0_.refs_8_ = bf16[480,256]{1,0:T(8,128)(2,1)S(1)} custom-call(s32[2]{0:T(128)S(1)} %pad_add_fusion.y_ref.here_ref, bf16[1,2,7168,256]{3,2,1,0:T(8,128)(2,1)} %gate_ref.5, bf16[1,2,7168,256]{3,2,1,0:T(8,128)(2,1)} %up_ref.5, bf16[80,7168]{1,0:T(8,128)(2,1)} %get-tuple-element.37.refs_0_.refs_5_, ...), custom_call_target="tpu_custom_call" | custom-call | flops 209715200000 | bytes 419430400 | tf_op jit(solution)/shard_map/pallas_call | solution.py:174
  116.3 14.5 %collective-permute-done.4.refs_0_.refs_6_ = bf16[80,7168]{1,0:T(8,128)(2,1)} collective-permute-done((bf16[80,7168]{1,0:T(8,128)(2,1)}, bf16[80,7168]{1,0:T(8,128)(2,1)}, u32[]{:S(2)}, u32[]{:S(2)}) %collective-permute-start.4) | collective-permute-done | bytes 1146912 | tf_op jit(solution)/shard_map/ppermute | solution.py:67
  134.2 7.2 %shard_map.192.refs_1_ = bf16[160,256]{1,0:T(8,128)(2,1)S(1)} custom-call(s32[2]{0:T(128)S(1)} %pad_add_fusion.y_ref.here_ref, bf16[1,2,7168,256]{3,2,1,0:T(8,128)(2,1)} %gate_ref.5, bf16[1,2,7168,256]{3,2,1,0:T(8,128)(2,1)} %up_ref.5, bf16[80,7168]{1,0:T(8,128)(2,1)} %collective-permute-done.4.refs_0_.refs_6_, ...), custom_call_target="tpu_custom_call" | custom-call | flops 209715200000 | bytes 419430400 | tf_op jit(solution)/shard_map/pallas_call | solution.py:174
  145.1 38.6 %collective-permute-done.8.refs_3_.refs_5_ = bf16[640,256]{1,0:T(8,128)(2,1)S(1)} collective-permute-done((bf16[640,256]{1,0:T(8,128)(2,1)S(1)}, bf16[640,256]{1,0:T(8,128)(2,1)S(1)}, u32[]{:S(2)}, u32[]{:S(2)}) %collective-permute-start.8) | collective-permute-done | bytes 327712 | tf_op jit(solution)/shard_map/ppermute | solution.py:67
  186.7 7.4 %collective-permute-done.6.refs_1_.refs_3_ = bf16[640,256]{1,0:T(8,128)(2,1)S(1)} collective-permute-done((bf16[640,256]{1,0:T(8,128)(2,1)S(1)}, bf16[640,256]{1,0:T(8,128)(2,1)S(1)}, u32[]{:S(2)}, u32[]{:S(2)}) %collective-permute-start.6) | collective-permute-done | bytes 327712 | tf_op jit(solution)/shard_map/ppermute | solution.py:67
  201.9 6.3 %shard_map.197.refs_1_ = bf16[640,1792]{1,0:T(8,128)(2,1)} custom-call(s32[2]{0:T(128)S(1)} %pad_add_fusion.y_ref.here_ref, bf16[640,256]{1,0:T(8,128)(2,1)S(1)} %shard_map.193.refs_0_, bf16[640,256]{1,0:T(8,128)(2,1)S(1)} %copy-done.12, bf16[640,256]{1,0:T(8,128)(2,1)S(1)} %copy-done.10, bf16[640,256]{1,0:T(8,128)(2,1)S(1)} %copy-done.8, ...), custom_call_target="tpu_custom_call" | custom-call | tf_op jit(solution)/shard_map/pallas_call | solution.py:230
  209.0 4.5 %all-to-all-start.2 = ((bf16[8,80,1792]{2,1,0:T(8,128)(2,1)}), bf16[8,80,1792]{2,1,0:T(8,128)(2,1)}, u32[]{:S(2)}, u32[]{:S(2)}) async-start(bf16[8,80,1792]{2,1,0:T(8,128)(2,1)} %bitcast.27), calls=%async_computation.2 | async-start | bytes 4587520 | tf_op jit(solution)/shard_map/all_to_all | solution.py:79
  213.5 10.8 %shard_map.200.refs_0_ = bf16[640,256]{1,0:T(8,128)(2,1)S(1)} custom-call(s32[2]{0:T(128)S(1)} %copy-done.22, bf16[1,2,7168,256]{3,2,1,0:T(8,128)(2,1)} %gate_ref.5, bf16[1,2,7168,256]{3,2,1,0:T(8,128)(2,1)} %up_ref.5, bf16[640,7168]{1,0:T(8,128)(2,1)} %bitcast.25.refs_0_), custom_call_target="tpu_custom_call" | custom-call | flops 209715200000 | bytes 419430400 | tf_op jit(solution)/shard_map/pallas_call | solution.py:174
  227.4 10.1 %collective-permute-done.22.refs_6_ = bf16[256,1792]{1,0:T(8,128)(2,1)} collective-permute-done((bf16[256,1792]{1,0:T(8,128)(2,1)}, bf16[256,1792]{1,0:T(8,128)(2,1)}, u32[]{:S(2)}, u32[]{:S(2)}) %collective-permute-start.22) | collective-permute-done | bytes 917536 | tf_op jit(solution)/shard_map/ppermute | solution.py:67
  238.5 9.4 %collective-permute-done.20.refs_3_ = bf16[640,256]{1,0:T(8,128)(2,1)S(1)} collective-permute-done((bf16[640,256]{1,0:T(8,128)(2,1)S(1)}, bf16[640,256]{1,0:T(8,128)(2,1)S(1)}, u32[]{:S(2)}, u32[]{:S(2)}) %collective-permute-start.20) | collective-permute-done | bytes 327712 | tf_op jit(solution)/shard_map/ppermute | solution.py:67
  247.9 5.6 %collective-permute-done.18.refs_1_ = bf16[640,256]{1,0:T(8,128)(2,1)S(1)} collective-permute-done((bf16[640,256]{1,0:T(8,128)(2,1)S(1)}, bf16[640,256]{1,0:T(8,128)(2,1)S(1)}, u32[]{:S(2)}, u32[]{:S(2)}) %collective-permute-start.18) | collective-permute-done | bytes 327712 | tf_op jit(solution)/shard_map/ppermute | solution.py:67
  253.5 6.3 %shard_map.202 = bf16[640,1792]{1,0:T(8,128)(2,1)} custom-call(s32[2]{0:T(128)S(1)} %pad_add_fusion.y_ref.here_ref, bf16[640,256]{1,0:T(8,128)(2,1)S(1)} %shard_map.200.refs_0_, bf16[640,256]{1,0:T(8,128)(2,1)S(1)} %collective-permute-done.18.refs_1_, bf16[640,256]{1,0:T(8,128)(2,1)S(1)} %collective-permute-done.19.refs_2_, ...), custom_call_target="tpu_custom_call" | custom-call | tf_op jit(solution)/shard_map/pallas_call | solution.py:230
  271.8 10.4 %collective-permute-done.24.refs_1_ = bf16[64,1792]{1,0:T(8,128)(2,1)S(1)} collective-permute-done((bf16[64,1792]{1,0:T(8,128)(2,1)S(1)}, bf16[64,1792]{1,0:T(8,128)(2,1)S(1)}, u32[]{:S(2)}, u32[]{:S(2)}) %collective-permute-start.24) | collective-permute-done | bytes 229408 | tf_op jit(solution)/shard_map/ppermute | solution.py:67
  283.5 6.6 %collective-permute-start.27 = (bf16[64,7168]{1,0:T(8,128)(2,1)S(1)}, bf16[64,7168]{1,0:T(8,128)(2,1)S(1)}, u32[]{:S(2)}, u32[]{:S(2)}) collective-permute-start(bf16[64,7168]{1,0:T(8,128)(2,1)S(1)} %shard_map.205.own_ref), channel_id=1, source_target_pairs={{0,32},{32,64},{64,96},{1,33},{33,65},{65,97},{2,34},{34,66},{66,9... | collective-permute-start | bytes 2752520 | tf_op jit(solution)/shard_map/ppermute | solution.py:405
  290.1 7.9 %all-to-all-done.3 = bf16[8,80,1792]{2,1,0:T(8,128)(2,1)} async-done(((bf16[8,80,1792]{2,1,0:T(8,128)(2,1)}), bf16[8,80,1792]{2,1,0:T(8,128)(2,1)}, u32[]{:S(2)}, u32[]{:S(2)}) %all-to-all-start.3) | async-done | bytes 2293792 | tf_op jit(solution)/shard_map/all_to_all | solution.py:79
  298.1 4.6 %shard_map.206 = (bf16[64,1792]{1,0:T(8,128)(2,1)S(1)}, bf16[64,1792]{1,0:T(8,128)(2,1)S(1)}, bf16[64,1792]{1,0:T(8,128)(2,1)S(1)}, bf16[64,1792]{1,0:T(8,128)(2,1)S(1)}) custom-call(s32[2]{0:T(128)S(1)} %pad_add_fusion.y_ref.here_ref, bf16[256,128]{1,0:T(8,128)(2,1)S(1)} %copy-done.19, bf16[256,128]{1,0:T(8,128)(2,1)S(1)} %get-tuple-element.74.high_ref, ...), custom_call_target="tpu_custom_call" | custom-call | tf_op jit(solution)/shard_map/pallas_call | solution.py:266
  310.5 5.1 %collective-permute-start.30 = (bf16[64,1792]{1,0:T(8,128)(2,1)S(1)}, bf16[64,1792]{1,0:T(8,128)(2,1)S(1)}, u32[]{:S(2)}, u32[]{:S(2)}) collective-permute-start(bf16[64,1792]{1,0:T(8,128)(2,1)S(1)} %get-tuple-element.67), channel_id=1, source_target_pairs={{32,2},{33,3},{34,0},{35,1},{64,34},{65,35},{66,32},{67,33},{96,66... | collective-permute-start | bytes 688136 | tf_op jit(solution)/shard_map/ppermute | solution.py:298
  319.3 5.6 %collective-permute-done.29.refs_1_ = bf16[64,1792]{1,0:T(8,128)(2,1)S(1)} collective-permute-done((bf16[64,1792]{1,0:T(8,128)(2,1)S(1)}, bf16[64,1792]{1,0:T(8,128)(2,1)S(1)}, u32[]{:S(2)}, u32[]{:S(2)}) %collective-permute-start.29) | collective-permute-done | bytes 229408 | tf_op jit(solution)/shard_map/ppermute | solution.py:298
  (173 shorter events, 95.5 us)
Async XLA Ops:
  1.5 28.1 %collective-permute-start.14 = (bf16[64,128]{0,1:T(8,128)(2,1)S(1)}, bf16[64,128]{0,1:T(8,128)(2,1)S(1)}, u32[]{:S(2)}, u32[]{:S(2)}) collective-permute-start(bf16[64,128]{0,1:T(8,128)(2,1)S(1)} %concatenate.34), channel_id=1, source_target_pairs={{0,3},{1,0},{2,1},{3,2},{4,7},{5,4},{6,5},{7,6},{8,11},{9,8},{10,9... | collective-permute-start | bytes 49160 | tf_op jit(solution)/shard_map/ppermute | solution.py:67
  7.8 48.6 %collective-permute-start.17 = (bf16[64,7168]{1,0:T(8,128)(2,1)S(1)}, bf16[64,7168]{1,0:T(8,128)(2,1)}, u32[]{:S(2)}, u32[]{:S(2)}) collective-permute-start(bf16[64,7168]{1,0:T(8,128)(2,1)S(1)} %get-tuple-element.69.refs_0_), channel_id=1, source_target_pairs={{0,3},{1,0},{2,1},{3,2},{4,7},{5,4},{6,5},{7,6},{8,11},{9,8},{10,9... | collective-permute-start | bytes 2752520 | tf_op jit(solution)/shard_map/ppermute | solution.py:67
  9.8 48.7 %collective-permute-start.16 = (bf16[64,7168]{1,0:T(8,128)(2,1)S(1)}, bf16[64,7168]{1,0:T(8,128)(2,1)}, u32[]{:S(2)}, u32[]{:S(2)}) collective-permute-start(bf16[64,7168]{1,0:T(8,128)(2,1)S(1)} %get-tuple-element.69.refs_0_), channel_id=1, source_target_pairs={{0,2},{1,3},{2,0},{3,1},{4,6},{5,7},{6,4},{7,5},{8,10},{9,11},{10,... | collective-permute-start | bytes 2752520 | tf_op jit(solution)/shard_map/ppermute | solution.py:67
  14.8 37.0 %all-to-all-start = ((bf16[8,40,3584]{2,1,0:T(8,128)(2,1)}), bf16[8,40,3584]{2,1,0:T(8,128)(2,1)S(1)}, u32[]{:S(2)}, u32[]{:S(2)}) async-start(bf16[8,40,3584]{2,1,0:T(8,128)(2,1)} %bitcast.72), calls=%async_computation | async-start | bytes 4587520 | tf_op jit(solution)/shard_map/all_to_all | solution.py:79
  29.6 28.9 %collective-permute-start.15 = (bf16[64,7168]{1,0:T(8,128)(2,1)S(1)}, bf16[64,7168]{1,0:T(8,128)(2,1)}, u32[]{:S(2)}, u32[]{:S(2)}) collective-permute-start(bf16[64,7168]{1,0:T(8,128)(2,1)S(1)} %get-tuple-element.69.refs_0_), channel_id=1, source_target_pairs={{0,1},{1,2},{2,3},{3,0},{4,5},{5,6},{6,7},{7,4},{8,9},{9,10},{10,1... | collective-permute-start | bytes 2752520 | tf_op jit(solution)/shard_map/ppermute | solution.py:67
  54.9 51.6 %collective-permute-start.2 = (bf16[80,7168]{1,0:T(8,128)(2,1)}, bf16[80,7168]{1,0:T(8,128)(2,1)S(1)}, u32[]{:S(2)}, u32[]{:S(2)}) collective-permute-start(bf16[80,7168]{1,0:T(8,128)(2,1)} %get-tuple-element.37.refs_0_.refs_5_), channel_id=1, source_target_pairs={{0,3},{1,0},{2,1},{3,2},{4,7},{5,4},{6,5},{7,6},{8,11},{9,8},{10,9... | collective-permute-start | bytes 3440648 | tf_op jit(solution)/shard_map/ppermute | solution.py:67
  55.9 25.8 %collective-permute-start = (bf16[80,7168]{1,0:T(8,128)(2,1)}, bf16[80,7168]{1,0:T(8,128)(2,1)}, u32[]{:S(2)}, u32[]{:S(2)}) collective-permute-start(bf16[80,7168]{1,0:T(8,128)(2,1)} %get-tuple-element.37.refs_0_.refs_5_), channel_id=1, source_target_pairs={{0,1},{1,2},{2,3},{3,0},{4,5},{5,6},{6,7},{7,4},{8,9},{9,10},{10,1... | collective-permute-start | bytes 3440648 | tf_op jit(solution)/shard_map/ppermute | solution.py:67
  56.4 47.9 %collective-permute-start.3 = (bf16[80,7168]{1,0:T(8,128)(2,1)}, bf16[80,7168]{1,0:T(8,128)(2,1)}, u32[]{:S(2)}, u32[]{:S(2)}) collective-permute-start(bf16[80,7168]{1,0:T(8,128)(2,1)} %get-tuple-element.38.refs_1_.refs_6_), channel_id=1, source_target_pairs={{0,3},{1,0},{2,1},{3,2},{4,7},{5,4},{6,5},{7,6},{8,11},{9,8},{10,9... | collective-permute-start | bytes 3440648 | tf_op jit(solution)/shard_map/ppermute | solution.py:67
  58.6 48.0 %collective-permute-start.1 = (bf16[80,7168]{1,0:T(8,128)(2,1)}, bf16[80,7168]{1,0:T(8,128)(2,1)S(1)}, u32[]{:S(2)}, u32[]{:S(2)}) collective-permute-start(bf16[80,7168]{1,0:T(8,128)(2,1)} %get-tuple-element.38.refs_1_.refs_6_), channel_id=1, source_target_pairs={{0,1},{1,2},{2,3},{3,0},{4,5},{5,6},{6,7},{7,4},{8,9},{9,10},{10,1... | collective-permute-start | bytes 3440648 | tf_op jit(solution)/shard_map/ppermute | solution.py:67
  67.2 141.7 %all-to-all-start.1 = ((bf16[8,80,7168]{2,1,0:T(8,128)(2,1)}), bf16[8,80,7168]{2,1,0:T(8,128)(2,1)}, u32[]{:S(2)}, u32[]{:S(2)}) async-start(bf16[8,80,7168]{2,1,0:T(8,128)(2,1)} %bitcast.71), calls=%async_computation.1 | async-start | bytes 18350080 | tf_op jit(solution)/shard_map/all_to_all | solution.py:79
  81.7 49.2 %collective-permute-start.4 = (bf16[80,7168]{1,0:T(8,128)(2,1)}, bf16[80,7168]{1,0:T(8,128)(2,1)}, u32[]{:S(2)}, u32[]{:S(2)}) collective-permute-start(bf16[80,7168]{1,0:T(8,128)(2,1)} %collective-permute-done.refs_2_), channel_id=1, source_target_pairs={{0,1},{1,2},{2,3},{3,0},{4,5},{5,6},{6,7},{7,4},{8,9},{9,10},{10,1... | collective-permute-start | bytes 3440648 | tf_op jit(solution)/shard_map/ppermute | solution.py:67
  104.2 26.6 %collective-permute-start.5 = (bf16[80,7168]{1,0:T(8,128)(2,1)}, bf16[80,7168]{1,0:T(8,128)(2,1)}, u32[]{:S(2)}, u32[]{:S(2)}) collective-permute-start(bf16[80,7168]{1,0:T(8,128)(2,1)} %collective-permute-done.3.refs_5_), channel_id=1, source_target_pairs={{0,3},{1,0},{2,1},{3,2},{4,7},{5,4},{6,5},{7,6},{8,11},{9,8},{10,9... | collective-permute-start | bytes 3440648 | tf_op jit(solution)/shard_map/ppermute | solution.py:67
  131.5 62.5 %collective-permute-start.9 = (bf16[256,1792]{1,0:T(8,128)(2,1)}, bf16[256,1792]{1,0:T(8,128)(2,1)}, u32[]{:S(2)}, u32[]{:S(2)}) collective-permute-start(bf16[256,1792]{1,0:T(8,128)(2,1)} %get-tuple-element.45), channel_id=1, source_target_pairs={{0,1},{1,2},{2,3},{3,0},{4,5},{5,6},{6,7},{7,4},{8,9},{9,10},{10,1... | collective-permute-start | bytes 2752520 | tf_op jit(solution)/shard_map/ppermute | solution.py:67
  131.5 62.5 %collective-permute-start.10 = (bf16[256,1792]{1,0:T(8,128)(2,1)}, bf16[256,1792]{1,0:T(8,128)(2,1)}, u32[]{:S(2)}, u32[]{:S(2)}) collective-permute-start(bf16[256,1792]{1,0:T(8,128)(2,1)} %get-tuple-element.46), channel_id=1, source_target_pairs={{0,2},{1,3},{2,0},{3,1},{4,6},{5,7},{6,4},{7,5},{8,10},{9,11},{10,... | collective-permute-start | bytes 2752520 | tf_op jit(solution)/shard_map/ppermute | solution.py:67
  133.6 60.5 %collective-permute-start.11 = (bf16[256,1792]{1,0:T(8,128)(2,1)}, bf16[256,1792]{1,0:T(8,128)(2,1)}, u32[]{:S(2)}, u32[]{:S(2)}) collective-permute-start(bf16[256,1792]{1,0:T(8,128)(2,1)} %get-tuple-element.47), channel_id=1, source_target_pairs={{0,3},{1,0},{2,1},{3,2},{4,7},{5,4},{6,5},{7,6},{8,11},{9,8},{10,9... | collective-permute-start | bytes 2752520 | tf_op jit(solution)/shard_map/ppermute | solution.py:67
  142.5 41.3 %collective-permute-start.8 = (bf16[640,256]{1,0:T(8,128)(2,1)S(1)}, bf16[640,256]{1,0:T(8,128)(2,1)S(1)}, u32[]{:S(2)}, u32[]{:S(2)}) collective-permute-start(bf16[640,256]{1,0:T(8,128)(2,1)S(1)} %shard_map.193.refs_0_), channel_id=1, source_target_pairs={{0,3},{1,0},{2,1},{3,2},{4,7},{5,4},{6,5},{7,6},{8,11},{9,8},{10,9... | collective-permute-start | bytes 983048 | tf_op jit(solution)/shard_map/ppermute | solution.py:67
  143.1 43.6 %collective-permute-start.7 = (bf16[640,256]{1,0:T(8,128)(2,1)S(1)}, bf16[640,256]{1,0:T(8,128)(2,1)S(1)}, u32[]{:S(2)}, u32[]{:S(2)}) collective-permute-start(bf16[640,256]{1,0:T(8,128)(2,1)S(1)} %shard_map.193.refs_0_), channel_id=1, source_target_pairs={{0,2},{1,3},{2,0},{3,1},{4,6},{5,7},{6,4},{7,5},{8,10},{9,11},{10,... | collective-permute-start | bytes 983048 | tf_op jit(solution)/shard_map/ppermute | solution.py:67
  195.5 31.9 %collective-permute-start.21 = (bf16[256,1792]{1,0:T(8,128)(2,1)}, bf16[256,1792]{1,0:T(8,128)(2,1)}, u32[]{:S(2)}, u32[]{:S(2)}) collective-permute-start(bf16[256,1792]{1,0:T(8,128)(2,1)} %get-tuple-element.52), channel_id=1, source_target_pairs={{0,1},{1,2},{2,3},{3,0},{4,5},{5,6},{6,7},{7,4},{8,9},{9,10},{10,1... | collective-permute-start | bytes 2752520 | tf_op jit(solution)/shard_map/ppermute | solution.py:67
  196.6 40.9 %collective-permute-start.22 = (bf16[256,1792]{1,0:T(8,128)(2,1)}, bf16[256,1792]{1,0:T(8,128)(2,1)}, u32[]{:S(2)}, u32[]{:S(2)}) collective-permute-start(bf16[256,1792]{1,0:T(8,128)(2,1)} %get-tuple-element.53), channel_id=1, source_target_pairs={{0,2},{1,3},{2,0},{3,1},{4,6},{5,7},{6,4},{7,5},{8,10},{9,11},{10,... | collective-permute-start | bytes 2752520 | tf_op jit(solution)/shard_map/ppermute | solution.py:67
  198.8 39.7 %collective-permute-start.23 = (bf16[256,1792]{1,0:T(8,128)(2,1)}, bf16[256,1792]{1,0:T(8,128)(2,1)}, u32[]{:S(2)}, u32[]{:S(2)}) collective-permute-start(bf16[256,1792]{1,0:T(8,128)(2,1)} %get-tuple-element.54), channel_id=1, source_target_pairs={{0,3},{1,0},{2,1},{3,2},{4,7},{5,4},{6,5},{7,6},{8,11},{9,8},{10,9... | collective-permute-start | bytes 2752520 | tf_op jit(solution)/shard_map/ppermute | solution.py:67
  209.0 50.9 %all-to-all-start.2 = ((bf16[8,80,1792]{2,1,0:T(8,128)(2,1)}), bf16[8,80,1792]{2,1,0:T(8,128)(2,1)}, u32[]{:S(2)}, u32[]{:S(2)}) async-start(bf16[8,80,1792]{2,1,0:T(8,128)(2,1)} %bitcast.27), calls=%async_computation.2 | async-start | bytes 4587520 | tf_op jit(solution)/shard_map/all_to_all | solution.py:79
  227.4 26.1 %collective-permute-start.18 = (bf16[640,256]{1,0:T(8,128)(2,1)S(1)}, bf16[640,256]{1,0:T(8,128)(2,1)S(1)}, u32[]{:S(2)}, u32[]{:S(2)}) collective-permute-start(bf16[640,256]{1,0:T(8,128)(2,1)S(1)} %shard_map.200.refs_0_), channel_id=1, source_target_pairs={{0,1},{1,2},{2,3},{3,0},{4,5},{5,6},{6,7},{7,4},{8,9},{9,10},{10,1... | collective-permute-start | bytes 983048 | tf_op jit(solution)/shard_map/ppermute | solution.py:67
  259.9 38.2 %all-to-all-start.3 = ((bf16[8,80,1792]{2,1,0:T(8,128)(2,1)}), bf16[8,80,1792]{2,1,0:T(8,128)(2,1)}, u32[]{:S(2)}, u32[]{:S(2)}) async-start(bf16[8,80,1792]{2,1,0:T(8,128)(2,1)} %get-tuple-element.64), calls=%async_computation.3 | async-start | bytes 4587520 | tf_op jit(solution)/shard_map/all_to_all | solution.py:79
  283.5 27.0 %collective-permute-start.27 = (bf16[64,7168]{1,0:T(8,128)(2,1)S(1)}, bf16[64,7168]{1,0:T(8,128)(2,1)S(1)}, u32[]{:S(2)}, u32[]{:S(2)}) collective-permute-start(bf16[64,7168]{1,0:T(8,128)(2,1)S(1)} %shard_map.205.own_ref), channel_id=1, source_target_pairs={{0,32},{32,64},{64,96},{1,33},{33,65},{65,97},{2,34},{34,66},{66,9... | collective-permute-start | bytes 2752520 | tf_op jit(solution)/shard_map/ppermute | solution.py:405
  (48 other events, 481.6 us)

commit v6 on v5

--- a/solution.py
+++ b/solution.py
@@ -379,10 +379,10 @@
     far = [shift(ahead[0], 1), shift(back[1], -1)]
     both = hidden_of(y, [*arrived, *ahead, *back], *weights, 0)
     up_one, down_one = [(p, p + 1) for p in range(last)], [(p + 1, p) for p in range(last)]
-    rest = tie([*cuts0, *cuts1], [*far, both])
-    cuts0, cuts1 = rest[:3], rest[3:]
-
-    parts0 = shifts(cuts0)
+    opposite = shift(cuts0[1], 2)
+    cut1, cut3, *cuts1 = tie([cuts0[0], cuts0[2], *cuts1], [*far, both, opposite])
+
+    parts0 = [shift(cut1, 1), opposite, shift(cut3, 3)]
     rows = np.arange(EXPERTS * CAP)
     target = np.tile((rows // CAP * GROUP * CAP + rows % CAP).astype(np.int32), GROUP)[None]
     step = np.repeat(np.asarray([0, 1, 3, 2], np.int32), EXPERTS * CAP)[None]

time: 332 us -> 322 us (0.970)
  waiting for transfers between devices: 160 us -> 146 us
    ppermute x27, waiting for transfers between devices: 129 us -> 118 us  [shift(): lax.ppermute(value, 'y', [(i, (i + steps) % GROUP) for i in range(GROUP)])]
    unnamed x67 -> x65, local copies, waits for them, and re-layouts: 8.71 us -> 8.69 us
  transfers between devices with their start and end apart: 39 -> 39, of which waited for: 14 -> 17; matrix products, arithmetic and copies ran while one was open for 6% -> 6% of each run, Pallas kernels for 19% -> 20%
where the time goes in v6:
time: 322 us; the launch traced here: 321 us
  waiting for transfers between devices  146 us (45%)
  starting transfers between devices  77.3 us (24%)
  Pallas kernels  66.7 us (21%)
  matrix products  12.1 us (4%)
  local copies, waits for them, and re-layouts  10.5 us (3%)
  other arithmetic  7.03 us (2%)
    ppermute x27, waiting for transfers between devices, shift(): lax.ppermute(value, 'y', [(i, (i + steps) % GROUP) for i in range(GROUP)])  118 us
    ppermute x27, starting transfers between devices, shift(): lax.ppermute(value, 'y', [(i, (i + steps) % GROUP) for i in range(GROUP)])  32.3 us
    pallas_call x3, Pallas kernels, hidden_of(): call(kernel, shape(total, block), (steps,), [weights, weights] + [columns...  27.2 us
    all_to_all x4, starting transfers between devices, exchange(): lax.all_to_all(value, ('x', 'z'), split_axis=0, concat_axis=0, tiled=True)  21.3 us
    all_to_all x4, waiting for transfers between devices, exchange(): lax.all_to_all(value, ('x', 'z'), split_axis=0, concat_axis=0, tiled=True)  20 us
    ppermute x7, starting transfers between devices, send(): lax.ppermute(pieces[k], ('pipe', 'y'), [(p * GROUP + i, q * GROUP + (i +...  17.1 us
    pallas_call x2, Pallas kernels, project(): call(kernel, shape(rows, part), (2,), [whole(unit) for unit in units] + [...  12.6 us
    dot_general x5, matrix products, dot(): return jnp.dot(a, b, preferred_element_type=F32)  11.1 us
  transfers between devices with their start and end apart: 39, of which 17 were waited for; matrix products, arithmetic and copies ran while one was open for 6% of the time, Pallas kernels for 20%

profile of v6, /device:TPU:1, one launch (start us, length us, event | category | flops | bytes accessed | tf_op | source)
XLA Modules:
  0.0 320.5 jit_solution(3209294184227277391)
XLA Ops:
  14.8 5.5 %all-to-all-start = ((bf16[8,40,3584]{2,1,0:T(8,128)(2,1)}), bf16[8,40,3584]{2,1,0:T(8,128)(2,1)S(1)}, u32[]{:S(2)}, u32[]{:S(2)}) async-start(bf16[8,40,3584]{2,1,0:T(8,128)(2,1)} %bitcast.72), calls=%async_computation | async-start | bytes 4587520 | tf_op jit(solution)/shard_map/all_to_all | solution.py:79
  39.7 12.1 %all-to-all-done = bf16[8,40,3584]{2,1,0:T(8,128)(2,1)S(1)} async-done(((bf16[8,40,3584]{2,1,0:T(8,128)(2,1)}), bf16[8,40,3584]{2,1,0:T(8,128)(2,1)S(1)}, u32[]{:S(2)}, u32[]{:S(2)}) %all-to-all-start) | async-done | bytes 2293792 | tf_op jit(solution)/shard_map/all_to_all | solution.py:79
  59.4 7.9 %convolution_convert_fusion = bf16[640,7168]{1,0:T(8,128)(2,1)} fusion(bf16[640,256]{1,0:T(8,128)(2,1)} %get-tuple-element.46, bf16[64,7168]{1,0:T(8,128)(2,1)} %collective-permute-done.17.refs_9_.refs_1_, bf16[64,7168]{1,0:T(8,128)(2,1)} %collective-permute-done.16.refs_8_.refs_2_, bf16[64,7168]{1,0:T(8,128)(2,1)} %collective-permute-done.15.refs_7_.refs_3_, ...), kind=kOutput, calls=%fused_computation | convolution fusion | flops 2368077824 | bytes 13172736 | tf_op jit(solution)/shard_map/dot_general | solution.py:22
  67.3 5.0 %all-to-all-start.1 = ((bf16[8,80,7168]{2,1,0:T(8,128)(2,1)}), bf16[8,80,7168]{2,1,0:T(8,128)(2,1)}, u32[]{:S(2)}, u32[]{:S(2)}) async-start(bf16[8,80,7168]{2,1,0:T(8,128)(2,1)} %bitcast.71), calls=%async_computation.1 | async-start | bytes 18350080 | tf_op jit(solution)/shard_map/all_to_all | solution.py:79
  72.4 24.8 %collective-permute-done.refs_2_ = bf16[80,7168]{1,0:T(8,128)(2,1)} collective-permute-done((bf16[80,7168]{1,0:T(8,128)(2,1)}, bf16[80,7168]{1,0:T(8,128)(2,1)}, u32[]{:S(2)}, u32[]{:S(2)}) %collective-permute-start) | collective-permute-done | bytes 1146912 | tf_op jit(solution)/shard_map/ppermute | solution.py:67
  97.1 21.0 %collective-permute-done.3.refs_5_ = bf16[80,7168]{1,0:T(8,128)(2,1)} collective-permute-done((bf16[80,7168]{1,0:T(8,128)(2,1)}, bf16[80,7168]{1,0:T(8,128)(2,1)}, u32[]{:S(2)}, u32[]{:S(2)}) %collective-permute-start.3) | collective-permute-done | bytes 1146912 | tf_op jit(solution)/shard_map/ppermute | solution.py:67
  121.7 9.1 %shard_map.191.refs_0_.refs_7_ = bf16[480,256]{1,0:T(8,128)(2,1)S(1)} custom-call(s32[2]{0:T(128)S(1)} %pad_add_fusion.y_ref.here_ref, bf16[1,2,7168,256]{3,2,1,0:T(8,128)(2,1)} %gate_ref.5, bf16[1,2,7168,256]{3,2,1,0:T(8,128)(2,1)} %up_ref.5, bf16[80,7168]{1,0:T(8,128)(2,1)} %get-tuple-element.36.refs_0_.refs_5_, ...), custom_call_target="tpu_custom_call" | custom-call | flops 209715200000 | bytes 419430400 | tf_op jit(solution)/shard_map/pallas_call | solution.py:174
  131.5 14.8 %collective-permute-done.4.refs_0_.refs_5_ = bf16[80,7168]{1,0:T(8,128)(2,1)} collective-permute-done((bf16[80,7168]{1,0:T(8,128)(2,1)}, bf16[80,7168]{1,0:T(8,128)(2,1)}, u32[]{:S(2)}, u32[]{:S(2)}) %collective-permute-start.4) | collective-permute-done | bytes 1146912 | tf_op jit(solution)/shard_map/ppermute | solution.py:67
  149.7 7.2 %shard_map.192.refs_1_ = bf16[160,256]{1,0:T(8,128)(2,1)S(1)} custom-call(s32[2]{0:T(128)S(1)} %pad_add_fusion.y_ref.here_ref, bf16[1,2,7168,256]{3,2,1,0:T(8,128)(2,1)} %gate_ref.5, bf16[1,2,7168,256]{3,2,1,0:T(8,128)(2,1)} %up_ref.5, bf16[80,7168]{1,0:T(8,128)(2,1)} %collective-permute-done.4.refs_0_.refs_5_, ...), custom_call_target="tpu_custom_call" | custom-call | flops 209715200000 | bytes 419430400 | tf_op jit(solution)/shard_map/pallas_call | solution.py:174
  160.6 14.5 %collective-permute-done.8.refs_3_.refs_5_ = bf16[640,256]{1,0:T(8,128)(2,1)S(1)} collective-permute-done((bf16[640,256]{1,0:T(8,128)(2,1)S(1)}, bf16[640,256]{1,0:T(8,128)(2,1)S(1)}, u32[]{:S(2)}, u32[]{:S(2)}) %collective-permute-start.8) | collective-permute-done | bytes 327712 | tf_op jit(solution)/shard_map/ppermute | solution.py:67
  176.7 6.0 %collective-permute-done.6.refs_1_.refs_3_ = bf16[640,256]{1,0:T(8,128)(2,1)S(1)} collective-permute-done((bf16[640,256]{1,0:T(8,128)(2,1)S(1)}, bf16[640,256]{1,0:T(8,128)(2,1)S(1)}, u32[]{:S(2)}, u32[]{:S(2)}) %collective-permute-start.6) | collective-permute-done | bytes 327712 | tf_op jit(solution)/shard_map/ppermute | solution.py:67
  191.3 6.3 %shard_map.197.refs_1_ = bf16[640,1792]{1,0:T(8,128)(2,1)} custom-call(s32[2]{0:T(128)S(1)} %pad_add_fusion.y_ref.here_ref, bf16[640,256]{1,0:T(8,128)(2,1)S(1)} %shard_map.193.refs_0_, bf16[640,256]{1,0:T(8,128)(2,1)S(1)} %copy-done.12, bf16[640,256]{1,0:T(8,128)(2,1)S(1)} %copy-done.10, bf16[640,256]{1,0:T(8,128)(2,1)S(1)} %copy-done.8, ...), custom_call_target="tpu_custom_call" | custom-call | tf_op jit(solution)/shard_map/pallas_call | solution.py:230
  198.3 5.4 %all-to-all-start.2 = ((bf16[8,80,1792]{2,1,0:T(8,128)(2,1)}), bf16[8,80,1792]{2,1,0:T(8,128)(2,1)}, u32[]{:S(2)}, u32[]{:S(2)}) async-start(bf16[8,80,1792]{2,1,0:T(8,128)(2,1)} %bitcast.27), calls=%async_computation.2 | async-start | bytes 4587520 | tf_op jit(solution)/shard_map/all_to_all | solution.py:79
  203.7 10.8 %shard_map.200.refs_0_ = bf16[640,256]{1,0:T(8,128)(2,1)S(1)} custom-call(s32[2]{0:T(128)S(1)} %copy-done.21, bf16[1,2,7168,256]{3,2,1,0:T(8,128)(2,1)} %gate_ref.5, bf16[1,2,7168,256]{3,2,1,0:T(8,128)(2,1)} %up_ref.5, bf16[640,7168]{1,0:T(8,128)(2,1)} %bitcast.25.refs_0_), custom_call_target="tpu_custom_call" | custom-call | flops 209715200000 | bytes 419430400 | tf_op jit(solution)/shard_map/pallas_call | solution.py:174
  216.8 7.5 %collective-permute-done.22.refs_6_ = bf16[256,1792]{1,0:T(8,128)(2,1)} collective-permute-done((bf16[256,1792]{1,0:T(8,128)(2,1)}, bf16[256,1792]{1,0:T(8,128)(2,1)}, u32[]{:S(2)}, u32[]{:S(2)}) %collective-permute-start.22) | collective-permute-done | bytes 917536 | tf_op jit(solution)/shard_map/ppermute | solution.py:67
  227.1 9.6 %collective-permute-done.20.refs_3_ = bf16[640,256]{1,0:T(8,128)(2,1)S(1)} collective-permute-done((bf16[640,256]{1,0:T(8,128)(2,1)S(1)}, bf16[640,256]{1,0:T(8,128)(2,1)S(1)}, u32[]{:S(2)}, u32[]{:S(2)}) %collective-permute-start.20) | collective-permute-done | bytes 327712 | tf_op jit(solution)/shard_map/ppermute | solution.py:67
  236.7 5.3 %collective-permute-done.18.refs_1_ = bf16[640,256]{1,0:T(8,128)(2,1)S(1)} collective-permute-done((bf16[640,256]{1,0:T(8,128)(2,1)S(1)}, bf16[640,256]{1,0:T(8,128)(2,1)S(1)}, u32[]{:S(2)}, u32[]{:S(2)}) %collective-permute-start.18) | collective-permute-done | bytes 327712 | tf_op jit(solution)/shard_map/ppermute | solution.py:67
  242.1 6.3 %shard_map.202 = bf16[640,1792]{1,0:T(8,128)(2,1)} custom-call(s32[2]{0:T(128)S(1)} %pad_add_fusion.y_ref.here_ref, bf16[640,256]{1,0:T(8,128)(2,1)S(1)} %shard_map.200.refs_0_, bf16[640,256]{1,0:T(8,128)(2,1)S(1)} %collective-permute-done.18.refs_1_, bf16[640,256]{1,0:T(8,128)(2,1)S(1)} %collective-permute-done.19.refs_2_, ...), custom_call_target="tpu_custom_call" | custom-call | tf_op jit(solution)/shard_map/pallas_call | solution.py:230
  248.4 5.4 %all-to-all-start.3 = ((bf16[8,80,1792]{2,1,0:T(8,128)(2,1)}), bf16[8,80,1792]{2,1,0:T(8,128)(2,1)}, u32[]{:S(2)}, u32[]{:S(2)}) async-start(bf16[8,80,1792]{2,1,0:T(8,128)(2,1)} %get-tuple-element.62), calls=%async_computation.3 | async-start | bytes 4587520 | tf_op jit(solution)/shard_map/all_to_all | solution.py:79
  262.1 6.6 %collective-permute-done.24.refs_1_ = bf16[64,1792]{1,0:T(8,128)(2,1)S(1)} collective-permute-done((bf16[64,1792]{1,0:T(8,128)(2,1)S(1)}, bf16[64,1792]{1,0:T(8,128)(2,1)S(1)}, u32[]{:S(2)}, u32[]{:S(2)}) %collective-permute-start.24) | collective-permute-done | bytes 229408 | tf_op jit(solution)/shard_map/ppermute | solution.py:67
  272.8 6.6 %collective-permute-start.27 = (bf16[64,7168]{1,0:T(8,128)(2,1)S(1)}, bf16[64,7168]{1,0:T(8,128)(2,1)S(1)}, u32[]{:S(2)}, u32[]{:S(2)}) collective-permute-start(bf16[64,7168]{1,0:T(8,128)(2,1)S(1)} %shard_map.205.own_ref), channel_id=1, source_target_pairs={{0,32},{32,64},{64,96},{1,33},{33,65},{65,97},{2,34},{34,66},{66,9... | collective-permute-start | bytes 2752520 | tf_op jit(solution)/shard_map/ppermute | solution.py:405
  279.5 7.9 %all-to-all-done.3 = bf16[8,80,1792]{2,1,0:T(8,128)(2,1)} async-done(((bf16[8,80,1792]{2,1,0:T(8,128)(2,1)}), bf16[8,80,1792]{2,1,0:T(8,128)(2,1)}, u32[]{:S(2)}, u32[]{:S(2)}) %all-to-all-start.3) | async-done | bytes 2293792 | tf_op jit(solution)/shard_map/all_to_all | solution.py:79
  287.4 4.6 %shard_map.206 = (bf16[64,1792]{1,0:T(8,128)(2,1)S(1)}, bf16[64,1792]{1,0:T(8,128)(2,1)S(1)}, bf16[64,1792]{1,0:T(8,128)(2,1)S(1)}, bf16[64,1792]{1,0:T(8,128)(2,1)S(1)}) custom-call(s32[2]{0:T(128)S(1)} %pad_add_fusion.y_ref.here_ref, bf16[256,128]{1,0:T(8,128)(2,1)S(1)} %copy-done.18, bf16[256,128]{1,0:T(8,128)(2,1)S(1)} %get-tuple-element.72.high_ref, ...), custom_call_target="tpu_custom_call" | custom-call | tf_op jit(solution)/shard_map/pallas_call | solution.py:266
  309.2 5.3 %collective-permute-done.29.refs_1_ = bf16[64,1792]{1,0:T(8,128)(2,1)S(1)} collective-permute-done((bf16[64,1792]{1,0:T(8,128)(2,1)S(1)}, bf16[64,1792]{1,0:T(8,128)(2,1)S(1)}, u32[]{:S(2)}, u32[]{:S(2)}) %collective-permute-start.29) | collective-permute-done | bytes 229408 | tf_op jit(solution)/shard_map/ppermute | solution.py:298
  (171 shorter events, 104.3 us)
Async XLA Ops:
  1.5 29.0 %collective-permute-start.14 = (bf16[64,128]{0,1:T(8,128)(2,1)S(1)}, bf16[64,128]{0,1:T(8,128)(2,1)S(1)}, u32[]{:S(2)}, u32[]{:S(2)}) collective-permute-start(bf16[64,128]{0,1:T(8,128)(2,1)S(1)} %concatenate.34), channel_id=1, source_target_pairs={{0,3},{1,0},{2,1},{3,2},{4,7},{5,4},{6,5},{7,6},{8,11},{9,8},{10,9... | collective-permute-start | bytes 49160 | tf_op jit(solution)/shard_map/ppermute | solution.py:67
  5.1 25.4 %collective-permute-start.13 = (bf16[64,128]{0,1:T(8,128)(2,1)S(1)}, bf16[64,128]{0,1:T(8,128)(2,1)}, u32[]{:S(2)}, u32[]{:S(2)}) collective-permute-start(bf16[64,128]{0,1:T(8,128)(2,1)S(1)} %concatenate.34), channel_id=1, source_target_pairs={{0,2},{1,3},{2,0},{3,1},{4,6},{5,7},{6,4},{7,5},{8,10},{9,11},{10,... | collective-permute-start | bytes 49160 | tf_op jit(solution)/shard_map/ppermute | solution.py:67
  5.5 27.0 %collective-permute-start.12 = (bf16[64,128]{0,1:T(8,128)(2,1)S(1)}, bf16[64,128]{0,1:T(8,128)(2,1)}, u32[]{:S(2)}, u32[]{:S(2)}) collective-permute-start(bf16[64,128]{0,1:T(8,128)(2,1)S(1)} %concatenate.34), channel_id=1, source_target_pairs={{0,1},{1,2},{2,3},{3,0},{4,5},{5,6},{6,7},{7,4},{8,9},{9,10},{10,1... | collective-permute-start | bytes 49160 | tf_op jit(solution)/shard_map/ppermute | solution.py:67
  7.8 48.2 %collective-permute-start.17 = (bf16[64,7168]{1,0:T(8,128)(2,1)S(1)}, bf16[64,7168]{1,0:T(8,128)(2,1)}, u32[]{:S(2)}, u32[]{:S(2)}) collective-permute-start(bf16[64,7168]{1,0:T(8,128)(2,1)S(1)} %get-tuple-element.67.refs_0_), channel_id=1, source_target_pairs={{0,3},{1,0},{2,1},{3,2},{4,7},{5,4},{6,5},{7,6},{8,11},{9,8},{10,9... | collective-permute-start | bytes 2752520 | tf_op jit(solution)/shard_map/ppermute | solution.py:67
  9.8 46.6 %collective-permute-start.16 = (bf16[64,7168]{1,0:T(8,128)(2,1)S(1)}, bf16[64,7168]{1,0:T(8,128)(2,1)}, u32[]{:S(2)}, u32[]{:S(2)}) collective-permute-start(bf16[64,7168]{1,0:T(8,128)(2,1)S(1)} %get-tuple-element.67.refs_0_), channel_id=1, source_target_pairs={{0,2},{1,3},{2,0},{3,1},{4,6},{5,7},{6,4},{7,5},{8,10},{9,11},{10,... | collective-permute-start | bytes 2752520 | tf_op jit(solution)/shard_map/ppermute | solution.py:67
  14.8 37.0 %all-to-all-start = ((bf16[8,40,3584]{2,1,0:T(8,128)(2,1)}), bf16[8,40,3584]{2,1,0:T(8,128)(2,1)S(1)}, u32[]{:S(2)}, u32[]{:S(2)}) async-start(bf16[8,40,3584]{2,1,0:T(8,128)(2,1)} %bitcast.72), calls=%async_computation | async-start | bytes 4587520 | tf_op jit(solution)/shard_map/all_to_all | solution.py:79
  30.5 28.2 %collective-permute-start.15 = (bf16[64,7168]{1,0:T(8,128)(2,1)S(1)}, bf16[64,7168]{1,0:T(8,128)(2,1)}, u32[]{:S(2)}, u32[]{:S(2)}) collective-permute-start(bf16[64,7168]{1,0:T(8,128)(2,1)S(1)} %get-tuple-element.67.refs_0_), channel_id=1, source_target_pairs={{0,1},{1,2},{2,3},{3,0},{4,5},{5,6},{6,7},{7,4},{8,9},{9,10},{10,1... | collective-permute-start | bytes 2752520 | tf_op jit(solution)/shard_map/ppermute | solution.py:67
  30.6 100.9 %collective-permute-start.9 = (bf16[256,1792]{1,0:T(8,128)(2,1)}, bf16[256,1792]{1,0:T(8,128)(2,1)}, u32[]{:S(2)}, u32[]{:S(2)}) collective-permute-start(bf16[256,1792]{1,0:T(8,128)(2,1)} %get-tuple-element.43), channel_id=1, source_target_pairs={{0,2},{1,3},{2,0},{3,1},{4,6},{5,7},{6,4},{7,5},{8,10},{9,11},{10,... | collective-permute-start | bytes 2752520 | tf_op jit(solution)/shard_map/ppermute | solution.py:67
  54.9 66.6 %collective-permute-start.2 = (bf16[80,7168]{1,0:T(8,128)(2,1)}, bf16[80,7168]{1,0:T(8,128)(2,1)S(1)}, u32[]{:S(2)}, u32[]{:S(2)}) collective-permute-start(bf16[80,7168]{1,0:T(8,128)(2,1)} %get-tuple-element.36.refs_0_.refs_5_), channel_id=1, source_target_pairs={{0,3},{1,0},{2,1},{3,2},{4,7},{5,4},{6,5},{7,6},{8,11},{9,8},{10,9... | collective-permute-start | bytes 3440648 | tf_op jit(solution)/shard_map/ppermute | solution.py:67
  56.0 41.1 %collective-permute-start = (bf16[80,7168]{1,0:T(8,128)(2,1)}, bf16[80,7168]{1,0:T(8,128)(2,1)}, u32[]{:S(2)}, u32[]{:S(2)}) collective-permute-start(bf16[80,7168]{1,0:T(8,128)(2,1)} %get-tuple-element.36.refs_0_.refs_5_), channel_id=1, source_target_pairs={{0,1},{1,2},{2,3},{3,0},{4,5},{5,6},{6,7},{7,4},{8,9},{9,10},{10,1... | collective-permute-start | bytes 3440648 | tf_op jit(solution)/shard_map/ppermute | solution.py:67
  56.4 61.7 %collective-permute-start.3 = (bf16[80,7168]{1,0:T(8,128)(2,1)}, bf16[80,7168]{1,0:T(8,128)(2,1)}, u32[]{:S(2)}, u32[]{:S(2)}) collective-permute-start(bf16[80,7168]{1,0:T(8,128)(2,1)} %get-tuple-element.37.refs_1_.refs_6_), channel_id=1, source_target_pairs={{0,3},{1,0},{2,1},{3,2},{4,7},{5,4},{6,5},{7,6},{8,11},{9,8},{10,9... | collective-permute-start | bytes 3440648 | tf_op jit(solution)/shard_map/ppermute | solution.py:67
  58.7 63.0 %collective-permute-start.1 = (bf16[80,7168]{1,0:T(8,128)(2,1)}, bf16[80,7168]{1,0:T(8,128)(2,1)S(1)}, u32[]{:S(2)}, u32[]{:S(2)}) collective-permute-start(bf16[80,7168]{1,0:T(8,128)(2,1)} %get-tuple-element.37.refs_1_.refs_6_), channel_id=1, source_target_pairs={{0,1},{1,2},{2,3},{3,0},{4,5},{5,6},{6,7},{7,4},{8,9},{9,10},{10,1... | collective-permute-start | bytes 3440648 | tf_op jit(solution)/shard_map/ppermute | solution.py:67
  67.3 130.9 %all-to-all-start.1 = ((bf16[8,80,7168]{2,1,0:T(8,128)(2,1)}), bf16[8,80,7168]{2,1,0:T(8,128)(2,1)}, u32[]{:S(2)}, u32[]{:S(2)}) async-start(bf16[8,80,7168]{2,1,0:T(8,128)(2,1)} %bitcast.71), calls=%async_computation.1 | async-start | bytes 18350080 | tf_op jit(solution)/shard_map/all_to_all | solution.py:79
  97.1 49.2 %collective-permute-start.4 = (bf16[80,7168]{1,0:T(8,128)(2,1)}, bf16[80,7168]{1,0:T(8,128)(2,1)}, u32[]{:S(2)}, u32[]{:S(2)}) collective-permute-start(bf16[80,7168]{1,0:T(8,128)(2,1)} %collective-permute-done.refs_2_), channel_id=1, source_target_pairs={{0,1},{1,2},{2,3},{3,0},{4,5},{5,6},{6,7},{7,4},{8,9},{9,10},{10,1... | collective-permute-start | bytes 3440648 | tf_op jit(solution)/shard_map/ppermute | solution.py:67
  118.1 28.2 %collective-permute-start.5 = (bf16[80,7168]{1,0:T(8,128)(2,1)}, bf16[80,7168]{1,0:T(8,128)(2,1)}, u32[]{:S(2)}, u32[]{:S(2)}) collective-permute-start(bf16[80,7168]{1,0:T(8,128)(2,1)} %collective-permute-done.3.refs_5_), channel_id=1, source_target_pairs={{0,3},{1,0},{2,1},{3,2},{4,7},{5,4},{6,5},{7,6},{8,11},{9,8},{10,9... | collective-permute-start | bytes 3440648 | tf_op jit(solution)/shard_map/ppermute | solution.py:67
  147.0 35.6 %collective-permute-start.10 = (bf16[256,1792]{1,0:T(8,128)(2,1)}, bf16[256,1792]{1,0:T(8,128)(2,1)}, u32[]{:S(2)}, u32[]{:S(2)}) collective-permute-start(bf16[256,1792]{1,0:T(8,128)(2,1)} %get-tuple-element.44), channel_id=1, source_target_pairs={{0,1},{1,2},{2,3},{3,0},{4,5},{5,6},{6,7},{7,4},{8,9},{9,10},{10,1... | collective-permute-start | bytes 2752520 | tf_op jit(solution)/shard_map/ppermute | solution.py:67
  147.6 35.0 %collective-permute-start.11 = (bf16[256,1792]{1,0:T(8,128)(2,1)}, bf16[256,1792]{1,0:T(8,128)(2,1)}, u32[]{:S(2)}, u32[]{:S(2)}) collective-permute-start(bf16[256,1792]{1,0:T(8,128)(2,1)} %get-tuple-element.45), channel_id=1, source_target_pairs={{0,3},{1,0},{2,1},{3,2},{4,7},{5,4},{6,5},{7,6},{8,11},{9,8},{10,9... | collective-permute-start | bytes 2752520 | tf_op jit(solution)/shard_map/ppermute | solution.py:67
  184.1 32.8 %collective-permute-start.21 = (bf16[256,1792]{1,0:T(8,128)(2,1)}, bf16[256,1792]{1,0:T(8,128)(2,1)}, u32[]{:S(2)}, u32[]{:S(2)}) collective-permute-start(bf16[256,1792]{1,0:T(8,128)(2,1)} %get-tuple-element.50), channel_id=1, source_target_pairs={{0,1},{1,2},{2,3},{3,0},{4,5},{5,6},{6,7},{7,4},{8,9},{9,10},{10,1... | collective-permute-start | bytes 2752520 | tf_op jit(solution)/shard_map/ppermute | solution.py:67
  185.9 38.5 %collective-permute-start.22 = (bf16[256,1792]{1,0:T(8,128)(2,1)}, bf16[256,1792]{1,0:T(8,128)(2,1)}, u32[]{:S(2)}, u32[]{:S(2)}) collective-permute-start(bf16[256,1792]{1,0:T(8,128)(2,1)} %get-tuple-element.51), channel_id=1, source_target_pairs={{0,2},{1,3},{2,0},{3,1},{4,6},{5,7},{6,4},{7,5},{8,10},{9,11},{10,... | collective-permute-start | bytes 2752520 | tf_op jit(solution)/shard_map/ppermute | solution.py:67
  187.3 39.7 %collective-permute-start.23 = (bf16[256,1792]{1,0:T(8,128)(2,1)}, bf16[256,1792]{1,0:T(8,128)(2,1)}, u32[]{:S(2)}, u32[]{:S(2)}) collective-permute-start(bf16[256,1792]{1,0:T(8,128)(2,1)} %get-tuple-element.52), channel_id=1, source_target_pairs={{0,3},{1,0},{2,1},{3,2},{4,7},{5,4},{6,5},{7,6},{8,11},{9,8},{10,9... | collective-permute-start | bytes 2752520 | tf_op jit(solution)/shard_map/ppermute | solution.py:67
  198.3 50.1 %all-to-all-start.2 = ((bf16[8,80,1792]{2,1,0:T(8,128)(2,1)}), bf16[8,80,1792]{2,1,0:T(8,128)(2,1)}, u32[]{:S(2)}, u32[]{:S(2)}) async-start(bf16[8,80,1792]{2,1,0:T(8,128)(2,1)} %bitcast.27), calls=%async_computation.2 | async-start | bytes 4587520 | tf_op jit(solution)/shard_map/all_to_all | solution.py:79
  216.8 25.2 %collective-permute-start.18 = (bf16[640,256]{1,0:T(8,128)(2,1)S(1)}, bf16[640,256]{1,0:T(8,128)(2,1)S(1)}, u32[]{:S(2)}, u32[]{:S(2)}) collective-permute-start(bf16[640,256]{1,0:T(8,128)(2,1)S(1)} %shard_map.200.refs_0_), channel_id=1, source_target_pairs={{0,1},{1,2},{2,3},{3,0},{4,5},{5,6},{6,7},{7,4},{8,9},{9,10},{10,1... | collective-permute-start | bytes 983048 | tf_op jit(solution)/shard_map/ppermute | solution.py:67
  248.4 39.0 %all-to-all-start.3 = ((bf16[8,80,1792]{2,1,0:T(8,128)(2,1)}), bf16[8,80,1792]{2,1,0:T(8,128)(2,1)}, u32[]{:S(2)}, u32[]{:S(2)}) async-start(bf16[8,80,1792]{2,1,0:T(8,128)(2,1)} %get-tuple-element.62), calls=%async_computation.3 | async-start | bytes 4587520 | tf_op jit(solution)/shard_map/all_to_all | solution.py:79
  272.8 27.9 %collective-permute-start.27 = (bf16[64,7168]{1,0:T(8,128)(2,1)S(1)}, bf16[64,7168]{1,0:T(8,128)(2,1)S(1)}, u32[]{:S(2)}, u32[]{:S(2)}) collective-permute-start(bf16[64,7168]{1,0:T(8,128)(2,1)S(1)} %shard_map.205.own_ref), channel_id=1, source_target_pairs={{0,32},{32,64},{64,96},{1,33},{33,65},{65,97},{2,34},{34,66},{66,9... | collective-permute-start | bytes 2752520 | tf_op jit(solution)/shard_map/ppermute | solution.py:405
  (47 other events, 468.8 us)

commit v7 on v6

--- a/solution.py
+++ b/solution.py
@@ -123,7 +123,11 @@
     )(y, pick, value)
 
 
-def quarters(y, down, section, runs):
+def section_of(here, role):
+    return lax.rem(here[1] + 1 - role, 2)
+
+
+def quarters(y, down, role, runs):
     depth, part = down.shape[2], down.shape[3] // GROUP // runs
     count = (GROUP - 1) * runs
 
@@ -135,7 +139,7 @@
                 refs[i][...] = down_ref[0, 0]
 
     def column(i, y):
-        return (0, section, 0, lax.rem(y[0] + i // runs + 1, GROUP) * runs + lax.rem(i, runs))
+        return (0, section_of(y, role), 0, lax.rem(y[0] + i // runs + 1, GROUP) * runs + lax.rem(i, runs))
 
     cuts = call(
         kernel,
@@ -147,7 +151,7 @@
     return [cuts[run::runs] for run in range(runs)]
 
 
-def hidden_of(y, rows, gate, up, section):
+def hidden_of(y, rows, gate, up, role):
     width, block = gate.shape[2:]
     total = sum(run.shape[0] for run in rows)
     tile = 1024
@@ -170,7 +174,7 @@
         def _():
             out_ref[...] = (jax.nn.silu(gate_sum[...]) * up_sum[...]).astype(BF)
 
-    weights = pl.BlockSpec((1, 1, tile, block), lambda j, y: (0, section, j, 0))
+    weights = pl.BlockSpec((1, 1, tile, block), lambda j, y: (0, section_of(y, role), j, 0))
     return call(
         kernel,
         shape(total, block),
@@ -200,7 +204,7 @@
     )(y, target, *pieces)
 
 
-def project(y, units, parts, down, section, moved):
+def project(y, units, parts, down, role, moved):
     rows, depth = units[0].shape
     part = sum(group[0].shape[1] for group in parts)
     tile = part // 2
@@ -225,7 +229,7 @@
                 matrix = jnp.concatenate([own[0, 0], *(ref[...] for ref in mine)], axis=0)
                 out_ref[...] = dot(joined[...], matrix).astype(BF)
 
-    own = pl.BlockSpec((1, 1, depth, tile), lambda j, y: (0, section, 0, y[0] * 2 + j))
+    own = pl.BlockSpec((1, 1, depth, tile), lambda j, y: (0, section_of(y, role), 0, y[0] * 2 + j))
     others = [columns_of(depth, tile) if runs == 1 else whole(value) for value in flat]
     out = call(
         kernel,
@@ -304,18 +308,20 @@
     ]
 
 
-def settle(here, last, ahead, own, behind, kept):
-    tokens, part = kept[0].shape
+def settle(here, last, ahead, own, late):
+    tokens, part = late[0].shape
 
     def kernel(here_ref, ahead_ref, own_ref, *refs):
         *refs, out_ref = refs
+        rank = here_ref[1]
+        odd, edge = lax.rem(rank, 2) == 1, jnp.logical_or(rank == 0, rank == last)
         for k in range(GROUP):
 
             @pl.when(pl.program_id(0) == k)
             def _():
-                first, final = here_ref[1] == 0, here_ref[1] == last
-                out_ref[0] = jnp.where(first, refs[GROUP + k][...], ahead_ref[...])
-                out_ref[1] = jnp.where(final, own_ref[...], refs[k][...])
+                early, piece = jnp.where(edge, own_ref[...], ahead_ref[...]), refs[k][...]
+                out_ref[0] = jnp.where(odd, piece, early)
+                out_ref[1] = jnp.where(odd, early, piece)
 
     def column(k, here):
         return lax.rem(here[0] + GROUP - k, GROUP)
@@ -325,9 +331,9 @@
         kernel,
         shape(2, *own.shape),
         (GROUP,),
-        [quarter] * 2 + [whole(piece) for piece in (*behind, *kept)],
+        [quarter] * 2 + [whole(piece) for piece in late],
         pl.BlockSpec((2, tokens, part), lambda k, here: (0, 0, column(k, here))),
-    )(here, ahead, own, *behind, *kept)
+    )(here, ahead, own, *late)
 
 
 def local(activations, expert_ids, gate_values, gate_weight, up_weight, down_weight):
@@ -335,17 +341,23 @@
     top = expert_ids.shape[3]
     half = width // 2
     index = lax.axis_index("y").astype(jnp.int32)
-    y = jnp.stack([index, lax.axis_index("pipe").astype(jnp.int32)])
-    last = lax.axis_size("pipe") - 1
-    first_rows, second_rows = activations[0, 0], activations[0, 1]
+    rank = lax.axis_index("pipe").astype(jnp.int32)
+    y = jnp.stack([index, rank])
+    odd = jnp.bitwise_and(rank, 1) == 1
+
+    def roles(value):
+        return jnp.where(odd, value[0, 0], value[0, 1]), jnp.where(odd, value[0, 1], value[0, 0])
+
+    first_rows, second_rows = roles(activations)
+    ids, gates = roles(expert_ids), roles(gate_values)
 
     before = np.asarray(np.tril(np.ones((tokens, tokens)), -1), dtype=BF)
-    key, _ = keys(expert_ids[0, 0], before, 0.0)
+    key, _ = keys(ids[0], before, 0.0)
     key = jnp.concatenate([key, jnp.where(key < 0, key, key + STRIDE)], axis=0)
     choose = (dot_t(expert_rows(2 * CAP), key) == codes(range(2))[:, None]).astype(BF)
     halves = jnp.concatenate([first_rows[:, :half], first_rows[:, half:]], axis=0)
     outgoing = dot(choose, halves).astype(BF).reshape(EXPERTS, 2 * CAP, half)
-    routing = [packed(expert_ids[0, s], gate_values[0, s]) for s in range(2)]
+    routing = [packed(ids[s], gates[s]) for s in range(2)]
     routing = jnp.concatenate([*routing, jnp.zeros((tokens, LANES - 8 * top), BF)], axis=1)
     arrived = exchange(outgoing)
 
@@ -361,10 +373,10 @@
     before = np.asarray(np.kron(np.eye(GROUP), np.tril(np.ones((tokens, tokens)), -1)), dtype=BF)
     key, weight = [], []
     for s in range(2):
-        ids, gates = unpacked(routing[:, 4 * top * s : 4 * top * (s + 1)])
-        found, named = keys(ids, before, (owner * STRIDE).astype(F32))
+        their_ids, their_gates = unpacked(routing[:, 4 * top * s : 4 * top * (s + 1)])
+        found, named = keys(their_ids, before, (owner * STRIDE).astype(F32))
         key.append(found)
-        weight.append(sum(jnp.where(named[k], gates[:, k : k + 1], 0.0) for k in range(top)))
+        weight.append(sum(jnp.where(named[k], their_gates[:, k : k + 1], 0.0) for k in range(top)))
     onehot = expert_rows(GROUP * CAP)
     choose = (dot_t(onehot, key[1]) == codes(range(GROUP))[:, None]).astype(BF)
     turned = [slice(k * tokens, (k + 1) * tokens) for k in (0, 3, 2, 1)]
@@ -378,7 +390,6 @@
     weights = (gate_weight, up_weight)
     far = [shift(ahead[0], 1), shift(back[1], -1)]
     both = hidden_of(y, [*arrived, *ahead, *back], *weights, 0)
-    up_one, down_one = [(p, p + 1) for p in range(last)], [(p + 1, p) for p in range(last)]
     opposite = shift(cuts0[1], 2)
     cut1, cut3, *cuts1 = tie([cuts0[0], cuts0[2], *cuts1], [*far, both, opposite])
 
@@ -402,12 +413,11 @@
     out, key0 = tie([out, key0], [])
     back1 = exchange(out)
     result0 = home(y, combine(y, back0, key0, weight0), first_rows)
-    ahead = lax.ppermute(result0, "pipe", up_one)
+    size = lax.axis_size("pipe")
+    ahead = lax.ppermute(result0, "pipe", [(p, p + 1) for p in range(1, size - 1, 2)] + [(p + 1, p) for p in range(1, size - 1, 2)])
     turned = [second_rows, near[2], near[1], near[0]]
-    sums1 = combine(y, back1, key1, weight1, turned)
-    behind = send(sums1, down_one, GROUP)
-    kept = [sums1[0], *send(sums1, [(0, 0)], GROUP)[1:]]
-    return settle(y, last, ahead, result0, behind, kept)[None]
+    late = send(combine(y, back1, key1, weight1, turned), [(p, p ^ 1) for p in range(size)], GROUP)
+    return settle(y, size - 1, ahead, result0, late)[None]
 
 
 def solution(mesh):

time: 322 us -> 312 us (0.969)
  starting transfers between devices: 77.3 us -> 65.6 us
    ppermute x7 -> x4, starting transfers between devices: 17.1 us -> 5.43 us  [send(): lax.ppermute(pieces[k], ('pipe', 'y'), [(p * GROUP + i, q * GROUP + (i +...]
    ppermute x7 -> x4, waiting for transfers between devices: 8.74 us -> 10.6 us  [send(): lax.ppermute(pieces[k], ('pipe', 'y'), [(p * GROUP + i, q * GROUP + (i +...]
  transfers between devices with their start and end apart: 39 -> 36, of which waited for: 17 -> 17; matrix products, arithmetic and copies ran while one was open for 6% -> 6% of each run, Pallas kernels for 20% -> 21%
where the time goes in v7:
time: 312 us; the launch traced here: 311 us
  waiting for transfers between devices  148 us (47%)
  Pallas kernels  66.9 us (21%)
  starting transfers between devices  65.6 us (21%)
  matrix products  12.1 us (4%)
  local copies, waits for them, and re-layouts  8.92 us (3%)
  other arithmetic  8.63 us (3%)
    ppermute x27, waiting for transfers between devices, shift(): lax.ppermute(value, 'y', [(i, (i + steps) % GROUP) for i in range(GROUP)])  117 us
    ppermute x27, starting transfers between devices, shift(): lax.ppermute(value, 'y', [(i, (i + steps) % GROUP) for i in range(GROUP)])  32.2 us
    pallas_call x3, Pallas kernels, hidden_of(): call(kernel, shape(total, block), (steps,), [weights, weights] + [columns...  27.3 us
    all_to_all x4, starting transfers between devices, exchange(): lax.all_to_all(value, ('x', 'z'), split_axis=0, concat_axis=0, tiled=True)  21.3 us
    all_to_all x4, waiting for transfers between devices, exchange(): lax.all_to_all(value, ('x', 'z'), split_axis=0, concat_axis=0, tiled=True)  20 us
    pallas_call x2, Pallas kernels, project(): call(kernel, shape(rows, part), (2,), [whole(unit) for unit in units] + [...  12.7 us
    dot_general x5, matrix products, dot(): return jnp.dot(a, b, preferred_element_type=F32)  11.1 us
    ppermute x4, waiting for transfers between devices, send(): lax.ppermute(pieces[k], ('pipe', 'y'), [(p * GROUP + i, q * GROUP + (i +...  10.6 us
  transfers between devices with their start and end apart: 36, of which 17 were waited for; matrix products, arithmetic and copies ran while one was open for 6% of the time, Pallas kernels for 21%

profile of v7, /device:TPU:1, one launch (start us, length us, event | category | flops | bytes accessed | tf_op | source)
XLA Modules:
  0.0 310.7 jit_solution(7824909802707819515)
XLA Ops:
  14.9 5.5 %all-to-all-start = ((bf16[8,40,3584]{2,1,0:T(8,128)(2,1)}), bf16[8,40,3584]{2,1,0:T(8,128)(2,1)S(1)}, u32[]{:S(2)}, u32[]{:S(2)}) async-start(bf16[8,40,3584]{2,1,0:T(8,128)(2,1)} %bitcast.71), calls=%async_computation | async-start | bytes 4587520 | tf_op jit(solution)/shard_map/all_to_all | solution.py:79
  39.8 12.1 %all-to-all-done = bf16[8,40,3584]{2,1,0:T(8,128)(2,1)S(1)} async-done(((bf16[8,40,3584]{2,1,0:T(8,128)(2,1)}), bf16[8,40,3584]{2,1,0:T(8,128)(2,1)S(1)}, u32[]{:S(2)}, u32[]{:S(2)}) %all-to-all-start) | async-done | bytes 2293792 | tf_op jit(solution)/shard_map/all_to_all | solution.py:79
  59.5 7.9 %convolution_convert_fusion = bf16[640,7168]{1,0:T(8,128)(2,1)} fusion(bf16[640,256]{1,0:T(8,128)(2,1)} %get-tuple-element.46, bf16[64,7168]{1,0:T(8,128)(2,1)} %collective-permute-done.17.refs_9_.refs_1_, bf16[64,7168]{1,0:T(8,128)(2,1)} %collective-permute-done.16.refs_8_.refs_2_, bf16[64,7168]{1,0:T(8,128)(2,1)} %collective-permute-done.15.refs_7_.refs_3_, ...), kind=kOutput, calls=%fused_computation | convolution fusion | flops 2368077824 | bytes 13172736 | tf_op jit(solution)/shard_map/dot_general | solution.py:22
  67.4 5.0 %all-to-all-start.1 = ((bf16[8,80,7168]{2,1,0:T(8,128)(2,1)}), bf16[8,80,7168]{2,1,0:T(8,128)(2,1)}, u32[]{:S(2)}, u32[]{:S(2)}) async-start(bf16[8,80,7168]{2,1,0:T(8,128)(2,1)} %bitcast.70), calls=%async_computation.1 | async-start | bytes 18350080 | tf_op jit(solution)/shard_map/all_to_all | solution.py:79
  72.4 24.8 %collective-permute-done.refs_2_ = bf16[80,7168]{1,0:T(8,128)(2,1)} collective-permute-done((bf16[80,7168]{1,0:T(8,128)(2,1)}, bf16[80,7168]{1,0:T(8,128)(2,1)}, u32[]{:S(2)}, u32[]{:S(2)}) %collective-permute-start) | collective-permute-done | bytes 1146912 | tf_op jit(solution)/shard_map/ppermute | solution.py:67
  97.2 20.9 %collective-permute-done.3.refs_5_ = bf16[80,7168]{1,0:T(8,128)(2,1)} collective-permute-done((bf16[80,7168]{1,0:T(8,128)(2,1)}, bf16[80,7168]{1,0:T(8,128)(2,1)}, u32[]{:S(2)}, u32[]{:S(2)}) %collective-permute-start.3) | collective-permute-done | bytes 1146912 | tf_op jit(solution)/shard_map/ppermute | solution.py:67
  121.8 9.2 %shard_map.191.refs_0_.refs_7_ = bf16[480,256]{1,0:T(8,128)(2,1)S(1)} custom-call(s32[2]{0:T(128)S(1)} %pad_add_fusion.y_ref.here_ref, bf16[1,2,7168,256]{3,2,1,0:T(8,128)(2,1)} %gate_ref.5, bf16[1,2,7168,256]{3,2,1,0:T(8,128)(2,1)} %up_ref.5, bf16[80,7168]{1,0:T(8,128)(2,1)} %get-tuple-element.36.refs_0_.refs_5_, ...), custom_call_target="tpu_custom_call" | custom-call | flops 209715200000 | bytes 419430400 | tf_op jit(solution)/shard_map/pallas_call | solution.py:178
  131.7 14.7 %collective-permute-done.4.refs_0_.refs_5_ = bf16[80,7168]{1,0:T(8,128)(2,1)} collective-permute-done((bf16[80,7168]{1,0:T(8,128)(2,1)}, bf16[80,7168]{1,0:T(8,128)(2,1)}, u32[]{:S(2)}, u32[]{:S(2)}) %collective-permute-start.4) | collective-permute-done | bytes 1146912 | tf_op jit(solution)/shard_map/ppermute | solution.py:67
  149.7 7.3 %shard_map.192.refs_1_ = bf16[160,256]{1,0:T(8,128)(2,1)S(1)} custom-call(s32[2]{0:T(128)S(1)} %pad_add_fusion.y_ref.here_ref, bf16[1,2,7168,256]{3,2,1,0:T(8,128)(2,1)} %gate_ref.5, bf16[1,2,7168,256]{3,2,1,0:T(8,128)(2,1)} %up_ref.5, bf16[80,7168]{1,0:T(8,128)(2,1)} %collective-permute-done.4.refs_0_.refs_5_, ...), custom_call_target="tpu_custom_call" | custom-call | flops 209715200000 | bytes 419430400 | tf_op jit(solution)/shard_map/pallas_call | solution.py:178
  160.7 14.5 %collective-permute-done.8.refs_3_.refs_5_ = bf16[640,256]{1,0:T(8,128)(2,1)S(1)} collective-permute-done((bf16[640,256]{1,0:T(8,128)(2,1)S(1)}, bf16[640,256]{1,0:T(8,128)(2,1)S(1)}, u32[]{:S(2)}, u32[]{:S(2)}) %collective-permute-start.8) | collective-permute-done | bytes 327712 | tf_op jit(solution)/shard_map/ppermute | solution.py:67
  176.7 6.0 %collective-permute-done.6.refs_1_.refs_3_ = bf16[640,256]{1,0:T(8,128)(2,1)S(1)} collective-permute-done((bf16[640,256]{1,0:T(8,128)(2,1)S(1)}, bf16[640,256]{1,0:T(8,128)(2,1)S(1)}, u32[]{:S(2)}, u32[]{:S(2)}) %collective-permute-start.6) | collective-permute-done | bytes 327712 | tf_op jit(solution)/shard_map/ppermute | solution.py:67
  191.3 6.3 %shard_map.197.refs_1_ = bf16[640,1792]{1,0:T(8,128)(2,1)} custom-call(s32[2]{0:T(128)S(1)} %pad_add_fusion.y_ref.here_ref, bf16[640,256]{1,0:T(8,128)(2,1)S(1)} %shard_map.193.refs_0_, bf16[640,256]{1,0:T(8,128)(2,1)S(1)} %copy-done.12, bf16[640,256]{1,0:T(8,128)(2,1)S(1)} %copy-done.10, bf16[640,256]{1,0:T(8,128)(2,1)S(1)} %copy-done.8, ...), custom_call_target="tpu_custom_call" | custom-call | tf_op jit(solution)/shard_map/pallas_call | solution.py:234
  198.3 5.4 %all-to-all-start.2 = ((bf16[8,80,1792]{2,1,0:T(8,128)(2,1)}), bf16[8,80,1792]{2,1,0:T(8,128)(2,1)}, u32[]{:S(2)}, u32[]{:S(2)}) async-start(bf16[8,80,1792]{2,1,0:T(8,128)(2,1)} %bitcast.27), calls=%async_computation.2 | async-start | bytes 4587520 | tf_op jit(solution)/shard_map/all_to_all | solution.py:79
  203.7 10.9 %shard_map.200.refs_0_ = bf16[640,256]{1,0:T(8,128)(2,1)S(1)} custom-call(s32[2]{0:T(128)S(1)} %copy-done.21, bf16[1,2,7168,256]{3,2,1,0:T(8,128)(2,1)} %gate_ref.5, bf16[1,2,7168,256]{3,2,1,0:T(8,128)(2,1)} %up_ref.5, bf16[640,7168]{1,0:T(8,128)(2,1)} %bitcast.25.refs_0_), custom_call_target="tpu_custom_call" | custom-call | flops 209715200000 | bytes 419430400 | tf_op jit(solution)/shard_map/pallas_call | solution.py:178
  216.9 7.4 %collective-permute-done.22.refs_6_ = bf16[256,1792]{1,0:T(8,128)(2,1)} collective-permute-done((bf16[256,1792]{1,0:T(8,128)(2,1)}, bf16[256,1792]{1,0:T(8,128)(2,1)}, u32[]{:S(2)}, u32[]{:S(2)}) %collective-permute-start.22) | collective-permute-done | bytes 917536 | tf_op jit(solution)/shard_map/ppermute | solution.py:67
  227.2 9.6 %collective-permute-done.20.refs_3_ = bf16[640,256]{1,0:T(8,128)(2,1)S(1)} collective-permute-done((bf16[640,256]{1,0:T(8,128)(2,1)S(1)}, bf16[640,256]{1,0:T(8,128)(2,1)S(1)}, u32[]{:S(2)}, u32[]{:S(2)}) %collective-permute-start.20) | collective-permute-done | bytes 327712 | tf_op jit(solution)/shard_map/ppermute | solution.py:67
  236.8 5.3 %collective-permute-done.18.refs_1_ = bf16[640,256]{1,0:T(8,128)(2,1)S(1)} collective-permute-done((bf16[640,256]{1,0:T(8,128)(2,1)S(1)}, bf16[640,256]{1,0:T(8,128)(2,1)S(1)}, u32[]{:S(2)}, u32[]{:S(2)}) %collective-permute-start.18) | collective-permute-done | bytes 327712 | tf_op jit(solution)/shard_map/ppermute | solution.py:67
  242.1 6.4 %shard_map.202 = bf16[640,1792]{1,0:T(8,128)(2,1)} custom-call(s32[2]{0:T(128)S(1)} %pad_add_fusion.y_ref.here_ref, bf16[640,256]{1,0:T(8,128)(2,1)S(1)} %shard_map.200.refs_0_, bf16[640,256]{1,0:T(8,128)(2,1)S(1)} %collective-permute-done.18.refs_1_, bf16[640,256]{1,0:T(8,128)(2,1)S(1)} %collective-permute-done.19.refs_2_, ...), custom_call_target="tpu_custom_call" | custom-call | tf_op jit(solution)/shard_map/pallas_call | solution.py:234
  248.5 5.4 %all-to-all-start.3 = ((bf16[8,80,1792]{2,1,0:T(8,128)(2,1)}), bf16[8,80,1792]{2,1,0:T(8,128)(2,1)}, u32[]{:S(2)}, u32[]{:S(2)}) async-start(bf16[8,80,1792]{2,1,0:T(8,128)(2,1)} %get-tuple-element.62), calls=%async_computation.3 | async-start | bytes 4587520 | tf_op jit(solution)/shard_map/all_to_all | solution.py:79
  262.1 6.5 %collective-permute-done.24.refs_1_ = bf16[64,1792]{1,0:T(8,128)(2,1)S(1)} collective-permute-done((bf16[64,1792]{1,0:T(8,128)(2,1)S(1)}, bf16[64,1792]{1,0:T(8,128)(2,1)S(1)}, u32[]{:S(2)}, u32[]{:S(2)}) %collective-permute-start.24) | collective-permute-done | bytes 229408 | tf_op jit(solution)/shard_map/ppermute | solution.py:67
  272.9 6.7 %collective-permute-start.27 = (bf16[64,7168]{1,0:T(8,128)(2,1)S(1)}, bf16[64,7168]{1,0:T(8,128)(2,1)S(1)}, u32[]{:S(2)}, u32[]{:S(2)}) collective-permute-start(bf16[64,7168]{1,0:T(8,128)(2,1)S(1)} %shard_map.205.own_ref), channel_id=1, source_target_pairs={{32,64},{64,32},{33,65},{65,33},{34,66},{66,34},{35,67},{67,35},{3... | collective-permute-start | bytes 2752520 | tf_op jit(solution)/shard_map/ppermute | solution.py:417
  279.6 7.9 %all-to-all-done.3 = bf16[8,80,1792]{2,1,0:T(8,128)(2,1)} async-done(((bf16[8,80,1792]{2,1,0:T(8,128)(2,1)}), bf16[8,80,1792]{2,1,0:T(8,128)(2,1)}, u32[]{:S(2)}, u32[]{:S(2)}) %all-to-all-start.3) | async-done | bytes 2293792 | tf_op jit(solution)/shard_map/all_to_all | solution.py:79
  287.5 4.6 %shard_map.206 = (bf16[64,1792]{1,0:T(8,128)(2,1)S(1)}, bf16[64,1792]{1,0:T(8,128)(2,1)S(1)}, bf16[64,1792]{1,0:T(8,128)(2,1)S(1)}, bf16[64,1792]{1,0:T(8,128)(2,1)S(1)}) custom-call(s32[2]{0:T(128)S(1)} %pad_add_fusion.y_ref.here_ref, bf16[256,128]{1,0:T(8,128)(2,1)S(1)} %copy-done.18, bf16[256,128]{1,0:T(8,128)(2,1)S(1)} %get-tuple-element.78.high_ref, ...), custom_call_target="tpu_custom_call" | custom-call | tf_op jit(solution)/shard_map/pallas_call | solution.py:270
  297.6 9.6 %collective-permute-done.29.refs_1_ = bf16[64,1792]{1,0:T(8,128)(2,1)S(1)} collective-permute-done((bf16[64,1792]{1,0:T(8,128)(2,1)S(1)}, bf16[64,1792]{1,0:T(8,128)(2,1)S(1)}, u32[]{:S(2)}, u32[]{:S(2)}) %collective-permute-start.29) | collective-permute-done | bytes 229408 | tf_op jit(solution)/shard_map/ppermute | solution.py:302
  (167 shorter events, 90.3 us)
Async XLA Ops:
  1.5 29.0 %collective-permute-start.14 = (bf16[64,128]{0,1:T(8,128)(2,1)S(1)}, bf16[64,128]{0,1:T(8,128)(2,1)S(1)}, u32[]{:S(2)}, u32[]{:S(2)}) collective-permute-start(bf16[64,128]{0,1:T(8,128)(2,1)S(1)} %concatenate.34), channel_id=1, source_target_pairs={{0,3},{1,0},{2,1},{3,2},{4,7},{5,4},{6,5},{7,6},{8,11},{9,8},{10,9... | collective-permute-start | bytes 49160 | tf_op jit(solution)/shard_map/ppermute | solution.py:67
  5.2 25.5 %collective-permute-start.13 = (bf16[64,128]{0,1:T(8,128)(2,1)S(1)}, bf16[64,128]{0,1:T(8,128)(2,1)}, u32[]{:S(2)}, u32[]{:S(2)}) collective-permute-start(bf16[64,128]{0,1:T(8,128)(2,1)S(1)} %concatenate.34), channel_id=1, source_target_pairs={{0,2},{1,3},{2,0},{3,1},{4,6},{5,7},{6,4},{7,5},{8,10},{9,11},{10,... | collective-permute-start | bytes 49160 | tf_op jit(solution)/shard_map/ppermute | solution.py:67
  5.5 27.0 %collective-permute-start.12 = (bf16[64,128]{0,1:T(8,128)(2,1)S(1)}, bf16[64,128]{0,1:T(8,128)(2,1)}, u32[]{:S(2)}, u32[]{:S(2)}) collective-permute-start(bf16[64,128]{0,1:T(8,128)(2,1)S(1)} %concatenate.34), channel_id=1, source_target_pairs={{0,1},{1,2},{2,3},{3,0},{4,5},{5,6},{6,7},{7,4},{8,9},{9,10},{10,1... | collective-permute-start | bytes 49160 | tf_op jit(solution)/shard_map/ppermute | solution.py:67
  7.8 48.3 %collective-permute-start.17 = (bf16[64,7168]{1,0:T(8,128)(2,1)S(1)}, bf16[64,7168]{1,0:T(8,128)(2,1)}, u32[]{:S(2)}, u32[]{:S(2)}) collective-permute-start(bf16[64,7168]{1,0:T(8,128)(2,1)S(1)} %get-tuple-element.73.refs_0_), channel_id=1, source_target_pairs={{0,3},{1,0},{2,1},{3,2},{4,7},{5,4},{6,5},{7,6},{8,11},{9,8},{10,9... | collective-permute-start | bytes 2752520 | tf_op jit(solution)/shard_map/ppermute | solution.py:67
  9.8 46.6 %collective-permute-start.16 = (bf16[64,7168]{1,0:T(8,128)(2,1)S(1)}, bf16[64,7168]{1,0:T(8,128)(2,1)}, u32[]{:S(2)}, u32[]{:S(2)}) collective-permute-start(bf16[64,7168]{1,0:T(8,128)(2,1)S(1)} %get-tuple-element.73.refs_0_), channel_id=1, source_target_pairs={{0,2},{1,3},{2,0},{3,1},{4,6},{5,7},{6,4},{7,5},{8,10},{9,11},{10,... | collective-permute-start | bytes 2752520 | tf_op jit(solution)/shard_map/ppermute | solution.py:67
  14.9 37.0 %all-to-all-start = ((bf16[8,40,3584]{2,1,0:T(8,128)(2,1)}), bf16[8,40,3584]{2,1,0:T(8,128)(2,1)S(1)}, u32[]{:S(2)}, u32[]{:S(2)}) async-start(bf16[8,40,3584]{2,1,0:T(8,128)(2,1)} %bitcast.71), calls=%async_computation | async-start | bytes 4587520 | tf_op jit(solution)/shard_map/all_to_all | solution.py:79
  30.6 28.2 %collective-permute-start.15 = (bf16[64,7168]{1,0:T(8,128)(2,1)S(1)}, bf16[64,7168]{1,0:T(8,128)(2,1)}, u32[]{:S(2)}, u32[]{:S(2)}) collective-permute-start(bf16[64,7168]{1,0:T(8,128)(2,1)S(1)} %get-tuple-element.73.refs_0_), channel_id=1, source_target_pairs={{0,1},{1,2},{2,3},{3,0},{4,5},{5,6},{6,7},{7,4},{8,9},{9,10},{10,1... | collective-permute-start | bytes 2752520 | tf_op jit(solution)/shard_map/ppermute | solution.py:67
  30.7 101.0 %collective-permute-start.9 = (bf16[256,1792]{1,0:T(8,128)(2,1)}, bf16[256,1792]{1,0:T(8,128)(2,1)}, u32[]{:S(2)}, u32[]{:S(2)}) collective-permute-start(bf16[256,1792]{1,0:T(8,128)(2,1)} %get-tuple-element.43), channel_id=1, source_target_pairs={{0,2},{1,3},{2,0},{3,1},{4,6},{5,7},{6,4},{7,5},{8,10},{9,11},{10,... | collective-permute-start | bytes 2752520 | tf_op jit(solution)/shard_map/ppermute | solution.py:67
  55.0 66.5 %collective-permute-start.2 = (bf16[80,7168]{1,0:T(8,128)(2,1)}, bf16[80,7168]{1,0:T(8,128)(2,1)S(1)}, u32[]{:S(2)}, u32[]{:S(2)}) collective-permute-start(bf16[80,7168]{1,0:T(8,128)(2,1)} %get-tuple-element.36.refs_0_.refs_5_), channel_id=1, source_target_pairs={{0,3},{1,0},{2,1},{3,2},{4,7},{5,4},{6,5},{7,6},{8,11},{9,8},{10,9... | collective-permute-start | bytes 3440648 | tf_op jit(solution)/shard_map/ppermute | solution.py:67
  56.0 41.2 %collective-permute-start = (bf16[80,7168]{1,0:T(8,128)(2,1)}, bf16[80,7168]{1,0:T(8,128)(2,1)}, u32[]{:S(2)}, u32[]{:S(2)}) collective-permute-start(bf16[80,7168]{1,0:T(8,128)(2,1)} %get-tuple-element.36.refs_0_.refs_5_), channel_id=1, source_target_pairs={{0,1},{1,2},{2,3},{3,0},{4,5},{5,6},{6,7},{7,4},{8,9},{9,10},{10,1... | collective-permute-start | bytes 3440648 | tf_op jit(solution)/shard_map/ppermute | solution.py:67
  56.4 61.7 %collective-permute-start.3 = (bf16[80,7168]{1,0:T(8,128)(2,1)}, bf16[80,7168]{1,0:T(8,128)(2,1)}, u32[]{:S(2)}, u32[]{:S(2)}) collective-permute-start(bf16[80,7168]{1,0:T(8,128)(2,1)} %get-tuple-element.37.refs_1_.refs_6_), channel_id=1, source_target_pairs={{0,3},{1,0},{2,1},{3,2},{4,7},{5,4},{6,5},{7,6},{8,11},{9,8},{10,9... | collective-permute-start | bytes 3440648 | tf_op jit(solution)/shard_map/ppermute | solution.py:67
  58.7 63.0 %collective-permute-start.1 = (bf16[80,7168]{1,0:T(8,128)(2,1)}, bf16[80,7168]{1,0:T(8,128)(2,1)S(1)}, u32[]{:S(2)}, u32[]{:S(2)}) collective-permute-start(bf16[80,7168]{1,0:T(8,128)(2,1)} %get-tuple-element.37.refs_1_.refs_6_), channel_id=1, source_target_pairs={{0,1},{1,2},{2,3},{3,0},{4,5},{5,6},{6,7},{7,4},{8,9},{9,10},{10,1... | collective-permute-start | bytes 3440648 | tf_op jit(solution)/shard_map/ppermute | solution.py:67
  67.4 130.9 %all-to-all-start.1 = ((bf16[8,80,7168]{2,1,0:T(8,128)(2,1)}), bf16[8,80,7168]{2,1,0:T(8,128)(2,1)}, u32[]{:S(2)}, u32[]{:S(2)}) async-start(bf16[8,80,7168]{2,1,0:T(8,128)(2,1)} %bitcast.70), calls=%async_computation.1 | async-start | bytes 18350080 | tf_op jit(solution)/shard_map/all_to_all | solution.py:79
  97.2 49.2 %collective-permute-start.4 = (bf16[80,7168]{1,0:T(8,128)(2,1)}, bf16[80,7168]{1,0:T(8,128)(2,1)}, u32[]{:S(2)}, u32[]{:S(2)}) collective-permute-start(bf16[80,7168]{1,0:T(8,128)(2,1)} %collective-permute-done.refs_2_), channel_id=1, source_target_pairs={{0,1},{1,2},{2,3},{3,0},{4,5},{5,6},{6,7},{7,4},{8,9},{9,10},{10,1... | collective-permute-start | bytes 3440648 | tf_op jit(solution)/shard_map/ppermute | solution.py:67
  118.1 28.2 %collective-permute-start.5 = (bf16[80,7168]{1,0:T(8,128)(2,1)}, bf16[80,7168]{1,0:T(8,128)(2,1)}, u32[]{:S(2)}, u32[]{:S(2)}) collective-permute-start(bf16[80,7168]{1,0:T(8,128)(2,1)} %collective-permute-done.3.refs_5_), channel_id=1, source_target_pairs={{0,3},{1,0},{2,1},{3,2},{4,7},{5,4},{6,5},{7,6},{8,11},{9,8},{10,9... | collective-permute-start | bytes 3440648 | tf_op jit(solution)/shard_map/ppermute | solution.py:67
  147.1 35.7 %collective-permute-start.10 = (bf16[256,1792]{1,0:T(8,128)(2,1)}, bf16[256,1792]{1,0:T(8,128)(2,1)}, u32[]{:S(2)}, u32[]{:S(2)}) collective-permute-start(bf16[256,1792]{1,0:T(8,128)(2,1)} %get-tuple-element.44), channel_id=1, source_target_pairs={{0,1},{1,2},{2,3},{3,0},{4,5},{5,6},{6,7},{7,4},{8,9},{9,10},{10,1... | collective-permute-start | bytes 2752520 | tf_op jit(solution)/shard_map/ppermute | solution.py:67
  147.6 35.1 %collective-permute-start.11 = (bf16[256,1792]{1,0:T(8,128)(2,1)}, bf16[256,1792]{1,0:T(8,128)(2,1)}, u32[]{:S(2)}, u32[]{:S(2)}) collective-permute-start(bf16[256,1792]{1,0:T(8,128)(2,1)} %get-tuple-element.45), channel_id=1, source_target_pairs={{0,3},{1,0},{2,1},{3,2},{4,7},{5,4},{6,5},{7,6},{8,11},{9,8},{10,9... | collective-permute-start | bytes 2752520 | tf_op jit(solution)/shard_map/ppermute | solution.py:67
  184.2 32.7 %collective-permute-start.21 = (bf16[256,1792]{1,0:T(8,128)(2,1)}, bf16[256,1792]{1,0:T(8,128)(2,1)}, u32[]{:S(2)}, u32[]{:S(2)}) collective-permute-start(bf16[256,1792]{1,0:T(8,128)(2,1)} %get-tuple-element.50), channel_id=1, source_target_pairs={{0,1},{1,2},{2,3},{3,0},{4,5},{5,6},{6,7},{7,4},{8,9},{9,10},{10,1... | collective-permute-start | bytes 2752520 | tf_op jit(solution)/shard_map/ppermute | solution.py:67
  185.9 38.4 %collective-permute-start.22 = (bf16[256,1792]{1,0:T(8,128)(2,1)}, bf16[256,1792]{1,0:T(8,128)(2,1)}, u32[]{:S(2)}, u32[]{:S(2)}) collective-permute-start(bf16[256,1792]{1,0:T(8,128)(2,1)} %get-tuple-element.51), channel_id=1, source_target_pairs={{0,2},{1,3},{2,0},{3,1},{4,6},{5,7},{6,4},{7,5},{8,10},{9,11},{10,... | collective-permute-start | bytes 2752520 | tf_op jit(solution)/shard_map/ppermute | solution.py:67
  187.4 39.8 %collective-permute-start.23 = (bf16[256,1792]{1,0:T(8,128)(2,1)}, bf16[256,1792]{1,0:T(8,128)(2,1)}, u32[]{:S(2)}, u32[]{:S(2)}) collective-permute-start(bf16[256,1792]{1,0:T(8,128)(2,1)} %get-tuple-element.52), channel_id=1, source_target_pairs={{0,3},{1,0},{2,1},{3,2},{4,7},{5,4},{6,5},{7,6},{8,11},{9,8},{10,9... | collective-permute-start | bytes 2752520 | tf_op jit(solution)/shard_map/ppermute | solution.py:67
  198.3 50.1 %all-to-all-start.2 = ((bf16[8,80,1792]{2,1,0:T(8,128)(2,1)}), bf16[8,80,1792]{2,1,0:T(8,128)(2,1)}, u32[]{:S(2)}, u32[]{:S(2)}) async-start(bf16[8,80,1792]{2,1,0:T(8,128)(2,1)} %bitcast.27), calls=%async_computation.2 | async-start | bytes 4587520 | tf_op jit(solution)/shard_map/all_to_all | solution.py:79
  216.9 25.2 %collective-permute-start.18 = (bf16[640,256]{1,0:T(8,128)(2,1)S(1)}, bf16[640,256]{1,0:T(8,128)(2,1)S(1)}, u32[]{:S(2)}, u32[]{:S(2)}) collective-permute-start(bf16[640,256]{1,0:T(8,128)(2,1)S(1)} %shard_map.200.refs_0_), channel_id=1, source_target_pairs={{0,1},{1,2},{2,3},{3,0},{4,5},{5,6},{6,7},{7,4},{8,9},{9,10},{10,1... | collective-permute-start | bytes 983048 | tf_op jit(solution)/shard_map/ppermute | solution.py:67
  248.5 39.0 %all-to-all-start.3 = ((bf16[8,80,1792]{2,1,0:T(8,128)(2,1)}), bf16[8,80,1792]{2,1,0:T(8,128)(2,1)}, u32[]{:S(2)}, u32[]{:S(2)}) async-start(bf16[8,80,1792]{2,1,0:T(8,128)(2,1)} %get-tuple-element.62), calls=%async_computation.3 | async-start | bytes 4587520 | tf_op jit(solution)/shard_map/all_to_all | solution.py:79
  272.9 24.7 %collective-permute-start.27 = (bf16[64,7168]{1,0:T(8,128)(2,1)S(1)}, bf16[64,7168]{1,0:T(8,128)(2,1)S(1)}, u32[]{:S(2)}, u32[]{:S(2)}) collective-permute-start(bf16[64,7168]{1,0:T(8,128)(2,1)S(1)} %shard_map.205.own_ref), channel_id=1, source_target_pairs={{32,64},{64,32},{33,65},{65,33},{34,66},{66,34},{35,67},{67,35},{3... | collective-permute-start | bytes 2752520 | tf_op jit(solution)/shard_map/ppermute | solution.py:417
  (44 other events, 422.8 us)

commit v8 on v7

--- a/solution.py
+++ b/solution.py
@@ -400,7 +400,7 @@
     far_piece = hidden_of(y, far, *weights, 0)
     hidden = arrange(y, target + jnp.bitwise_and(index - step + GROUP, GROUP - 1) * CAP, [both, far_piece])
     units = spread(hidden)
-    cuts1 = tie(cuts1, [*units, *parts0])
+    cuts1 = tie(cuts1, [parts0[0], parts0[2]])
     units = [hidden, *units]
 
     parts1 = shifts(cuts1)

time: 312 us -> 300 us (0.962)
  waiting for transfers between devices: 148 us -> 127 us
  starting transfers between devices: 65.6 us -> 79.3 us
  local copies, waits for them, and re-layouts: 8.92 us -> 5.26 us
    ppermute x27, waiting for transfers between devices: 117 us -> 104 us  [shift(): lax.ppermute(value, 'y', [(i, (i + steps) % GROUP) for i in range(GROUP)])]
    ppermute x1, starting transfers between devices: 6.66 us -> 18.3 us  [local(): lax.ppermute(result0, 'pipe', [(p, p + 1) for p in range(1, size - 1, 2)]...]
    all_to_all x4, waiting for transfers between devices: 20 us -> 12.1 us  [exchange(): lax.all_to_all(value, ('x', 'z'), split_axis=0, concat_axis=0, tiled=True)]
    ppermute x27, starting transfers between devices: 32.2 us -> 36 us  [shift(): lax.ppermute(value, 'y', [(i, (i + steps) % GROUP) for i in range(GROUP)])]
    unnamed x65 -> x53, local copies, waits for them, and re-layouts: 8.72 us -> 5.06 us
  transfers between devices with their start and end apart: 36 -> 36, of which waited for: 17 -> 17; matrix products, arithmetic and copies ran while one was open for 6% -> 7% of each run, Pallas kernels for 21% -> 21%
where the time goes in v8:
time: 300 us; the launch traced here: 299 us
  waiting for transfers between devices  127 us (42%)
  starting transfers between devices  79.3 us (26%)
  Pallas kernels  66.8 us (22%)
  matrix products  12.1 us (4%)
  other arithmetic  8.64 us (3%)
  local copies, waits for them, and re-layouts  5.26 us (2%)
    ppermute x27, waiting for transfers between devices, shift(): lax.ppermute(value, 'y', [(i, (i + steps) % GROUP) for i in range(GROUP)])  104 us
    ppermute x27, starting transfers between devices, shift(): lax.ppermute(value, 'y', [(i, (i + steps) % GROUP) for i in range(GROUP)])  36 us
    pallas_call x3, Pallas kernels, hidden_of(): call(kernel, shape(total, block), (steps,), [weights, weights] + [columns...  27.3 us
    all_to_all x4, starting transfers between devices, exchange(): lax.all_to_all(value, ('x', 'z'), split_axis=0, concat_axis=0, tiled=True)  21.3 us
    ppermute x1, starting transfers between devices, local(): lax.ppermute(result0, 'pipe', [(p, p + 1) for p in range(1, size - 1, 2)]...  18.3 us
    pallas_call x2, Pallas kernels, project(): call(kernel, shape(rows, part), (2,), [whole(unit) for unit in units] + [...  12.7 us
    all_to_all x4, waiting for transfers between devices, exchange(): lax.all_to_all(value, ('x', 'z'), split_axis=0, concat_axis=0, tiled=True)  12.1 us
    dot_general x5, matrix products, dot(): return jnp.dot(a, b, preferred_element_type=F32)  11.1 us
  transfers between devices with their start and end apart: 36, of which 17 were waited for; matrix products, arithmetic and copies ran while one was open for 7% of the time, Pallas kernels for 21%

profile of v8, /device:TPU:1, one launch (start us, length us, event | category | flops | bytes accessed | tf_op | source)
XLA Modules:
  0.0 299.2 jit_solution(8213381401220153853)
XLA Ops:
  14.8 5.5 %all-to-all-start = ((bf16[8,40,3584]{2,1,0:T(8,128)(2,1)}), bf16[8,40,3584]{2,1,0:T(8,128)(2,1)S(1)}, u32[]{:S(2)}, u32[]{:S(2)}) async-start(bf16[8,40,3584]{2,1,0:T(8,128)(2,1)} %bitcast.71), calls=%async_computation | async-start | bytes 4587520 | tf_op jit(solution)/shard_map/all_to_all | solution.py:79
  26.4 4.1 %shard_map.194 = (bf16[256,1792]{1,0:T(8,128)(2,1)S(1)}, bf16[256,1792]{1,0:T(8,128)(2,1)}, bf16[256,1792]{1,0:T(8,128)(2,1)S(1)}) custom-call(s32[2]{0:T(128)S(1)} %pad_add_fusion.y_ref.here_ref, bf16[1,2,256,7168]{3,2,1,0:T(8,128)(2,1)} %refs_4_.3), custom_call_target="tpu_custom_call" | custom-call | tf_op jit(solution)/shard_map/pallas_call | solution.py:144
  39.7 12.1 %all-to-all-done = bf16[8,40,3584]{2,1,0:T(8,128)(2,1)S(1)} async-done(((bf16[8,40,3584]{2,1,0:T(8,128)(2,1)}), bf16[8,40,3584]{2,1,0:T(8,128)(2,1)S(1)}, u32[]{:S(2)}, u32[]{:S(2)}) %all-to-all-start) | async-done | bytes 2293792 | tf_op jit(solution)/shard_map/all_to_all | solution.py:79
  59.4 8.0 %convolution_convert_fusion = bf16[640,7168]{1,0:T(8,128)(2,1)} fusion(bf16[640,256]{1,0:T(8,128)(2,1)} %get-tuple-element.46, bf16[64,7168]{1,0:T(8,128)(2,1)} %collective-permute-done.17.refs_9_.refs_1_, bf16[64,7168]{1,0:T(8,128)(2,1)} %collective-permute-done.16.refs_8_.refs_2_, bf16[64,7168]{1,0:T(8,128)(2,1)} %collective-permute-done.15.refs_7_.refs_3_, ...), kind=kOutput, calls=%fused_computation | convolution fusion | flops 2368077824 | bytes 13172736 | tf_op jit(solution)/shard_map/dot_general | solution.py:22
  67.4 5.0 %all-to-all-start.1 = ((bf16[8,80,7168]{2,1,0:T(8,128)(2,1)}), bf16[8,80,7168]{2,1,0:T(8,128)(2,1)}, u32[]{:S(2)}, u32[]{:S(2)}) async-start(bf16[8,80,7168]{2,1,0:T(8,128)(2,1)} %bitcast.70), calls=%async_computation.1 | async-start | bytes 18350080 | tf_op jit(solution)/shard_map/all_to_all | solution.py:79
  72.4 24.8 %collective-permute-done.refs_2_ = bf16[80,7168]{1,0:T(8,128)(2,1)} collective-permute-done((bf16[80,7168]{1,0:T(8,128)(2,1)}, bf16[80,7168]{1,0:T(8,128)(2,1)}, u32[]{:S(2)}, u32[]{:S(2)}) %collective-permute-start) | collective-permute-done | bytes 1146912 | tf_op jit(solution)/shard_map/ppermute | solution.py:67
  97.2 20.9 %collective-permute-done.3.refs_5_ = bf16[80,7168]{1,0:T(8,128)(2,1)} collective-permute-done((bf16[80,7168]{1,0:T(8,128)(2,1)}, bf16[80,7168]{1,0:T(8,128)(2,1)}, u32[]{:S(2)}, u32[]{:S(2)}) %collective-permute-start.3) | collective-permute-done | bytes 1146912 | tf_op jit(solution)/shard_map/ppermute | solution.py:67
  121.7 9.2 %shard_map.191.refs_0_.refs_7_ = bf16[480,256]{1,0:T(8,128)(2,1)S(1)} custom-call(s32[2]{0:T(128)S(1)} %pad_add_fusion.y_ref.here_ref, bf16[1,2,7168,256]{3,2,1,0:T(8,128)(2,1)} %gate_ref.5, bf16[1,2,7168,256]{3,2,1,0:T(8,128)(2,1)} %up_ref.5, bf16[80,7168]{1,0:T(8,128)(2,1)} %get-tuple-element.36.refs_0_.refs_5_, ...), custom_call_target="tpu_custom_call" | custom-call | flops 209715200000 | bytes 419430400 | tf_op jit(solution)/shard_map/pallas_call | solution.py:178
  131.6 14.7 %collective-permute-done.4.refs_0_.refs_5_ = bf16[80,7168]{1,0:T(8,128)(2,1)} collective-permute-done((bf16[80,7168]{1,0:T(8,128)(2,1)}, bf16[80,7168]{1,0:T(8,128)(2,1)}, u32[]{:S(2)}, u32[]{:S(2)}) %collective-permute-start.4) | collective-permute-done | bytes 1146912 | tf_op jit(solution)/shard_map/ppermute | solution.py:67
  149.7 7.3 %shard_map.192.refs_1_ = bf16[160,256]{1,0:T(8,128)(2,1)S(1)} custom-call(s32[2]{0:T(128)S(1)} %pad_add_fusion.y_ref.here_ref, bf16[1,2,7168,256]{3,2,1,0:T(8,128)(2,1)} %gate_ref.5, bf16[1,2,7168,256]{3,2,1,0:T(8,128)(2,1)} %up_ref.5, bf16[80,7168]{1,0:T(8,128)(2,1)} %collective-permute-done.4.refs_0_.refs_5_, ...), custom_call_target="tpu_custom_call" | custom-call | flops 209715200000 | bytes 419430400 | tf_op jit(solution)/shard_map/pallas_call | solution.py:178
  160.6 8.0 %collective-permute-done.10.refs_5_.refs_3_ = bf16[256,1792]{1,0:T(8,128)(2,1)} collective-permute-done((bf16[256,1792]{1,0:T(8,128)(2,1)}, bf16[256,1792]{1,0:T(8,128)(2,1)}, u32[]{:S(2)}, u32[]{:S(2)}) %collective-permute-start.10) | collective-permute-done | bytes 917536 | tf_op jit(solution)/shard_map/ppermute | solution.py:67
  178.4 4.3 %collective-permute-done.6.refs_1_ = bf16[640,256]{1,0:T(8,128)(2,1)S(1)} collective-permute-done((bf16[640,256]{1,0:T(8,128)(2,1)S(1)}, bf16[640,256]{1,0:T(8,128)(2,1)S(1)}, u32[]{:S(2)}, u32[]{:S(2)}) %collective-permute-start.6) | collective-permute-done | bytes 327712 | tf_op jit(solution)/shard_map/ppermute | solution.py:67
  182.7 6.4 %shard_map.197.refs_1_ = bf16[640,1792]{1,0:T(8,128)(2,1)} custom-call(s32[2]{0:T(128)S(1)} %pad_add_fusion.y_ref.here_ref, bf16[640,256]{1,0:T(8,128)(2,1)S(1)} %shard_map.193.refs_0_, bf16[640,256]{1,0:T(8,128)(2,1)S(1)} %collective-permute-done.6.refs_1_, bf16[640,256]{1,0:T(8,128)(2,1)S(1)} %collective-permute-done.7.refs_2_, ...), custom_call_target="tpu_custom_call" | custom-call | tf_op jit(solution)/shard_map/pallas_call | solution.py:234
  189.7 5.5 %all-to-all-start.2 = ((bf16[8,80,1792]{2,1,0:T(8,128)(2,1)}), bf16[8,80,1792]{2,1,0:T(8,128)(2,1)}, u32[]{:S(2)}, u32[]{:S(2)}) async-start(bf16[8,80,1792]{2,1,0:T(8,128)(2,1)} %bitcast.27), calls=%async_computation.2 | async-start | bytes 4587520 | tf_op jit(solution)/shard_map/all_to_all | solution.py:79
  195.3 10.9 %shard_map.200.refs_0_ = bf16[640,256]{1,0:T(8,128)(2,1)S(1)} custom-call(s32[2]{0:T(128)S(1)} %copy-done.15, bf16[1,2,7168,256]{3,2,1,0:T(8,128)(2,1)} %gate_ref.5, bf16[1,2,7168,256]{3,2,1,0:T(8,128)(2,1)} %up_ref.5, bf16[640,7168]{1,0:T(8,128)(2,1)} %bitcast.25.refs_0_), custom_call_target="tpu_custom_call" | custom-call | flops 209715200000 | bytes 419430400 | tf_op jit(solution)/shard_map/pallas_call | solution.py:178
  209.6 13.6 %collective-permute-done.22.refs_6_ = bf16[256,1792]{1,0:T(8,128)(2,1)} collective-permute-done((bf16[256,1792]{1,0:T(8,128)(2,1)}, bf16[256,1792]{1,0:T(8,128)(2,1)}, u32[]{:S(2)}, u32[]{:S(2)}) %collective-permute-start.22) | collective-permute-done | bytes 917536 | tf_op jit(solution)/shard_map/ppermute | solution.py:67
  223.2 4.1 %collective-permute-done.20.refs_3_ = bf16[640,256]{1,0:T(8,128)(2,1)S(1)} collective-permute-done((bf16[640,256]{1,0:T(8,128)(2,1)S(1)}, bf16[640,256]{1,0:T(8,128)(2,1)S(1)}, u32[]{:S(2)}, u32[]{:S(2)}) %collective-permute-start.20) | collective-permute-done | bytes 327712 | tf_op jit(solution)/shard_map/ppermute | solution.py:67
  232.5 6.3 %shard_map.202 = bf16[640,1792]{1,0:T(8,128)(2,1)} custom-call(s32[2]{0:T(128)S(1)} %pad_add_fusion.y_ref.here_ref, bf16[640,256]{1,0:T(8,128)(2,1)S(1)} %shard_map.200.refs_0_, bf16[640,256]{1,0:T(8,128)(2,1)S(1)} %collective-permute-done.18.refs_1_, bf16[640,256]{1,0:T(8,128)(2,1)S(1)} %collective-permute-done.19.refs_2_, ...), custom_call_target="tpu_custom_call" | custom-call | tf_op jit(solution)/shard_map/pallas_call | solution.py:234
  238.9 5.3 %all-to-all-start.3 = ((bf16[8,80,1792]{2,1,0:T(8,128)(2,1)}), bf16[8,80,1792]{2,1,0:T(8,128)(2,1)}, u32[]{:S(2)}, u32[]{:S(2)}) async-start(bf16[8,80,1792]{2,1,0:T(8,128)(2,1)} %get-tuple-element.62), calls=%async_computation.3 | async-start | bytes 4587520 | tf_op jit(solution)/shard_map/all_to_all | solution.py:79
  244.2 4.5 %shard_map.204 = (bf16[64,1792]{1,0:T(8,128)(2,1)S(1)}, bf16[64,1792]{1,0:T(8,128)(2,1)S(1)}, bf16[64,1792]{1,0:T(8,128)(2,1)S(1)}, bf16[64,1792]{1,0:T(8,128)(2,1)S(1)}) custom-call(s32[2]{0:T(128)S(1)} %pad_add_fusion.y_ref.here_ref, bf16[256,128]{1,0:T(8,128)(2,1)S(1)} %copy-done.7, bf16[256,128]{1,0:T(8,128)(2,1)S(1)} %get-tuple-element.80.high_ref, ...), custom_call_target="tpu_custom_call" | custom-call | tf_op jit(solution)/shard_map/pallas_call | solution.py:270
  252.4 4.9 %collective-permute-done.24.refs_1_ = bf16[64,1792]{1,0:T(8,128)(2,1)S(1)} collective-permute-done((bf16[64,1792]{1,0:T(8,128)(2,1)S(1)}, bf16[64,1792]{1,0:T(8,128)(2,1)S(1)}, u32[]{:S(2)}, u32[]{:S(2)}) %collective-permute-start.24) | collective-permute-done | bytes 229408 | tf_op jit(solution)/shard_map/ppermute | solution.py:67
  259.0 18.3 %collective-permute-start.27 = (bf16[64,7168]{1,0:T(8,128)(2,1)S(1)}, bf16[64,7168]{1,0:T(8,128)(2,1)S(1)}, u32[]{:S(2)}, u32[]{:S(2)}) collective-permute-start(bf16[64,7168]{1,0:T(8,128)(2,1)S(1)} %shard_map.205.own_ref), channel_id=1, source_target_pairs={{32,64},{64,32},{33,65},{65,33},{34,66},{66,34},{35,67},{67,35},{3... | collective-permute-start | bytes 2752520 | tf_op jit(solution)/shard_map/ppermute | solution.py:417
  277.5 4.6 %shard_map.206 = (bf16[64,1792]{1,0:T(8,128)(2,1)S(1)}, bf16[64,1792]{1,0:T(8,128)(2,1)S(1)}, bf16[64,1792]{1,0:T(8,128)(2,1)S(1)}, bf16[64,1792]{1,0:T(8,128)(2,1)S(1)}) custom-call(s32[2]{0:T(128)S(1)} %pad_add_fusion.y_ref.here_ref, bf16[256,128]{1,0:T(8,128)(2,1)S(1)} %copy-done.12, bf16[256,128]{1,0:T(8,128)(2,1)S(1)} %get-tuple-element.78.high_ref, ...), custom_call_target="tpu_custom_call" | custom-call | tf_op jit(solution)/shard_map/pallas_call | solution.py:270
  291.1 5.5 %collective-permute-done.30.refs_2_ = bf16[64,1792]{1,0:T(8,128)(2,1)S(1)} collective-permute-done((bf16[64,1792]{1,0:T(8,128)(2,1)S(1)}, bf16[64,1792]{1,0:T(8,128)(2,1)S(1)}, u32[]{:S(2)}, u32[]{:S(2)}) %collective-permute-start.30) | collective-permute-done | bytes 229408 | tf_op jit(solution)/shard_map/ppermute | solution.py:302
  (155 shorter events, 85.1 us)
Async XLA Ops:
  1.5 29.0 %collective-permute-start.14 = (bf16[64,128]{0,1:T(8,128)(2,1)S(1)}, bf16[64,128]{0,1:T(8,128)(2,1)S(1)}, u32[]{:S(2)}, u32[]{:S(2)}) collective-permute-start(bf16[64,128]{0,1:T(8,128)(2,1)S(1)} %concatenate.34), channel_id=1, source_target_pairs={{0,3},{1,0},{2,1},{3,2},{4,7},{5,4},{6,5},{7,6},{8,11},{9,8},{10,9... | collective-permute-start | bytes 49160 | tf_op jit(solution)/shard_map/ppermute | solution.py:67
  5.2 25.5 %collective-permute-start.13 = (bf16[64,128]{0,1:T(8,128)(2,1)S(1)}, bf16[64,128]{0,1:T(8,128)(2,1)}, u32[]{:S(2)}, u32[]{:S(2)}) collective-permute-start(bf16[64,128]{0,1:T(8,128)(2,1)S(1)} %concatenate.34), channel_id=1, source_target_pairs={{0,2},{1,3},{2,0},{3,1},{4,6},{5,7},{6,4},{7,5},{8,10},{9,11},{10,... | collective-permute-start | bytes 49160 | tf_op jit(solution)/shard_map/ppermute | solution.py:67
  5.5 27.0 %collective-permute-start.12 = (bf16[64,128]{0,1:T(8,128)(2,1)S(1)}, bf16[64,128]{0,1:T(8,128)(2,1)}, u32[]{:S(2)}, u32[]{:S(2)}) collective-permute-start(bf16[64,128]{0,1:T(8,128)(2,1)S(1)} %concatenate.34), channel_id=1, source_target_pairs={{0,1},{1,2},{2,3},{3,0},{4,5},{5,6},{6,7},{7,4},{8,9},{9,10},{10,1... | collective-permute-start | bytes 49160 | tf_op jit(solution)/shard_map/ppermute | solution.py:67
  7.8 48.2 %collective-permute-start.17 = (bf16[64,7168]{1,0:T(8,128)(2,1)S(1)}, bf16[64,7168]{1,0:T(8,128)(2,1)}, u32[]{:S(2)}, u32[]{:S(2)}) collective-permute-start(bf16[64,7168]{1,0:T(8,128)(2,1)S(1)} %get-tuple-element.73.refs_0_), channel_id=1, source_target_pairs={{0,3},{1,0},{2,1},{3,2},{4,7},{5,4},{6,5},{7,6},{8,11},{9,8},{10,9... | collective-permute-start | bytes 2752520 | tf_op jit(solution)/shard_map/ppermute | solution.py:67
  9.8 46.6 %collective-permute-start.16 = (bf16[64,7168]{1,0:T(8,128)(2,1)S(1)}, bf16[64,7168]{1,0:T(8,128)(2,1)}, u32[]{:S(2)}, u32[]{:S(2)}) collective-permute-start(bf16[64,7168]{1,0:T(8,128)(2,1)S(1)} %get-tuple-element.73.refs_0_), channel_id=1, source_target_pairs={{0,2},{1,3},{2,0},{3,1},{4,6},{5,7},{6,4},{7,5},{8,10},{9,11},{10,... | collective-permute-start | bytes 2752520 | tf_op jit(solution)/shard_map/ppermute | solution.py:67
  14.8 37.0 %all-to-all-start = ((bf16[8,40,3584]{2,1,0:T(8,128)(2,1)}), bf16[8,40,3584]{2,1,0:T(8,128)(2,1)S(1)}, u32[]{:S(2)}, u32[]{:S(2)}) async-start(bf16[8,40,3584]{2,1,0:T(8,128)(2,1)} %bitcast.71), calls=%async_computation | async-start | bytes 4587520 | tf_op jit(solution)/shard_map/all_to_all | solution.py:79
  30.5 28.1 %collective-permute-start.15 = (bf16[64,7168]{1,0:T(8,128)(2,1)S(1)}, bf16[64,7168]{1,0:T(8,128)(2,1)}, u32[]{:S(2)}, u32[]{:S(2)}) collective-permute-start(bf16[64,7168]{1,0:T(8,128)(2,1)S(1)} %get-tuple-element.73.refs_0_), channel_id=1, source_target_pairs={{0,1},{1,2},{2,3},{3,0},{4,5},{5,6},{6,7},{7,4},{8,9},{9,10},{10,1... | collective-permute-start | bytes 2752520 | tf_op jit(solution)/shard_map/ppermute | solution.py:67
  30.6 101.0 %collective-permute-start.9 = (bf16[256,1792]{1,0:T(8,128)(2,1)}, bf16[256,1792]{1,0:T(8,128)(2,1)}, u32[]{:S(2)}, u32[]{:S(2)}) collective-permute-start(bf16[256,1792]{1,0:T(8,128)(2,1)} %get-tuple-element.43), channel_id=1, source_target_pairs={{0,2},{1,3},{2,0},{3,1},{4,6},{5,7},{6,4},{7,5},{8,10},{9,11},{10,... | collective-permute-start | bytes 2752520 | tf_op jit(solution)/shard_map/ppermute | solution.py:67
  54.9 66.6 %collective-permute-start.2 = (bf16[80,7168]{1,0:T(8,128)(2,1)}, bf16[80,7168]{1,0:T(8,128)(2,1)S(1)}, u32[]{:S(2)}, u32[]{:S(2)}) collective-permute-start(bf16[80,7168]{1,0:T(8,128)(2,1)} %get-tuple-element.36.refs_0_.refs_5_), channel_id=1, source_target_pairs={{0,3},{1,0},{2,1},{3,2},{4,7},{5,4},{6,5},{7,6},{8,11},{9,8},{10,9... | collective-permute-start | bytes 3440648 | tf_op jit(solution)/shard_map/ppermute | solution.py:67
  56.0 41.2 %collective-permute-start = (bf16[80,7168]{1,0:T(8,128)(2,1)}, bf16[80,7168]{1,0:T(8,128)(2,1)}, u32[]{:S(2)}, u32[]{:S(2)}) collective-permute-start(bf16[80,7168]{1,0:T(8,128)(2,1)} %get-tuple-element.36.refs_0_.refs_5_), channel_id=1, source_target_pairs={{0,1},{1,2},{2,3},{3,0},{4,5},{5,6},{6,7},{7,4},{8,9},{9,10},{10,1... | collective-permute-start | bytes 3440648 | tf_op jit(solution)/shard_map/ppermute | solution.py:67
  56.4 61.7 %collective-permute-start.3 = (bf16[80,7168]{1,0:T(8,128)(2,1)}, bf16[80,7168]{1,0:T(8,128)(2,1)}, u32[]{:S(2)}, u32[]{:S(2)}) collective-permute-start(bf16[80,7168]{1,0:T(8,128)(2,1)} %get-tuple-element.37.refs_1_.refs_6_), channel_id=1, source_target_pairs={{0,3},{1,0},{2,1},{3,2},{4,7},{5,4},{6,5},{7,6},{8,11},{9,8},{10,9... | collective-permute-start | bytes 3440648 | tf_op jit(solution)/shard_map/ppermute | solution.py:67
  58.7 63.1 %collective-permute-start.1 = (bf16[80,7168]{1,0:T(8,128)(2,1)}, bf16[80,7168]{1,0:T(8,128)(2,1)S(1)}, u32[]{:S(2)}, u32[]{:S(2)}) collective-permute-start(bf16[80,7168]{1,0:T(8,128)(2,1)} %get-tuple-element.37.refs_1_.refs_6_), channel_id=1, source_target_pairs={{0,1},{1,2},{2,3},{3,0},{4,5},{5,6},{6,7},{7,4},{8,9},{9,10},{10,1... | collective-permute-start | bytes 3440648 | tf_op jit(solution)/shard_map/ppermute | solution.py:67
  67.4 122.3 %all-to-all-start.1 = ((bf16[8,80,7168]{2,1,0:T(8,128)(2,1)}), bf16[8,80,7168]{2,1,0:T(8,128)(2,1)}, u32[]{:S(2)}, u32[]{:S(2)}) async-start(bf16[8,80,7168]{2,1,0:T(8,128)(2,1)} %bitcast.70), calls=%async_computation.1 | async-start | bytes 18350080 | tf_op jit(solution)/shard_map/all_to_all | solution.py:79
  97.2 49.2 %collective-permute-start.4 = (bf16[80,7168]{1,0:T(8,128)(2,1)}, bf16[80,7168]{1,0:T(8,128)(2,1)}, u32[]{:S(2)}, u32[]{:S(2)}) collective-permute-start(bf16[80,7168]{1,0:T(8,128)(2,1)} %collective-permute-done.refs_2_), channel_id=1, source_target_pairs={{0,1},{1,2},{2,3},{3,0},{4,5},{5,6},{6,7},{7,4},{8,9},{9,10},{10,1... | collective-permute-start | bytes 3440648 | tf_op jit(solution)/shard_map/ppermute | solution.py:67
  118.1 28.2 %collective-permute-start.5 = (bf16[80,7168]{1,0:T(8,128)(2,1)}, bf16[80,7168]{1,0:T(8,128)(2,1)}, u32[]{:S(2)}, u32[]{:S(2)}) collective-permute-start(bf16[80,7168]{1,0:T(8,128)(2,1)} %collective-permute-done.3.refs_5_), channel_id=1, source_target_pairs={{0,3},{1,0},{2,1},{3,2},{4,7},{5,4},{6,5},{7,6},{8,11},{9,8},{10,9... | collective-permute-start | bytes 3440648 | tf_op jit(solution)/shard_map/ppermute | solution.py:67
  147.0 21.6 %collective-permute-start.10 = (bf16[256,1792]{1,0:T(8,128)(2,1)}, bf16[256,1792]{1,0:T(8,128)(2,1)}, u32[]{:S(2)}, u32[]{:S(2)}) collective-permute-start(bf16[256,1792]{1,0:T(8,128)(2,1)} %get-tuple-element.44), channel_id=1, source_target_pairs={{0,1},{1,2},{2,3},{3,0},{4,5},{5,6},{6,7},{7,4},{8,9},{9,10},{10,1... | collective-permute-start | bytes 2752520 | tf_op jit(solution)/shard_map/ppermute | solution.py:67
  159.4 23.2 %collective-permute-start.6 = (bf16[640,256]{1,0:T(8,128)(2,1)S(1)}, bf16[640,256]{1,0:T(8,128)(2,1)S(1)}, u32[]{:S(2)}, u32[]{:S(2)}) collective-permute-start(bf16[640,256]{1,0:T(8,128)(2,1)S(1)} %shard_map.193.refs_0_), channel_id=1, source_target_pairs={{0,1},{1,2},{2,3},{3,0},{4,5},{5,6},{6,7},{7,4},{8,9},{9,10},{10,1... | collective-permute-start | bytes 983048 | tf_op jit(solution)/shard_map/ppermute | solution.py:67
  169.3 40.2 %collective-permute-start.21 = (bf16[256,1792]{1,0:T(8,128)(2,1)}, bf16[256,1792]{1,0:T(8,128)(2,1)}, u32[]{:S(2)}, u32[]{:S(2)}) collective-permute-start(bf16[256,1792]{1,0:T(8,128)(2,1)} %get-tuple-element.50), channel_id=1, source_target_pairs={{0,1},{1,2},{2,3},{3,0},{4,5},{5,6},{6,7},{7,4},{8,9},{9,10},{10,1... | collective-permute-start | bytes 2752520 | tf_op jit(solution)/shard_map/ppermute | solution.py:67
  170.1 53.1 %collective-permute-start.22 = (bf16[256,1792]{1,0:T(8,128)(2,1)}, bf16[256,1792]{1,0:T(8,128)(2,1)}, u32[]{:S(2)}, u32[]{:S(2)}) collective-permute-start(bf16[256,1792]{1,0:T(8,128)(2,1)} %get-tuple-element.51), channel_id=1, source_target_pairs={{0,2},{1,3},{2,0},{3,1},{4,6},{5,7},{6,4},{7,5},{8,10},{9,11},{10,... | collective-permute-start | bytes 2752520 | tf_op jit(solution)/shard_map/ppermute | solution.py:67
  175.2 48.0 %collective-permute-start.23 = (bf16[256,1792]{1,0:T(8,128)(2,1)}, bf16[256,1792]{1,0:T(8,128)(2,1)}, u32[]{:S(2)}, u32[]{:S(2)}) collective-permute-start(bf16[256,1792]{1,0:T(8,128)(2,1)} %get-tuple-element.52), channel_id=1, source_target_pairs={{0,3},{1,0},{2,1},{3,2},{4,7},{5,4},{6,5},{7,6},{8,11},{9,8},{10,9... | collective-permute-start | bytes 2752520 | tf_op jit(solution)/shard_map/ppermute | solution.py:67
  189.7 49.1 %all-to-all-start.2 = ((bf16[8,80,1792]{2,1,0:T(8,128)(2,1)}), bf16[8,80,1792]{2,1,0:T(8,128)(2,1)}, u32[]{:S(2)}, u32[]{:S(2)}) async-start(bf16[8,80,1792]{2,1,0:T(8,128)(2,1)} %bitcast.27), calls=%async_computation.2 | async-start | bytes 4587520 | tf_op jit(solution)/shard_map/all_to_all | solution.py:79
  209.6 22.9 %collective-permute-start.18 = (bf16[640,256]{1,0:T(8,128)(2,1)S(1)}, bf16[640,256]{1,0:T(8,128)(2,1)S(1)}, u32[]{:S(2)}, u32[]{:S(2)}) collective-permute-start(bf16[640,256]{1,0:T(8,128)(2,1)S(1)} %shard_map.200.refs_0_), channel_id=1, source_target_pairs={{0,1},{1,2},{2,3},{3,0},{4,5},{5,6},{6,7},{7,4},{8,9},{9,10},{10,1... | collective-permute-start | bytes 983048 | tf_op jit(solution)/shard_map/ppermute | solution.py:67
  238.9 38.6 %all-to-all-start.3 = ((bf16[8,80,1792]{2,1,0:T(8,128)(2,1)}), bf16[8,80,1792]{2,1,0:T(8,128)(2,1)}, u32[]{:S(2)}, u32[]{:S(2)}) async-start(bf16[8,80,1792]{2,1,0:T(8,128)(2,1)} %get-tuple-element.62), calls=%async_computation.3 | async-start | bytes 4587520 | tf_op jit(solution)/shard_map/all_to_all | solution.py:79
  259.0 29.4 %collective-permute-start.27 = (bf16[64,7168]{1,0:T(8,128)(2,1)S(1)}, bf16[64,7168]{1,0:T(8,128)(2,1)S(1)}, u32[]{:S(2)}, u32[]{:S(2)}) collective-permute-start(bf16[64,7168]{1,0:T(8,128)(2,1)S(1)} %shard_map.205.own_ref), channel_id=1, source_target_pairs={{32,64},{64,32},{33,65},{65,33},{34,66},{66,34},{35,67},{67,35},{3... | collective-permute-start | bytes 2752520 | tf_op jit(solution)/shard_map/ppermute | solution.py:417
  (38 other events, 392.4 us)
